TPU v7x, 32 devices: a whole 2x2x4 slice. The times are simulated.
32 devices in a mesh: lat: 8 (over z, x), lon: 4 (over y, core).
Axes of the slice: x: 2, y: 2, z: 4, core: 2. Of those that a mesh axis runs over, the one named last changes fastest.
Arguments:
- observed: float32 [1024, 2048], P(('lat', 'lon')), may hold values from -12 to 12
- gauged: int32 [1024, 2048], P('lat', 'lon'), may hold values from 0 to 1, as said below
Outputs:
- coarsest_coeffs: float32 [128, 256], P('lat', 'lon')
- coarse_coeffs: float32 [256, 512], P('lat', 'lon')
- fine_coeffs: float32 [512, 1024], P('lat', 'lon')
- finest_coeffs: float32 [1024, 2048], P('lat', 'lon')
- imputed: float32 [1024, 2048], P(('lat', 'lon'))
Inputs may be any that keep to these rules, and one draw needn't show every extreme that they name: 1 marks a gauged cell.
All inputs are finite; a program needn't handle non-finite values.
Results may differ from a plain program's by a relative error of at most 0.00029.
Values sent between devices are 32-bit elements; how exact they have to be, the bound alone decides.
No kernel may reach another device: no remote copies, remote signals or barrier semaphores. Data moves between devices by JAX's collectives and lax.ppermute only.
A program may use at most 64 MiB of HBM per device.

v0:
```python
import math

import jax
import jax.numpy as jnp
import numpy as np
from jax import lax
from jax.experimental import pallas as pl
from jax.experimental.pallas import tpu as pltpu
from jax.sharding import PartitionSpec as P

LEVELS = 4
SPACINGS = tuple(2 ** (LEVELS - 1 - k) for k in range(LEVELS))
COARSE = LEVELS - 1
HALO = 64
INNER = 32
LANES = 128

data_weight = 2.0
kappa_term = 5.0
level_scales = (0.02, 0.03, 0.05, 0.08)

VMEM_LIMIT = 48 * 1024 * 1024


def wendland(distance):
    remain = np.maximum(1.0 - distance, 0.0)
    return remain**6 * (35.0 * distance * distance + 18.0 * distance + 3.0) / 3.0


def frame_index(total, tile, halo):
    place = np.arange(total)
    index = np.where(place < tile + halo, place, place - total)
    return index, (place < tile + halo) | (place >= total - halo)


def basis(cells, nodes, spacing):
    (cell, cell_ok), (node, node_ok) = cells, nodes
    numerator = np.abs(2 * cell[:, None] - 2 * spacing * node[None, :] - (spacing - 1))
    table = wendland(numerator / (5.0 * spacing)) / math.sqrt(spacing)
    return np.where(cell_ok[:, None] & node_ok[None, :], table, 0.0).astype(np.float32)


def halves(table):
    high = table.astype(jnp.bfloat16)
    low = (table - high.astype(np.float32)).astype(jnp.bfloat16)
    return np.stack([high, low])


def split(x):
    high = x.astype(jnp.bfloat16)
    return high, (x - high.astype(jnp.float32)).astype(jnp.bfloat16)


def dot(a, b, contract):
    return lax.dot_general(a, b, ((contract[0:1], contract[1:2]), ((), ())), preferred_element_type=jnp.float32)


def dot3(a, b, contract=(1, 0)):
    (ah, al), (bh, bl) = a, b
    return dot(ah, bh, contract) + (dot(ah, bl, contract) + dot(al, bh, contract))


TAPS = (float(wendland(np.float64(0.4))), float(wendland(np.float64(0.8))))


def shift(x, step, axis):
    return pltpu.roll(x, step % x.shape[axis], axis)


def smooth(x):
    for axis in (0, 1):
        near = shift(x, 1, axis) + shift(x, -1, axis)
        far = shift(x, 2, axis) + shift(x, -2, axis)
        x = x + (TAPS[0] * near + TAPS[1] * far)
    return x


def autoreg(x):
    beside = shift(x, 1, 0) + shift(x, -1, 0) + shift(x, 1, 1) + shift(x, -1, 1)
    return kappa_term * x - beside


def side_mask(total, tile, halo, at, last, dim):
    shape = (total, 1) if dim == 0 else (1, total)
    place = lax.broadcasted_iota(jnp.int32, shape, dim)
    after = (place < tile + halo) & (at < last)
    before = (place >= total - halo) & (at > 0)
    return ((place < tile) | after | before).astype(jnp.float32)


def fold(x):
    rows, cols = x.shape
    total = x[0:8]
    for r in range(8, rows, 8):
        total = total + x[r : r + 8]
    if cols < LANES:
        return jnp.concatenate([total, jnp.zeros((8, LANES - cols), jnp.float32)], axis=1)
    out = total[:, 0:LANES]
    for c in range(LANES, cols, LANES):
        out = out + total[:, c : c + LANES]
    return out


class Plan:
    def __init__(self, swath_shape, tile_shape, lat_total, lon_total):
        self.swath_rows, self.width = swath_shape
        self.rows, self.cols = tile_shape
        self.lat_total, self.lon_total = lat_total, lon_total
        self.row_frame = self.rows + 2 * HALO
        self.col_frame = self.cols + 2 * HALO
        self.inner_rows = self.rows + 2 * INNER
        self.node_rows = [self.row_frame // s for s in SPACINGS]
        self.node_cols = [-(-self.col_frame // (s * LANES)) * LANES for s in SPACINGS]
        self.row_starts = np.cumsum([0] + self.node_rows[:COARSE]).tolist()
        col_cells = frame_index(self.col_frame, self.cols, HALO)
        outer = frame_index(self.row_frame, self.rows, HALO)
        inner = frame_index(self.inner_rows, self.rows, INNER)
        col_tables, outer_rows, inner_rows = [], [], []
        for k in range(COARSE):
            s = SPACINGS[k]
            col_nodes = frame_index(self.node_cols[k], self.cols // s, HALO // s)
            row_nodes = frame_index(self.node_rows[k], self.rows // s, HALO // s)
            col_tables.append(halves(basis(col_cells, col_nodes, s)))
            outer_rows.append(basis(outer, row_nodes, s))
            inner_rows.append(basis(inner, row_nodes, s))
        outer_all = np.concatenate(outer_rows, axis=1)
        inner_all = np.concatenate(inner_rows, axis=1)
        self.tables = [
            *col_tables,
            halves(outer_all.T.copy()),
            halves(inner_all.T.copy()),
            halves(inner_all),
        ]


def call(kernel, outs, scratch=()):
    def run(*operands):
        return pl.pallas_call(
            kernel,
            out_shape=[jax.ShapeDtypeStruct(shape, jnp.float32) for shape in outs],
            in_specs=[pl.BlockSpec(memory_space=pltpu.VMEM)] * len(operands),
            out_specs=[pl.BlockSpec(memory_space=pltpu.VMEM)] * len(outs),
            scratch_shapes=list(scratch),
            compiler_params=pltpu.CompilerParams(vmem_limit_bytes=VMEM_LIMIT),
        )(*operands)

    return run


def pack(plan, observed, gauged):
    sr, width, cols, rows = plan.swath_rows, plan.width, plan.cols, plan.rows
    tiles = plan.col_frame // LANES

    def kernel(obs_ref, gauge_ref, own_ref, pair_ref, *rest):
        far_refs, odd_ref, wide = rest[:-2], rest[-2], rest[-1]
        at = lax.axis_index("lon")
        wide[:, 0:LANES] = jnp.zeros((sr, LANES), jnp.float32)
        wide[:, LANES : LANES + width] = obs_ref[...]
        wide[:, LANES + width :] = jnp.zeros((sr, LANES), jnp.float32)
        lane = lax.broadcasted_iota(jnp.int32, (sr, LANES), 1)

        def window(to):
            base = pl.multiple_of(to * cols, LANES)
            before = wide[:, pl.ds(base, LANES)]
            after = wide[:, pl.ds(base + LANES + cols, LANES)]
            return wide[:, pl.ds(base + LANES, cols)], jnp.where(lane < HALO, after, before)

        for k, ref in [(0, own_ref)] + list(enumerate(far_refs, 2)):
            main, sides = window(at ^ k)
            ref[:, 0:cols] = main
            ref[:, cols:] = sides
        main, sides = window(at ^ 1)
        for t in range(tiles - 1):
            pair_ref[t * sr : (t + 1) * sr, :] = main[:, t * LANES : (t + 1) * LANES]
        pair_ref[(tiles - 1) * sr : tiles * sr, :] = sides
        even = at % 2 == 0
        first = gauge_ref[:, 0:LANES].astype(jnp.float32)
        last = gauge_ref[:, cols - LANES :].astype(jnp.float32)
        pair_ref[tiles * sr :, :] = jnp.where(even, last, first)
        odd_ref[...] = jnp.where(even, first, last)

    outs = [(sr, plan.col_frame), (tiles * sr + rows, LANES)]
    outs += [(sr, plan.col_frame)] * (plan.lon_total - 2)
    outs += [(rows, LANES)]
    scratch = [pltpu.VMEM((sr, width + 2 * LANES), jnp.float32)]
    return call(kernel, outs, scratch)(observed, gauged)


def misfit(plan, own, pair, far, odd, gauged):
    sr, cols, rows = plan.swath_rows, plan.cols, plan.rows
    tiles = plan.col_frame // LANES

    def kernel(own_ref, pair_ref, odd_ref, gauge_ref, *rest):
        far_refs, (mis_ref, wt_ref, near_ref, next_ref) = rest[:-4], rest[-4:]
        at = lax.axis_index("lon")
        lat = lax.axis_index("lat")
        even = at % 2 == 0
        lane = lax.broadcasted_iota(jnp.int32, (rows, LANES), 1)
        from_pair = pair_ref[tiles * sr :, :]
        from_odd = odd_ref[...]
        right = jnp.where(even, from_pair, from_odd)
        left = jnp.where(even, from_odd, from_pair)
        wt_ref[:, 0:cols] = data_weight * gauge_ref[...].astype(jnp.float32)
        wt_ref[:, cols:] = data_weight * jnp.where(lane < HALO, right, left)

        def rows_of(k):
            return pl.ds(pl.multiple_of((at ^ k) * sr, sr), sr)

        for k, ref in [(0, own_ref)] + list(enumerate(far_refs, 2)):
            mis_ref[rows_of(k), :] = wt_ref[rows_of(k), :] * ref[...]
        for t in range(tiles):
            lanes = slice(t * LANES, (t + 1) * LANES)
            mis_ref[rows_of(1), lanes] = wt_ref[rows_of(1), lanes] * pair_ref[t * sr : (t + 1) * sr, :]
        up = lat % 2
        for ref, low in ((near_ref, 1 - up), (next_ref, up)):
            ref[0:HALO, :] = mis_ref[pl.ds(pl.multiple_of(low * (rows - HALO), 8), HALO), :]
            ref[HALO:, :] = wt_ref[pl.ds(pl.multiple_of(low * (rows - INNER), 8), INNER), :]

    outs = [(rows, plan.col_frame)] * 2 + [(HALO + INNER, plan.col_frame)] * 2
    return call(kernel, outs)(own, pair, odd, gauged, *far)


def operate(plan, mis, wt, near, following):
    rows, cols, sr, lon_total = plan.rows, plan.cols, plan.swath_rows, plan.lon_total
    starts = plan.row_starts
    inner_rows = plan.inner_rows
    n_tables = len(plan.tables)
    n_dev = plan.lat_total * lon_total

    def kernel(mis_ref, wt_ref, near_ref, next_ref, *rest):
        table_refs, out_refs = rest[:n_tables], rest[n_tables:]
        base_refs, image_refs = out_refs[:LEVELS], out_refs[LEVELS : 2 * LEVELS]
        surface_refs, part_ref = out_refs[2 * LEVELS : -1], out_refs[-1]
        lat = lax.axis_index("lat")
        lon = lax.axis_index("lon")
        even = lat % 2 == 0
        tables = [(ref[0], ref[1]) for ref in table_refs]
        col_tables, outer_t, inner_t, inner_s = tables[:COARSE], *tables[COARSE:]

        near_all, next_all = near_ref[...], next_ref[...]
        below = jnp.where(even, near_all, next_all)
        above = jnp.where(even, next_all, near_all)
        outer = jnp.concatenate([mis_ref[...], below[0:HALO], above[0:HALO]], axis=0)
        weight = jnp.concatenate([wt_ref[...], below[HALO:], above[HALO:]], axis=0)

        masks = []
        for k in range(LEVELS):
            s = SPACINGS[k]
            masks.append(
                side_mask(plan.node_rows[k], rows // s, HALO // s, lat, plan.lat_total - 1, 0)
                * side_mask(plan.node_cols[k], cols // s, HALO // s, lon, lon_total - 1, 1)
            )
        inner_mask = side_mask(inner_rows, rows, INNER, lat, plan.lat_total - 1, 0) * side_mask(
            plan.col_frame, cols, HALO, lon, lon_total - 1, 1
        )

        def collect(values, row_table):
            gathered = dot3(row_table, split(values))
            return [
                dot3(split(gathered[starts[k] : starts[k + 1]]), col_tables[k]) for k in range(COARSE)
            ]

        def spread(coeffs):
            return split(
                jnp.concatenate([dot3(split(coeffs[k]), col_tables[k], (1, 1)) for k in range(COARSE)], axis=0)
            )

        def cut(x):
            return jnp.concatenate([x[0 : rows + INNER], x[x.shape[0] - INNER :]], axis=0)

        base = collect(outer, outer_t)
        base = [base[k] * masks[k] for k in range(COARSE)]
        finest = smooth(outer) * masks[COARSE]
        surface = dot3(inner_s, spread(base)) + cut(smooth(finest))
        base.append(cut(finest))
        masks[COARSE] = inner_mask

        image = collect(weight * surface, inner_t)
        image.append(smooth(weight * surface))
        rough_base, rough_image = [], []
        for k in range(LEVELS):
            once = autoreg(base[k]) * masks[k]
            rough_base.append(once)
            image[k] = (image[k] + level_scales[k] * autoreg(once)) * masks[k]
            rough_image.append(autoreg(image[k]))
        tile_table = tuple(part[0:rows] for part in inner_s)
        second = dot3(tile_table, spread(image)) + smooth(image[COARSE])[0:rows]

        own = [(slice(0, rows // s), slice(0, cols // s)) for s in SPACINGS]
        b = [base[k][own[k]] for k in range(LEVELS)]
        ab = [image[k][own[k]] for k in range(LEVELS)]
        rb = [rough_base[k][own[k]] for k in range(LEVELS)]
        rab = [rough_image[k][own[k]] for k in range(LEVELS)]
        sb, sab = surface[0:rows, 0:cols], second[:, 0:cols]
        w = weight[0:rows, 0:cols]

        for k in range(LEVELS):
            base_refs[k][...] = b[k]
            image_refs[k][...] = ab[k]
        surface_refs[0][0:rows, :] = sb
        surface_refs[0][rows:, :] = sab
        for k in range(1, lon_total):
            take = pl.ds(pl.multiple_of((lon ^ k) * sr, sr), sr)
            surface_refs[k][0:sr, :] = surface_refs[0][take, :]
            take = pl.ds(pl.multiple_of(rows + (lon ^ k) * sr, sr), sr)
            surface_refs[k][sr:, :] = surface_refs[0][take, :]

        def inner(first, other):
            total = fold(first[0] * other[0])
            for k in range(1, LEVELS):
                total = total + fold(first[k] * other[k])
            return total

        def curvature(first, other, field, other_field):
            total = fold(w * field * other_field)
            for k in range(LEVELS):
                total = total + level_scales[k] * fold(first[k] * other[k])
            return total

        a0 = inner(b, b)
        a1 = curvature(rb, rb, sb, sb)
        top = jnp.sum(a0, keepdims=True)
        bottom = jnp.sum(a1, keepdims=True)
        tau = jnp.where(bottom > 0.0, top / jnp.where(bottom > 0.0, bottom, 1.0), 0.0)
        r = [b[k] - tau * ab[k] for k in range(LEVELS)]
        rr = [rb[k] - tau * rab[k] for k in range(LEVELS)]
        sr_field = sb - tau * sab
        blocks = [
            a0,
            a1,
            inner(r, r),
            inner(r, ab),
            inner(ab, ab),
            curvature(rr, rr, sr_field, sr_field),
            curvature(rr, rab, sr_field, sab),
            curvature(rab, rab, sab, sab),
            curvature(rr, rb, sr_field, sb),
            curvature(rab, rb, sab, sb),
        ]
        lines = [jnp.sum(block, axis=0, keepdims=True) for block in blocks]
        lane = lax.broadcasted_iota(jnp.int32, (1, LANES), 1)
        lines.append(jnp.where(lane == 0, tau, 0.0))
        lines.append(jnp.zeros((16 - len(lines), LANES), jnp.float32))
        sums = jnp.sum(jnp.concatenate(lines, axis=0), axis=1, keepdims=True)
        place = lax.broadcasted_iota(jnp.int32, (16, LANES), 0)
        lanes = lax.broadcasted_iota(jnp.int32, (16, LANES), 1)
        line = jnp.sum(jnp.where(place == lanes, sums, 0.0), axis=0, keepdims=True)
        part_ref[...] = jnp.broadcast_to(line, (n_dev, LANES))

    level_shapes = [(rows // s, cols // s) for s in SPACINGS]
    outs = level_shapes * 2 + [(2 * rows, cols)] + [(2 * sr, cols)] * (lon_total - 1) + [(n_dev, LANES)]
    tables = [jnp.asarray(t) for t in plan.tables]
    results = call(kernel, outs)(mis, wt, near, following, *tables)
    return results[:LEVELS], results[LEVELS : 2 * LEVELS], results[2 * LEVELS : -1], results[-1]


def finish(plan, parts, base, image, own_surface, far_surfaces):
    rows, cols, sr, lon_total = plan.rows, plan.cols, plan.swath_rows, plan.lon_total

    def kernel(part_ref, *rest):
        base_refs, image_refs = rest[:LEVELS], rest[LEVELS : 2 * LEVELS]
        own_ref, far_refs = rest[2 * LEVELS], rest[2 * LEVELS + 1 : 2 * LEVELS + lon_total]
        out_refs, swath_ref = rest[-LEVELS - 1 : -1], rest[-1]
        lon = lax.axis_index("lon")
        part = part_ref[...]
        lane = lax.broadcasted_iota(jnp.int32, part.shape, 1)

        def column(n):
            return jnp.sum(jnp.where(lane == n, part, 0.0), axis=1, keepdims=True)

        def total(values):
            return jnp.sum(values, axis=0, keepdims=True)

        a0, a1, p1, p2, p3, c1, c2, c3, c4, c5, tau = [column(n) for n in range(11)]
        sum0, sum1 = total(a0), total(a1)
        step = sum0 / sum1
        gap = tau - step
        norm = total(p1 + 2.0 * gap * p2 + gap * gap * p3)
        curv_res = total(c1 + 2.0 * gap * c2 + gap * gap * c3)
        curv_mix = total(c4 + gap * c5)
        ratio = norm / sum0
        curv = curv_res + 2.0 * ratio * curv_mix + ratio * ratio * sum1
        next_step = norm / curv
        alpha = step + next_step * (1.0 + ratio)
        beta = -next_step * step
        for k in range(LEVELS):
            out_refs[k][...] = alpha * base_refs[k][...] + beta * image_refs[k][...]
        take = pl.ds(pl.multiple_of(lon * sr, sr), sr)
        later = pl.ds(pl.multiple_of(rows + lon * sr, sr), sr)
        fields = [(own_ref[take, :], own_ref[later, :])]
        fields += [(ref[0:sr, :], ref[sr:, :]) for ref in far_refs]
        for k in range(lon_total):
            here = pl.ds(pl.multiple_of((lon ^ k) * cols, LANES), cols)
            swath_ref[:, here] = alpha * fields[k][0] + beta * fields[k][1]

    outs = [(rows // s, cols // s) for s in SPACINGS] + [(sr, plan.width)]
    return call(kernel, outs)(parts, *base, *image, own_surface, *far_surfaces)


def flip(x, axis, total, k):
    return lax.ppermute(x, axis, [(i, i ^ k) for i in range(total)])


def odd_swap(x, axis, total):
    pairs = [(i, i + 1) for i in range(1, total - 1, 2)]
    return lax.ppermute(x, axis, pairs + [(j, i) for i, j in pairs])


def body(observed, gauged):
    lat_total, lon_total = lax.axis_size("lat"), lax.axis_size("lon")
    plan = Plan(observed.shape, gauged.shape, lat_total, lon_total)
    own, pair, *far, odd = pack(plan, observed, gauged)
    far = [flip(x, "lon", lon_total, k) for k, x in enumerate(far, 2)]
    odd = odd_swap(odd, "lon", lon_total)
    pair = flip(pair, "lon", lon_total, 1)
    mis, wt, near, following = misfit(plan, own, pair, far, odd, gauged)
    following = odd_swap(following, "lat", lat_total)
    near = flip(near, "lat", lat_total, 1)
    base, image, surfaces, parts = operate(plan, mis, wt, near, following)
    far_surfaces = [flip(x, "lon", lon_total, k) for k, x in enumerate(surfaces[1:], 1)]
    parts = lax.all_to_all(parts, ("lat", "lon"), split_axis=0, concat_axis=0, tiled=True)
    return tuple(finish(plan, parts, base, image, surfaces[0], far_surfaces))


def solution(mesh):
    return jax.shard_map(
        body,
        mesh=mesh,
        in_specs=(P(("lat", "lon"), None), P("lat", "lon")),
        out_specs=(
            P("lat", "lon"),
            P("lat", "lon"),
            P("lat", "lon"),
            P("lat", "lon"),
            P(("lat", "lon"), None),
        ),
        check_vma=False,
    )
```

profile of v0, /device:TPU:0, one launch (start us, length us, event | category | flops | bytes accessed | tf_op | source)
XLA Modules:
  0.0 49.2 jit_solution(11761728345098096516)
XLA Ops:
  0.6 0.0 copy-start
  0.6 0.9 %copy-done = s32[128,512]{1,0:T(8,128)S(1)} copy-done((s32[128,512]{1,0:T(8,128)S(1)}, s32[128,512]{1,0:T(8,128)}, u32[]{:S(2)}) %copy-start) | copy-done | bytes 262168
  1.6 0.9 %copy-done.5 = f32[32,2048]{1,0:T(8,128)S(1)} copy-done((f32[32,2048]{1,0:T(8,128)S(1)}, f32[32,2048]{1,0:T(8,128)}, u32[]{:S(2)}) %copy-start.5) | copy-done | bytes 262168
  2.5 0.1 shard_map.119
  2.6 0.5 %collective-permute-start = (f32[288,128]{1,0:T(8,128)S(1)}, f32[288,128]{1,0:T(8,128)S(1)}, u32[]{:S(2)}, u32[]{:S(2)}) collective-permute-start(f32[288,128]{1,0:T(8,128)S(1)} %get-tuple-element.28), channel_id=1, source_target_pairs={{0,1},{1,0},{2,3},{3,2},{4,5},{5,4},{6,7},{7,6},{8,9},{9,8},{10,11... | collective-permute-start | bytes 442376 | tf_op jit(solution)/shard_map/ppermute | solution.py:401
  3.1 2.6 %collective-permute-start.2 = (f32[32,640]{1,0:T(8,128)S(1)}, f32[32,640]{1,0:T(8,128)S(1)}, u32[]{:S(2)}, u32[]{:S(2)}) collective-permute-start(f32[32,640]{1,0:T(8,128)S(1)} %get-tuple-element.30), channel_id=1, source_target_pairs={{0,2},{1,3},{2,0},{3,1},{4,6},{5,7},{6,4},{7,5},{8,10},{9,11},{10,... | collective-permute-start | bytes 245768 | tf_op jit(solution)/shard_map/ppermute | solution.py:401
  5.7 0.1 collective-permute-start.3
  5.8 0.7 %collective-permute-start.1 = (f32[128,128]{1,0:T(8,128)S(1)}, f32[128,128]{1,0:T(8,128)S(1)}, u32[]{:S(2)}, u32[]{:S(2)}) collective-permute-start(f32[128,128]{1,0:T(8,128)S(1)} %get-tuple-element.29), channel_id=1, source_target_pairs={{1,2},{2,1},{5,6},{6,5},{9,10},{10,9},{13,14},{14,13},{17,18},{18,... | collective-permute-start | bytes 196616 | tf_op jit(solution)/shard_map/ppermute | solution.py:406
  6.4 0.0 collective-permute-done.1.odd_ref
  6.4 2.3 %collective-permute-done.2.rest_0_ = f32[32,640]{1,0:T(8,128)S(1)} collective-permute-done((f32[32,640]{1,0:T(8,128)S(1)}, f32[32,640]{1,0:T(8,128)S(1)}, u32[]{:S(2)}, u32[]{:S(2)}) %collective-permute-start.2) | collective-permute-done | bytes 81952 | tf_op jit(solution)/shard_map/ppermute | solution.py:401
  8.7 1.5 %collective-permute-done.3.rest_1_ = f32[32,640]{1,0:T(8,128)S(1)} collective-permute-done((f32[32,640]{1,0:T(8,128)S(1)}, f32[32,640]{1,0:T(8,128)S(1)}, u32[]{:S(2)}, u32[]{:S(2)}) %collective-permute-start.3) | collective-permute-done | bytes 81952 | tf_op jit(solution)/shard_map/ppermute | solution.py:401
  10.2 0.0 collective-permute-done.pair_ref
  10.2 0.0 copy-done.1
  10.2 0.1 shard_map.120
  10.3 1.8 %collective-permute-start.4 = (f32[96,640]{1,0:T(8,128)S(1)}, f32[96,640]{1,0:T(8,128)S(1)}, u32[]{:S(2)}, u32[]{:S(2)}) collective-permute-start(f32[96,640]{1,0:T(8,128)S(1)} %get-tuple-element.34), channel_id=1, source_target_pairs={{0,4},{4,0},{8,12},{12,8},{16,20},{20,16},{24,28},{28,24},{1,5},{5... | collective-permute-start | bytes 737288 | tf_op jit(solution)/shard_map/ppermute | solution.py:401
  12.1 0.7 %collective-permute-start.5 = (f32[96,640]{1,0:T(8,128)S(1)}, f32[96,640]{1,0:T(8,128)S(1)}, u32[]{:S(2)}, u32[]{:S(2)}) collective-permute-start(f32[96,640]{1,0:T(8,128)S(1)} %get-tuple-element.35), channel_id=1, source_target_pairs={{4,8},{12,16},{20,24},{8,4},{16,12},{24,20},{5,9},{13,17},{21,25},... | collective-permute-start | bytes 737288 | tf_op jit(solution)/shard_map/ppermute | solution.py:406
  12.8 10.5 %collective-permute-done.4.near_ref = f32[96,640]{1,0:T(8,128)S(1)} collective-permute-done((f32[96,640]{1,0:T(8,128)S(1)}, f32[96,640]{1,0:T(8,128)S(1)}, u32[]{:S(2)}, u32[]{:S(2)}) %collective-permute-start.4) | collective-permute-done | bytes 245792 | tf_op jit(solution)/shard_map/ppermute | solution.py:401
  23.3 0.0 collective-permute-done.5.next_ref
  23.3 1.1 %copy-done.3 = bf16[2,640,256]{2,1,0:T(8,128)(2,1)S(1)} copy-done((bf16[2,640,256]{2,1,0:T(8,128)(2,1)S(1)}, bf16[2,640,256]{2,1,0:T(8,128)(2,1)}, u32[]{:S(2)}) %copy-start.3) | copy-done | bytes 655384
  24.4 1.0 %copy-done.4 = bf16[2,640,128]{2,1,0:T(8,128)(2,1)S(1)} copy-done((bf16[2,640,128]{2,1,0:T(8,128)(2,1)S(1)}, bf16[2,640,128]{2,1,0:T(8,128)(2,1)}, u32[]{:S(2)}) %copy-start.4) | copy-done | bytes 327704
  25.3 0.9 %copy-done.6 = bf16[2,224,192]{2,1,0:T(8,128)(2,1)S(1)} copy-done((bf16[2,224,192]{2,1,0:T(8,128)(2,1)S(1)}, bf16[2,224,192]{2,1,0:T(8,128)(2,1)}, u32[]{:S(2)}) %copy-start.6) | copy-done | bytes 172056
  26.3 0.9 %copy-done.7 = bf16[2,224,256]{2,1,0:T(8,128)(2,1)S(1)} copy-done((bf16[2,224,256]{2,1,0:T(8,128)(2,1)S(1)}, bf16[2,224,256]{2,1,0:T(8,128)(2,1)}, u32[]{:S(2)}) %copy-start.7) | copy-done | bytes 229400
  27.2 0.9 %copy-done.8 = bf16[2,192,224]{2,1,0:T(8,128)(2,1)S(1)} copy-done((bf16[2,192,224]{2,1,0:T(8,128)(2,1)S(1)}, bf16[2,192,224]{2,1,0:T(8,128)(2,1)}, u32[]{:S(2)}) %copy-start.8) | copy-done | bytes 172056
  28.2 5.7 %shard_map.121 = (f32[16,64]{1,0:T(8,128)S(1)}, f32[32,128]{1,0:T(8,128)S(1)}, f32[64,256]{1,0:T(8,128)S(1)}, f32[128,512]{1,0:T(8,128)S(1)}, f32[16,64]{1,0:T(8...) custom-call(f32[128,640]{1,0:T(8,128)S(1)} %get-tuple-element.32.mis, ...), custom_call_target="tpu_custom_call" | custom-call | tf_op jit(solution)/shard_map/pallas_call | solution.py:138
  33.9 0.6 %collective-permute-start.6 = (f32[64,512]{1,0:T(8,128)S(1)}, f32[64,512]{1,0:T(8,128)S(1)}, u32[]{:S(2)}, u32[]{:S(2)}) collective-permute-start(f32[64,512]{1,0:T(8,128)S(1)} %get-tuple-element.46), channel_id=1, source_target_pairs={{0,1},{1,0},{2,3},{3,2},{4,5},{5,4},{6,7},{7,6},{8,9},{9,8},{10,11... | collective-permute-start | bytes 393224 | tf_op jit(solution)/shard_map/ppermute | solution.py:401
  34.4 0.6 %collective-permute-start.7 = (f32[64,512]{1,0:T(8,128)S(1)}, f32[64,512]{1,0:T(8,128)S(1)}, u32[]{:S(2)}, u32[]{:S(2)}) collective-permute-start(f32[64,512]{1,0:T(8,128)S(1)} %get-tuple-element.47), channel_id=1, source_target_pairs={{0,2},{1,3},{2,0},{3,1},{4,6},{5,7},{6,4},{7,5},{8,10},{9,11},{10,... | collective-permute-start | bytes 393224 | tf_op jit(solution)/shard_map/ppermute | solution.py:401
  35.1 0.8 %collective-permute-start.8 = (f32[64,512]{1,0:T(8,128)S(1)}, f32[64,512]{1,0:T(8,128)S(1)}, u32[]{:S(2)}, u32[]{:S(2)}) collective-permute-start(f32[64,512]{1,0:T(8,128)S(1)} %get-tuple-element.48), channel_id=1, source_target_pairs={{0,3},{1,2},{2,1},{3,0},{4,7},{5,6},{6,5},{7,4},{8,11},{9,10},{10,... | collective-permute-start | bytes 393224 | tf_op jit(solution)/shard_map/ppermute | solution.py:401
  35.9 12.3 %all_to_all.11 = f32[32,1,128]{2,1,0:T(1,128)S(1)} all-to-all(f32[32,1,128]{2,1,0:T(1,128)S(1)} %bitcast.5), channel_id=1, replica_groups=mesh['lat'=8,'lon'=4] {'lat','lon'}, dimensions={0} | all-to-all | bytes 32768 | tf_op jit(solution)/shard_map/all_to_all | solution.py:421
  48.2 0.0 collective-permute-done.6.rest_9_
  48.2 0.0 collective-permute-done.7.rest_10_
  48.2 0.0 collective-permute-done.8.rest_11_
  48.2 1.0 %shard_map.122 = (f32[16,64]{1,0:T(8,128)}, f32[32,128]{1,0:T(8,128)}, f32[64,256]{1,0:T(8,128)}, f32[128,512]{1,0:T(8,128)}, f32[32,2048]{1,0:T(8,128)}) custom-call(f32[32,128]{1,0:T(8,128)S(1)} %bitcast.4, f32[16,64]{1,0:T(8,128)S(1)} %get-tuple-element.37.rest_0_, f32[32,128]{1,0:T(8,128)S(1)} %get-tuple-element.38.rest_1_, ...), custom_call_target="tpu_custom_call" | custom-call | tf_op jit(solution)/shard_map/pallas_call | solution.py:138
  (9 shorter events, 0.0 us)
Async XLA Ops:
  0.6 1.0 %copy-start = (s32[128,512]{1,0:T(8,128)S(1)}, s32[128,512]{1,0:T(8,128)}, u32[]{:S(2)}) copy-start(s32[128,512]{1,0:T(8,128)} %gauge_ref.3) | copy-start | bytes 786436
  1.6 0.9 %copy-start.5 = (f32[32,2048]{1,0:T(8,128)S(1)}, f32[32,2048]{1,0:T(8,128)}, u32[]{:S(2)}) copy-start(f32[32,2048]{1,0:T(8,128)} %obs_ref.1) | copy-start | bytes 786436
  2.5 7.7 %copy-start.1 = (s32[128,512]{1,0:T(8,128)S(1)}, s32[128,512]{1,0:T(8,128)}, u32[]{:S(2)}) copy-start(s32[128,512]{1,0:T(8,128)} %gauge_ref.3) | copy-start | bytes 786436
  2.5 20.7 %copy-start.2 = (bf16[2,640,384]{2,1,0:T(8,128)(2,1)S(1)}, bf16[2,640,384]{2,1,0:T(8,128)(2,1)}, u32[]{:S(2)}) copy-start(bf16[2,640,384]{2,1,0:T(8,128)(2,1)} %constant.14.clone.rest_2_) | copy-start | bytes 2949124
  2.6 7.6 %collective-permute-start = (f32[288,128]{1,0:T(8,128)S(1)}, f32[288,128]{1,0:T(8,128)S(1)}, u32[]{:S(2)}, u32[]{:S(2)}) collective-permute-start(f32[288,128]{1,0:T(8,128)S(1)} %get-tuple-element.28), channel_id=1, source_target_pairs={{0,1},{1,0},{2,3},{3,2},{4,5},{5,4},{6,7},{7,6},{8,9},{9,8},{10,11... | collective-permute-start | bytes 442376 | tf_op jit(solution)/shard_map/ppermute | solution.py:401
  3.1 5.6 %collective-permute-start.2 = (f32[32,640]{1,0:T(8,128)S(1)}, f32[32,640]{1,0:T(8,128)S(1)}, u32[]{:S(2)}, u32[]{:S(2)}) collective-permute-start(f32[32,640]{1,0:T(8,128)S(1)} %get-tuple-element.30), channel_id=1, source_target_pairs={{0,2},{1,3},{2,0},{3,1},{4,6},{5,7},{6,4},{7,5},{8,10},{9,11},{10,... | collective-permute-start | bytes 245768 | tf_op jit(solution)/shard_map/ppermute | solution.py:401
  5.7 4.5 %collective-permute-start.3 = (f32[32,640]{1,0:T(8,128)S(1)}, f32[32,640]{1,0:T(8,128)S(1)}, u32[]{:S(2)}, u32[]{:S(2)}) collective-permute-start(f32[32,640]{1,0:T(8,128)S(1)} %get-tuple-element.31), channel_id=1, source_target_pairs={{0,3},{1,2},{2,1},{3,0},{4,7},{5,6},{6,5},{7,4},{8,11},{9,10},{10,... | collective-permute-start | bytes 245768 | tf_op jit(solution)/shard_map/ppermute | solution.py:401
  5.8 0.7 %collective-permute-start.1 = (f32[128,128]{1,0:T(8,128)S(1)}, f32[128,128]{1,0:T(8,128)S(1)}, u32[]{:S(2)}, u32[]{:S(2)}) collective-permute-start(f32[128,128]{1,0:T(8,128)S(1)} %get-tuple-element.29), channel_id=1, source_target_pairs={{1,2},{2,1},{5,6},{6,5},{9,10},{10,9},{13,14},{14,13},{17,18},{18,... | collective-permute-start | bytes 196616 | tf_op jit(solution)/shard_map/ppermute | solution.py:406
  10.3 13.0 %collective-permute-start.4 = (f32[96,640]{1,0:T(8,128)S(1)}, f32[96,640]{1,0:T(8,128)S(1)}, u32[]{:S(2)}, u32[]{:S(2)}) collective-permute-start(f32[96,640]{1,0:T(8,128)S(1)} %get-tuple-element.34), channel_id=1, source_target_pairs={{0,4},{4,0},{8,12},{12,8},{16,20},{20,16},{24,28},{28,24},{1,5},{5... | collective-permute-start | bytes 737288 | tf_op jit(solution)/shard_map/ppermute | solution.py:401
  12.1 11.2 %collective-permute-start.5 = (f32[96,640]{1,0:T(8,128)S(1)}, f32[96,640]{1,0:T(8,128)S(1)}, u32[]{:S(2)}, u32[]{:S(2)}) collective-permute-start(f32[96,640]{1,0:T(8,128)S(1)} %get-tuple-element.35), channel_id=1, source_target_pairs={{4,8},{12,16},{20,24},{8,4},{16,12},{24,20},{5,9},{13,17},{21,25},... | collective-permute-start | bytes 737288 | tf_op jit(solution)/shard_map/ppermute | solution.py:406
  23.3 1.1 %copy-start.3 = (bf16[2,640,256]{2,1,0:T(8,128)(2,1)S(1)}, bf16[2,640,256]{2,1,0:T(8,128)(2,1)}, u32[]{:S(2)}) copy-start(bf16[2,640,256]{2,1,0:T(8,128)(2,1)} %constant.13.clone.rest_1_) | copy-start | bytes 1966084
  24.4 1.0 %copy-start.4 = (bf16[2,640,128]{2,1,0:T(8,128)(2,1)S(1)}, bf16[2,640,128]{2,1,0:T(8,128)(2,1)}, u32[]{:S(2)}) copy-start(bf16[2,640,128]{2,1,0:T(8,128)(2,1)} %constant.12.clone.rest_0_) | copy-start | bytes 983044
  25.3 0.9 %copy-start.6 = (bf16[2,224,192]{2,1,0:T(8,128)(2,1)S(1)}, bf16[2,224,192]{2,1,0:T(8,128)(2,1)}, u32[]{:S(2)}) copy-start(bf16[2,224,192]{2,1,0:T(8,128)(2,1)} %constant.16.clone.rest_4_) | copy-start | bytes 516100
  26.3 0.9 %copy-start.7 = (bf16[2,224,256]{2,1,0:T(8,128)(2,1)S(1)}, bf16[2,224,256]{2,1,0:T(8,128)(2,1)}, u32[]{:S(2)}) copy-start(bf16[2,224,256]{2,1,0:T(8,128)(2,1)} %constant.15.clone.rest_3_) | copy-start | bytes 688132
  27.2 0.9 %copy-start.8 = (bf16[2,192,224]{2,1,0:T(8,128)(2,1)S(1)}, bf16[2,192,224]{2,1,0:T(8,128)(2,1)}, u32[]{:S(2)}) copy-start(bf16[2,192,224]{2,1,0:T(8,128)(2,1)} %constant.17.clone.rest_5_) | copy-start | bytes 516100
  33.9 14.3 %collective-permute-start.6 = (f32[64,512]{1,0:T(8,128)S(1)}, f32[64,512]{1,0:T(8,128)S(1)}, u32[]{:S(2)}, u32[]{:S(2)}) collective-permute-start(f32[64,512]{1,0:T(8,128)S(1)} %get-tuple-element.46), channel_id=1, source_target_pairs={{0,1},{1,0},{2,3},{3,2},{4,5},{5,4},{6,7},{7,6},{8,9},{9,8},{10,11... | collective-permute-start | bytes 393224 | tf_op jit(solution)/shard_map/ppermute | solution.py:401
  34.4 13.8 %collective-permute-start.7 = (f32[64,512]{1,0:T(8,128)S(1)}, f32[64,512]{1,0:T(8,128)S(1)}, u32[]{:S(2)}, u32[]{:S(2)}) collective-permute-start(f32[64,512]{1,0:T(8,128)S(1)} %get-tuple-element.47), channel_id=1, source_target_pairs={{0,2},{1,3},{2,0},{3,1},{4,6},{5,7},{6,4},{7,5},{8,10},{9,11},{10,... | collective-permute-start | bytes 393224 | tf_op jit(solution)/shard_map/ppermute | solution.py:401
  35.1 13.1 %collective-permute-start.8 = (f32[64,512]{1,0:T(8,128)S(1)}, f32[64,512]{1,0:T(8,128)S(1)}, u32[]{:S(2)}, u32[]{:S(2)}) collective-permute-start(f32[64,512]{1,0:T(8,128)S(1)} %get-tuple-element.48), channel_id=1, source_target_pairs={{0,3},{1,2},{2,1},{3,0},{4,7},{5,6},{6,5},{7,4},{8,11},{9,10},{10,... | collective-permute-start | bytes 393224 | tf_op jit(solution)/shard_map/ppermute | solution.py:401
where the time goes:
time: 49.6 us; the launch traced here: 49.2 us
  waiting for transfers between devices  14.3 us (29%)
  blocking collectives  12.3 us (25%)
  starting transfers between devices  8.28 us (17%)
  Pallas kernels  6.88 us (14%)
  local copies, waits for them, and re-layouts  6.76 us (14%)
  between operations  0.69 us (1%)
    ppermute x7, waiting for transfers between devices, flip(): return lax.ppermute(x, axis, [(i, i ^ k) for i in range(total)])  14.3 us
    all_to_all x1, blocking collectives, body(): lax.all_to_all(parts, ('lat', 'lon'), split_axis=0, concat_axis=0, tiled=...  12.3 us
    ppermute x7, starting transfers between devices, flip(): return lax.ppermute(x, axis, [(i, i ^ k) for i in range(total)])  6.97 us
    pallas_call x4, Pallas kernels, run(): pl.pallas_call(kernel, out_shape=[jax.ShapeDtypeStruct(shape, jnp.float32...  6.88 us
    unnamed x18, local copies, waits for them, and re-layouts  6.76 us
    ppermute x2, starting transfers between devices, odd_swap(): return lax.ppermute(x, axis, pairs + [(j, i) for i, j in pairs])  1.32 us
  transfers between devices with their start and end apart: 9, of which 3 were waited for; matrix products, arithmetic and copies ran while one was open for 0% of the time, Pallas kernels for 0%

commit v1 on v0

--- a/solution.py
+++ b/solution.py
@@ -13,18 +13,21 @@
 COARSE = LEVELS - 1
 HALO = 64
 INNER = 32
+RAW = 40
+PART_ROWS = 8
 LANES = 128
 
 data_weight = 2.0
 kappa_term = 5.0
 level_scales = (0.02, 0.03, 0.05, 0.08)
 
-VMEM_LIMIT = 48 * 1024 * 1024
-
-
-def wendland(distance):
-    remain = np.maximum(1.0 - distance, 0.0)
-    return remain**6 * (35.0 * distance * distance + 18.0 * distance + 3.0) / 3.0
+MIB = 1024 * 1024
+
+
+def wendland(distance, of=np):
+    remain = of.maximum(1.0 - distance, 0.0)
+    cube = remain * remain * remain
+    return cube * cube * (35.0 * distance * distance + 18.0 * distance + 3.0) / 3.0
 
 
 def frame_index(total, tile, halo):
@@ -106,148 +109,223 @@
         self.swath_rows, self.width = swath_shape
         self.rows, self.cols = tile_shape
         self.lat_total, self.lon_total = lat_total, lon_total
-        self.row_frame = self.rows + 2 * HALO
         self.col_frame = self.cols + 2 * HALO
+        self.outer_rows = self.rows + 2 * RAW
         self.inner_rows = self.rows + 2 * INNER
-        self.node_rows = [self.row_frame // s for s in SPACINGS]
+        self.node_rows = [(self.rows + 2 * HALO) // s for s in SPACINGS[:COARSE]] + [self.outer_rows]
         self.node_cols = [-(-self.col_frame // (s * LANES)) * LANES for s in SPACINGS]
         self.row_starts = np.cumsum([0] + self.node_rows[:COARSE]).tolist()
+        self.col_starts = np.cumsum([0] + self.node_cols[:COARSE]).tolist()
         col_cells = frame_index(self.col_frame, self.cols, HALO)
-        outer = frame_index(self.row_frame, self.rows, HALO)
+        outer = frame_index(self.outer_rows, self.rows, RAW)
         inner = frame_index(self.inner_rows, self.rows, INNER)
         col_tables, outer_rows, inner_rows = [], [], []
+        self.part_nodes, place_all = [], []
         for k in range(COARSE):
             s = SPACINGS[k]
+            tile = self.rows // s
             col_nodes = frame_index(self.node_cols[k], self.cols // s, HALO // s)
-            row_nodes = frame_index(self.node_rows[k], self.rows // s, HALO // s)
-            col_tables.append(halves(basis(col_cells, col_nodes, s)))
+            row_nodes = frame_index(self.node_rows[k], tile, HALO // s)
+            col_tables.append(basis(col_cells, col_nodes, s))
             outer_rows.append(basis(outer, row_nodes, s))
             inner_rows.append(basis(inner, row_nodes, s))
-        outer_all = np.concatenate(outer_rows, axis=1)
+            for away in range((RAW - 2 * s) // s, INNER // s + 2):
+                self.part_nodes.append((s, away))
+                at = self.row_starts[k]
+                place_all.append((at + tile + away, at + self.node_rows[k] - 1 - away))
+        nodes = self.row_starts[-1]
+        joins = np.zeros((2 * PART_ROWS, nodes), np.float32)
+        for n, (after_at, before_at) in enumerate(place_all):
+            joins[n, after_at] = 1.0
+            joins[PART_ROWS + n, before_at] = 1.0
+        outer_all = np.concatenate([np.concatenate(outer_rows, axis=1), joins], axis=0)
         inner_all = np.concatenate(inner_rows, axis=1)
-        self.tables = [
-            *col_tables,
-            halves(outer_all.T.copy()),
-            halves(inner_all.T.copy()),
-            halves(inner_all),
-        ]
-
-
-def call(kernel, outs, scratch=()):
+        row_tables = [outer_all.T, inner_all.T, inner_all]
+        self.row_places, at = [], 0
+        for table in row_tables:
+            self.row_places.append((at, table.shape[0], table.shape[1]))
+            at += table.shape[0]
+        lanes = -(-max(t.shape[1] for t in row_tables) // LANES) * LANES
+        col_all = np.concatenate(col_tables, axis=1)
+        self.turned_start = self.col_starts[-1] + lanes
+        whole = np.zeros((max(at, *col_all.shape), self.turned_start + self.col_frame), np.float32)
+        whole[: self.col_frame, : self.col_starts[-1]] = col_all
+        whole[: self.col_starts[-1], self.turned_start :] = col_all.T
+        for (start, height, width), table in zip(self.row_places, row_tables):
+            whole[start : start + height, self.col_starts[-1] : self.col_starts[-1] + width] = table
+        self.tables = halves(whole)
+
+
+def call(kernel, outs, limit, scratch=(), spaces=None):
     def run(*operands):
+        in_spaces = spaces or [pltpu.VMEM] * len(operands)
         return pl.pallas_call(
             kernel,
             out_shape=[jax.ShapeDtypeStruct(shape, jnp.float32) for shape in outs],
-            in_specs=[pl.BlockSpec(memory_space=pltpu.VMEM)] * len(operands),
+            in_specs=[pl.BlockSpec(memory_space=space) for space in in_spaces],
             out_specs=[pl.BlockSpec(memory_space=pltpu.VMEM)] * len(outs),
             scratch_shapes=list(scratch),
-            compiler_params=pltpu.CompilerParams(vmem_limit_bytes=VMEM_LIMIT),
+            compiler_params=pltpu.CompilerParams(vmem_limit_bytes=limit * MIB),
         )(*operands)
 
     return run
 
 
-def pack(plan, observed, gauged):
-    sr, width, cols, rows = plan.swath_rows, plan.width, plan.cols, plan.rows
-    tiles = plan.col_frame // LANES
-
-    def kernel(obs_ref, gauge_ref, own_ref, pair_ref, *rest):
-        far_refs, odd_ref, wide = rest[:-2], rest[-2], rest[-1]
+def opposite(plan, observed):
+    sr, width, cols, n = plan.swath_rows, plan.width, plan.cols, plan.lon_total
+
+    def kernel(obs_ref, *out_refs):
         at = lax.axis_index("lon")
-        wide[:, 0:LANES] = jnp.zeros((sr, LANES), jnp.float32)
-        wide[:, LANES : LANES + width] = obs_ref[...]
-        wide[:, LANES + width :] = jnp.zeros((sr, LANES), jnp.float32)
-        lane = lax.broadcasted_iota(jnp.int32, (sr, LANES), 1)
-
-        def window(to):
-            base = pl.multiple_of(to * cols, LANES)
-            before = wide[:, pl.ds(base, LANES)]
-            after = wide[:, pl.ds(base + LANES + cols, LANES)]
-            return wide[:, pl.ds(base + LANES, cols)], jnp.where(lane < HALO, after, before)
-
-        for k, ref in [(0, own_ref)] + list(enumerate(far_refs, 2)):
-            main, sides = window(at ^ k)
+        for k, ref in enumerate(out_refs, 2):
+            main, sides = window(plan, obs_ref, lax.rem(at + k, n))
             ref[:, 0:cols] = main
             ref[:, cols:] = sides
-        main, sides = window(at ^ 1)
-        for t in range(tiles - 1):
-            pair_ref[t * sr : (t + 1) * sr, :] = main[:, t * LANES : (t + 1) * LANES]
-        pair_ref[(tiles - 1) * sr : tiles * sr, :] = sides
-        even = at % 2 == 0
-        first = gauge_ref[:, 0:LANES].astype(jnp.float32)
-        last = gauge_ref[:, cols - LANES :].astype(jnp.float32)
-        pair_ref[tiles * sr :, :] = jnp.where(even, last, first)
-        odd_ref[...] = jnp.where(even, first, last)
-
-    outs = [(sr, plan.col_frame), (tiles * sr + rows, LANES)]
-    outs += [(sr, plan.col_frame)] * (plan.lon_total - 2)
-    outs += [(rows, LANES)]
-    scratch = [pltpu.VMEM((sr, width + 2 * LANES), jnp.float32)]
-    return call(kernel, outs, scratch)(observed, gauged)
-
-
-def misfit(plan, own, pair, far, odd, gauged):
-    sr, cols, rows = plan.swath_rows, plan.cols, plan.rows
+
+    return call(kernel, [(sr, plan.col_frame)] * (n - 3), 4)(observed)
+
+
+def window(plan, obs_ref, to):
+    sr, width, cols = plan.swath_rows, plan.width, plan.cols
+    base = pl.multiple_of(to * cols, LANES)
+    lane = lax.broadcasted_iota(jnp.int32, (sr, LANES), 1)
+    before = obs_ref[:, pl.ds(pl.multiple_of(jnp.maximum(base - LANES, 0), LANES), LANES)]
+    after = obs_ref[:, pl.ds(pl.multiple_of(jnp.minimum(base + cols, width - LANES), LANES), LANES)]
+    before = jnp.where(to > 0, before, 0.0)
+    after = jnp.where(to < plan.lon_total - 1, after, 0.0)
+    return obs_ref[:, pl.ds(base, cols)], jnp.where(lane < HALO, after, before)
+
+
+def beside(plan, observed, weight):
+    sr, cols, rows, n = plan.swath_rows, plan.cols, plan.rows, plan.lon_total
     tiles = plan.col_frame // LANES
 
-    def kernel(own_ref, pair_ref, odd_ref, gauge_ref, *rest):
-        far_refs, (mis_ref, wt_ref, near_ref, next_ref) = rest[:-4], rest[-4:]
+    def kernel(obs_ref, wt_ref, own_ref, right_ref, left_ref):
         at = lax.axis_index("lon")
-        lat = lax.axis_index("lat")
-        even = at % 2 == 0
+        main, sides = window(plan, obs_ref, at)
+        own_ref[:, 0:cols] = main
+        own_ref[:, cols:] = sides
+        half_lane = lax.broadcasted_iota(jnp.int32, (rows // 2, LANES), 1)
+        for ref, k in ((right_ref, 1), (left_ref, n - 1)):
+            main, sides = window(plan, obs_ref, lax.rem(at + k, n))
+            for t in range(tiles - 1):
+                ref[t * sr : (t + 1) * sr, :] = main[:, t * LANES : (t + 1) * LANES]
+            ref[(tiles - 1) * sr : tiles * sr, :] = sides
+            edge = wt_ref[:, cols - LANES :] if k == 1 else wt_ref[:, 0:LANES]
+            kept = (half_lane >= HALO) if k == 1 else (half_lane < HALO)
+            turned = pltpu.roll(edge[rows // 2 :], HALO, 1)
+            ref[tiles * sr :, :] = jnp.where(kept, edge[0 : rows // 2], turned)
+
+    side = (tiles * sr + rows // 2, LANES)
+    outs = [(sr, plan.col_frame), side, side]
+    return call(kernel, outs, 4)(observed, weight)
+
+
+def misfit(plan, own, right, left, far, weight):
+    sr, cols, rows, n = plan.swath_rows, plan.cols, plan.rows, plan.lon_total
+    tiles = plan.col_frame // LANES
+
+    def kernel(own_ref, right_ref, left_ref, wt_ref, *rest):
+        far_refs, (mis_ref, side_ref, near_ref, next_ref) = rest[: n - 3], rest[n - 3 :]
+        at = lax.axis_index("lon")
         lane = lax.broadcasted_iota(jnp.int32, (rows, LANES), 1)
-        from_pair = pair_ref[tiles * sr :, :]
-        from_odd = odd_ref[...]
-        right = jnp.where(even, from_pair, from_odd)
-        left = jnp.where(even, from_odd, from_pair)
-        wt_ref[:, 0:cols] = data_weight * gauge_ref[...].astype(jnp.float32)
-        wt_ref[:, cols:] = data_weight * jnp.where(lane < HALO, right, left)
-
-        def rows_of(k):
-            return pl.ds(pl.multiple_of((at ^ k) * sr, sr), sr)
-
-        for k, ref in [(0, own_ref)] + list(enumerate(far_refs, 2)):
-            mis_ref[rows_of(k), :] = wt_ref[rows_of(k), :] * ref[...]
-        for t in range(tiles):
-            lanes = slice(t * LANES, (t + 1) * LANES)
-            mis_ref[rows_of(1), lanes] = wt_ref[rows_of(1), lanes] * pair_ref[t * sr : (t + 1) * sr, :]
-        up = lat % 2
+
+        def side(ref, present):
+            packed = ref[tiles * sr :, :]
+            both = jnp.concatenate([packed, pltpu.roll(packed, HALO, 1)], axis=0)
+            return jnp.where(present, both, 0.0)
+
+        side_ref[...] = jnp.where(lane < HALO, side(left_ref, at < n - 1), side(right_ref, at > 0))
+
+        for k, ref in enumerate((own_ref, right_ref, *far_refs, left_ref)):
+            here = pl.ds(pl.multiple_of(lax.rem(at + (n - k), n) * sr, sr), sr)
+            if k in (1, n - 1):
+                for t in range(tiles - 1):
+                    lanes = slice(t * LANES, (t + 1) * LANES)
+                    mis_ref[here, lanes] = wt_ref[here, lanes] * ref[t * sr : (t + 1) * sr, :]
+                mis_ref[here, cols:] = side_ref[here, :] * ref[(tiles - 1) * sr : tiles * sr, :]
+            else:
+                mis_ref[here, 0:cols] = wt_ref[here, :] * ref[:, 0:cols]
+                mis_ref[here, cols:] = side_ref[here, :] * ref[:, cols:]
+
+        up = lax.axis_index("lat") % 2
+        depth = HALO - RAW
+        shape = (PART_ROWS, depth)
+        line = lax.broadcasted_iota(jnp.int32, shape, 0)
+        cell = lax.broadcasted_iota(jnp.int32, shape, 1)
         for ref, low in ((near_ref, 1 - up), (next_ref, up)):
-            ref[0:HALO, :] = mis_ref[pl.ds(pl.multiple_of(low * (rows - HALO), 8), HALO), :]
-            ref[HALO:, :] = wt_ref[pl.ds(pl.multiple_of(low * (rows - INNER), 8), INNER), :]
-
-    outs = [(rows, plan.col_frame)] * 2 + [(HALO + INNER, plan.col_frame)] * 2
-    return call(kernel, outs)(own, pair, odd, gauged, *far)
-
-
-def operate(plan, mis, wt, near, following):
+            far = mis_ref[pl.ds(pl.multiple_of(RAW + low * (rows - HALO - RAW), 8), depth), :]
+            table = jnp.zeros(shape, jnp.float32)
+            distance = jnp.where(low == 1, HALO - 1 - cell, RAW + cell)
+            for m, (s, away) in enumerate(plan.part_nodes):
+                numerator = jnp.abs(2 * distance - 2 * s * away - (s - 1)).astype(jnp.float32)
+                table = jnp.where(line == m, wendland(numerator / (5.0 * s), jnp) / math.sqrt(s), table)
+            ref[0:RAW, :] = mis_ref[pl.ds(pl.multiple_of(low * (rows - RAW), 8), RAW), :]
+            ref[RAW : RAW + PART_ROWS, :] = jnp.dot(
+                table, far, precision=lax.Precision.HIGHEST, preferred_element_type=jnp.float32
+            )
+            edge = pl.ds(pl.multiple_of(low * (rows - INNER), 8), INNER)
+            ref[RAW + PART_ROWS :, 0:cols] = wt_ref[edge, :]
+            ref[RAW + PART_ROWS :, cols:] = side_ref[edge, :]
+
+    outs = [(rows, plan.col_frame), (rows, LANES)] + [(RAW + PART_ROWS + INNER, plan.col_frame)] * 2
+    return call(kernel, outs, 4)(own, right, left, weight, *far)
+
+
+def fetch(plan, after):
+    def kernel(table_ref, after_ref, out_ref, sem):
+        copy = pltpu.make_async_copy(table_ref, out_ref, sem)
+        copy.start()
+        copy.wait()
+
+    table = jnp.asarray(plan.tables)
+    return pl.pallas_call(
+        kernel,
+        out_shape=jax.ShapeDtypeStruct(table.shape, table.dtype),
+        in_specs=[pl.BlockSpec(memory_space=pltpu.HBM), pl.BlockSpec(memory_space=pltpu.VMEM)],
+        out_specs=pl.BlockSpec(memory_space=pltpu.VMEM),
+        scratch_shapes=[pltpu.SemaphoreType.DMA],
+        compiler_params=pltpu.CompilerParams(vmem_limit_bytes=MIB),
+        cost_estimate=pl.CostEstimate(flops=0, bytes_accessed=2 * table.nbytes, transcendentals=0),
+    )(table, after)
+
+
+def operate(plan, mis, wt, side, near, following, tables):
     rows, cols, sr, lon_total = plan.rows, plan.cols, plan.swath_rows, plan.lon_total
     starts = plan.row_starts
     inner_rows = plan.inner_rows
-    n_tables = len(plan.tables)
     n_dev = plan.lat_total * lon_total
 
-    def kernel(mis_ref, wt_ref, near_ref, next_ref, *rest):
-        table_refs, out_refs = rest[:n_tables], rest[n_tables:]
+    def kernel(mis_ref, wt_ref, side_ref, near_ref, next_ref, table_ref, *out_refs):
         base_refs, image_refs = out_refs[:LEVELS], out_refs[LEVELS : 2 * LEVELS]
         surface_refs, part_ref = out_refs[2 * LEVELS : -1], out_refs[-1]
         lat = lax.axis_index("lat")
         lon = lax.axis_index("lon")
         even = lat % 2 == 0
-        tables = [(ref[0], ref[1]) for ref in table_refs]
-        col_tables, outer_t, inner_t, inner_s = tables[:COARSE], *tables[COARSE:]
+        col_tables, turned_tables, row_tables = [], [], []
+        for k in range(COARSE):
+            places = slice(plan.col_starts[k], plan.col_starts[k + 1])
+            turned_tables.append(tuple(table_ref[half, places, plan.turned_start :] for half in (0, 1)))
+            lanes = slice(plan.col_starts[k], plan.col_starts[k + 1])
+            col_tables.append(tuple(table_ref[half, 0 : plan.col_frame, lanes] for half in (0, 1)))
+        for start, height, width in plan.row_places:
+            lanes = slice(plan.col_starts[-1], plan.col_starts[-1] + width)
+            row_tables.append(tuple(table_ref[half, start : start + height, lanes] for half in (0, 1)))
+        outer_t, inner_t, inner_s = row_tables
 
         near_all, next_all = near_ref[...], next_ref[...]
         below = jnp.where(even, near_all, next_all)
         above = jnp.where(even, next_all, near_all)
-        outer = jnp.concatenate([mis_ref[...], below[0:HALO], above[0:HALO]], axis=0)
-        weight = jnp.concatenate([wt_ref[...], below[HALO:], above[HALO:]], axis=0)
+        cells = jnp.concatenate([mis_ref[...], below[0:RAW], above[0:RAW]], axis=0)
+        sums = slice(RAW, RAW + PART_ROWS)
+        outer = jnp.concatenate([cells, below[sums], above[sums]], axis=0)
+        own_weight = jnp.concatenate([wt_ref[...], side_ref[...]], axis=1)
+        weight = jnp.concatenate([own_weight, below[RAW + PART_ROWS :], above[RAW + PART_ROWS :]], axis=0)
 
         masks = []
         for k in range(LEVELS):
             s = SPACINGS[k]
             masks.append(
-                side_mask(plan.node_rows[k], rows // s, HALO // s, lat, plan.lat_total - 1, 0)
+                side_mask(plan.node_rows[k], rows // s, (HALO if k < COARSE else RAW) // s, lat, plan.lat_total - 1, 0)
                 * side_mask(plan.node_cols[k], cols // s, HALO // s, lon, lon_total - 1, 1)
             )
         inner_mask = side_mask(inner_rows, rows, INNER, lat, plan.lat_total - 1, 0) * side_mask(
@@ -262,7 +340,7 @@
 
         def spread(coeffs):
             return split(
-                jnp.concatenate([dot3(split(coeffs[k]), col_tables[k], (1, 1)) for k in range(COARSE)], axis=0)
+                jnp.concatenate([dot3(split(coeffs[k]), turned_tables[k]) for k in range(COARSE)], axis=0)
             )
 
         def cut(x):
@@ -270,7 +348,7 @@
 
         base = collect(outer, outer_t)
         base = [base[k] * masks[k] for k in range(COARSE)]
-        finest = smooth(outer) * masks[COARSE]
+        finest = smooth(cells) * masks[COARSE]
         surface = dot3(inner_s, spread(base)) + cut(smooth(finest))
         base.append(cut(finest))
         masks[COARSE] = inner_mask
@@ -349,8 +427,7 @@
 
     level_shapes = [(rows // s, cols // s) for s in SPACINGS]
     outs = level_shapes * 2 + [(2 * rows, cols)] + [(2 * sr, cols)] * (lon_total - 1) + [(n_dev, LANES)]
-    tables = [jnp.asarray(t) for t in plan.tables]
-    results = call(kernel, outs)(mis, wt, near, following, *tables)
+    results = call(kernel, outs, 24)(mis, wt, side, near, following, tables)
     return results[:LEVELS], results[LEVELS : 2 * LEVELS], results[2 * LEVELS : -1], results[-1]
 
 
@@ -394,7 +471,11 @@
             swath_ref[:, here] = alpha * fields[k][0] + beta * fields[k][1]
 
     outs = [(rows // s, cols // s) for s in SPACINGS] + [(sr, plan.width)]
-    return call(kernel, outs)(parts, *base, *image, own_surface, *far_surfaces)
+    return call(kernel, outs, 8)(parts, *base, *image, own_surface, *far_surfaces)
+
+
+def turn(x, axis, total, k):
+    return lax.ppermute(x, axis, [(i, (i + k) % total) for i in range(total)])
 
 
 def flip(x, axis, total, k):
@@ -409,14 +490,17 @@
 def body(observed, gauged):
     lat_total, lon_total = lax.axis_size("lat"), lax.axis_size("lon")
     plan = Plan(observed.shape, gauged.shape, lat_total, lon_total)
-    own, pair, *far, odd = pack(plan, observed, gauged)
-    far = [flip(x, "lon", lon_total, k) for k, x in enumerate(far, 2)]
-    odd = odd_swap(odd, "lon", lon_total)
-    pair = flip(pair, "lon", lon_total, 1)
-    mis, wt, near, following = misfit(plan, own, pair, far, odd, gauged)
+    far = opposite(plan, observed)
+    far = [turn(x, "lon", lon_total, k) for k, x in enumerate(far, 2)]
+    weight = data_weight * gauged.astype(jnp.float32)
+    own, right, left = beside(plan, observed, weight)
+    right = turn(right, "lon", lon_total, 1)
+    left = turn(left, "lon", lon_total, lon_total - 1)
+    mis, side, near, following = misfit(plan, own, right, left, far, weight)
+    tables = fetch(plan, side)
+    near = flip(near, "lat", lat_total, 1)
     following = odd_swap(following, "lat", lat_total)
-    near = flip(near, "lat", lat_total, 1)
-    base, image, surfaces, parts = operate(plan, mis, wt, near, following)
+    base, image, surfaces, parts = operate(plan, mis, weight, side, near, following, tables)
     far_surfaces = [flip(x, "lon", lon_total, k) for k, x in enumerate(surfaces[1:], 1)]
     parts = lax.all_to_all(parts, ("lat", "lon"), split_axis=0, concat_axis=0, tiled=True)
     return tuple(finish(plan, parts, base, image, surfaces[0], far_surfaces))

time: 49.6 us -> 42.7 us (0.86)
  waiting for transfers between devices: 14.3 us -> 8.14 us
  local copies, waits for them, and re-layouts: 6.76 us -> 3.39 us
  other arithmetic: 0 us -> 0.97 us
  starting transfers between devices: 8.28 us -> 9 us
  blocking collectives: 12.3 us -> 13 us
    ppermute x7 -> x4, waiting for transfers between devices: 14.3 us -> 4.19 us  [flip(): return lax.ppermute(x, axis, [(i, i ^ k) for i in range(total)])]
    ppermute x0 -> x3, starting transfers between devices: none -> 4.83 us  [turn(): return lax.ppermute(x, axis, [(i, (i + k) % total) for i in range(total)])]
    ppermute x0 -> x3, waiting for transfers between devices: none -> 3.96 us  [turn(): return lax.ppermute(x, axis, [(i, (i + k) % total) for i in range(total)])]
    ppermute x7 -> x4, starting transfers between devices: 6.97 us -> 3.51 us  [flip(): return lax.ppermute(x, axis, [(i, i ^ k) for i in range(total)])]
    unnamed x18 -> x4, local copies, waits for them, and re-layouts: 6.76 us -> 3.39 us
    mul x0 -> x1, other arithmetic: none -> 0.97 us  [body(): weight = data_weight * gauged.astype(jnp.float32)]
    all_to_all x1, blocking collectives: 12.3 us -> 13 us  [body(): lax.all_to_all(parts, ('lat', 'lon'), split_axis=0, concat_axis=0, tiled=...]
    ppermute x2 -> x1, starting transfers between devices: 1.32 us -> 0.66 us  [odd_swap(): return lax.ppermute(x, axis, pairs + [(j, i) for i, j in pairs])]
  transfers between devices with their start and end apart: 9 -> 8, of which waited for: 3 -> 2; matrix products, arithmetic and copies ran while one was open for 0% -> 0% of each run, Pallas kernels for 0% -> 1%
where the time goes in v1:
time: 42.7 us; the launch traced here: 42.5 us
  blocking collectives  13 us (30%)
  starting transfers between devices  9 us (21%)
  waiting for transfers between devices  8.14 us (19%)
  Pallas kernels  7.28 us (17%)
  local copies, waits for them, and re-layouts  3.39 us (8%)
  other arithmetic  0.97 us (2%)
  between operations  0.69 us (2%)
    all_to_all x1, blocking collectives, body(): lax.all_to_all(parts, ('lat', 'lon'), split_axis=0, concat_axis=0, tiled=...  13 us
    pallas_call x5, Pallas kernels, run(): pl.pallas_call(kernel, out_shape=[jax.ShapeDtypeStruct(shape, jnp.float32...  6.77 us
    ppermute x3, starting transfers between devices, turn(): return lax.ppermute(x, axis, [(i, (i + k) % total) for i in range(total)])  4.83 us
    ppermute x4, waiting for transfers between devices, flip(): return lax.ppermute(x, axis, [(i, i ^ k) for i in range(total)])  4.19 us
    ppermute x3, waiting for transfers between devices, turn(): return lax.ppermute(x, axis, [(i, (i + k) % total) for i in range(total)])  3.96 us
    ppermute x4, starting transfers between devices, flip(): return lax.ppermute(x, axis, [(i, i ^ k) for i in range(total)])  3.51 us
    unnamed x4, local copies, waits for them, and re-layouts  3.39 us
    mul x1, other arithmetic, body(): weight = data_weight * gauged.astype(jnp.float32)  0.97 us
  transfers between devices with their start and end apart: 8, of which 2 were waited for; matrix products, arithmetic and copies ran while one was open for 0% of the time, Pallas kernels for 1%

profile of v1, /device:TPU:0, one launch (start us, length us, event | category | flops | bytes accessed | tf_op | source)
XLA Modules:
  0.0 42.5 jit_solution(2186721894088495615)
XLA Ops:
  0.6 1.0 %convert_multiply_fusion.wt_ref = f32[128,512]{1,0:T(8,128)S(1)} fusion(s32[128,512]{1,0:T(8,128)} %param.4), kind=kLoop, calls=%fused_computation | loop fusion | flops 131072 | bytes 524288 | tf_op jit(solution)/shard_map/mul | solution.py:495
  1.6 0.0 copy-start.1
  1.6 0.9 %copy-done.1 = f32[32,2048]{1,0:T(8,128)S(1)} copy-done((f32[32,2048]{1,0:T(8,128)S(1)}, f32[32,2048]{1,0:T(8,128)}, u32[]{:S(2)}) %copy-start.1) | copy-done | bytes 262168
  2.6 0.1 shard_map.74
  2.6 0.5 %collective-permute-start = (f32[224,128]{1,0:T(8,128)S(1)}, f32[224,128]{1,0:T(8,128)S(1)}, u32[]{:S(2)}, u32[]{:S(2)}) collective-permute-start(f32[224,128]{1,0:T(8,128)S(1)} %get-tuple-element.26), channel_id=1, source_target_pairs={{0,1},{1,2},{2,3},{3,0},{4,5},{5,6},{6,7},{7,4},{8,9},{9,10},{10,1... | collective-permute-start | bytes 344072 | tf_op jit(solution)/shard_map/ppermute | solution.py:478
  3.2 2.0 %collective-permute-start.1 = (f32[224,128]{1,0:T(8,128)S(1)}, f32[224,128]{1,0:T(8,128)S(1)}, u32[]{:S(2)}, u32[]{:S(2)}) collective-permute-start(f32[224,128]{1,0:T(8,128)S(1)} %get-tuple-element.27), channel_id=1, source_target_pairs={{0,3},{1,0},{2,1},{3,2},{4,7},{5,4},{6,5},{7,6},{8,11},{9,8},{10,9... | collective-permute-start | bytes 344072 | tf_op jit(solution)/shard_map/ppermute | solution.py:478
  5.2 2.3 %collective-permute-start.2 = (f32[32,640]{1,0:T(8,128)S(1)}, f32[32,640]{1,0:T(8,128)S(1)}, u32[]{:S(2)}, u32[]{:S(2)}) collective-permute-start(f32[32,640]{1,0:T(8,128)S(1)} %shard_map.75), channel_id=1, source_target_pairs={{0,2},{1,3},{2,0},{3,1},{4,6},{5,7},{6,4},{7,5},{8,10},{9,11},{10,... | collective-permute-start | bytes 245768 | tf_op jit(solution)/shard_map/ppermute | solution.py:478
  7.5 4.0 %collective-permute-done.2.rest_0_ = f32[32,640]{1,0:T(8,128)S(1)} collective-permute-done((f32[32,640]{1,0:T(8,128)S(1)}, f32[32,640]{1,0:T(8,128)S(1)}, u32[]{:S(2)}, u32[]{:S(2)}) %collective-permute-start.2) | collective-permute-done | bytes 81952 | tf_op jit(solution)/shard_map/ppermute | solution.py:478
  11.4 0.0 collective-permute-done.right_ref
  11.4 0.0 collective-permute-done.1.left_ref
  11.5 0.3 shard_map.76
  11.7 1.5 %collective-permute-start.3 = (f32[80,640]{1,0:T(8,128)S(1)}, f32[80,640]{1,0:T(8,128)S(1)}, u32[]{:S(2)}, u32[]{:S(2)}) collective-permute-start(f32[80,640]{1,0:T(8,128)S(1)} %get-tuple-element.30), channel_id=1, source_target_pairs={{0,4},{4,0},{8,12},{12,8},{16,20},{20,16},{24,28},{28,24},{1,5},{5... | collective-permute-start | bytes 614408 | tf_op jit(solution)/shard_map/ppermute | solution.py:482
  13.3 0.7 %collective-permute-start.4 = (f32[80,640]{1,0:T(8,128)S(1)}, f32[80,640]{1,0:T(8,128)S(1)}, u32[]{:S(2)}, u32[]{:S(2)}) collective-permute-start(f32[80,640]{1,0:T(8,128)S(1)} %get-tuple-element.31), channel_id=1, source_target_pairs={{4,8},{12,16},{20,24},{8,4},{16,12},{24,20},{5,9},{13,17},{21,25},... | collective-permute-start | bytes 614408 | tf_op jit(solution)/shard_map/ppermute | solution.py:487
  13.9 0.0 copy-start
  13.9 2.4 %copy-done = bf16[2,768,1664]{2,1,0:T(8,128)(2,1)S(1)} copy-done((bf16[2,768,1664]{2,1,0:T(8,128)(2,1)S(1)}, bf16[2,768,1664]{2,1,0:T(8,128)(2,1)}, u32[]{:S(2)}) %copy-start) | copy-done | bytes 5111832
  16.4 0.5 %shard_map.77.table_ref = bf16[2,768,1664]{2,1,0:T(8,128)(2,1)S(1)} custom-call(bf16[2,768,1664]{2,1,0:T(8,128)(2,1)S(1)} %copy-done, f32[128,128]{1,0:T(8,128)S(1)} %get-tuple-element.29.after_ref.side_ref), custom_call_target="tpu_custom_call" | custom-call | bytes 10223616 | tf_op jit(solution)/shard_map/pallas_call | solution.py:281
  16.9 4.2 %collective-permute-done.3.near_ref = f32[80,640]{1,0:T(8,128)S(1)} collective-permute-done((f32[80,640]{1,0:T(8,128)S(1)}, f32[80,640]{1,0:T(8,128)S(1)}, u32[]{:S(2)}, u32[]{:S(2)}) %collective-permute-start.3) | collective-permute-done | bytes 204832 | tf_op jit(solution)/shard_map/ppermute | solution.py:482
  21.1 0.0 collective-permute-done.4.next_ref
  21.1 5.4 %shard_map.78 = (f32[16,64]{1,0:T(8,128)S(1)}, f32[32,128]{1,0:T(8,128)S(1)}, f32[64,256]{1,0:T(8,128)S(1)}, f32[128,512]{1,0:T(8,128)S(1)}, f32[16,64]{1,0:T(8,...) custom-call(f32[128,640]{1,0:T(8,128)S(1)} %get-tuple-element.28.mis, ...), custom_call_target="tpu_custom_call" | custom-call | tf_op jit(solution)/shard_map/pallas_call | solution.py:162
  26.4 0.0 collective-permute-start.5
  26.5 1.9 %collective-permute-start.6 = (f32[64,512]{1,0:T(8,128)S(1)}, f32[64,512]{1,0:T(8,128)S(1)}, u32[]{:S(2)}, u32[]{:S(2)}) collective-permute-start(f32[64,512]{1,0:T(8,128)S(1)} %get-tuple-element.43), channel_id=1, source_target_pairs={{0,2},{1,3},{2,0},{3,1},{4,6},{5,7},{6,4},{7,5},{8,10},{9,11},{10,... | collective-permute-start | bytes 393224 | tf_op jit(solution)/shard_map/ppermute | solution.py:482
  28.4 0.1 collective-permute-start.7
  28.5 13.0 %all_to_all.11 = f32[32,1,128]{2,1,0:T(1,128)S(1)} all-to-all(f32[32,1,128]{2,1,0:T(1,128)S(1)} %bitcast.5), channel_id=1, replica_groups=mesh['lat'=8,'lon'=4] {'lat','lon'}, dimensions={0} | all-to-all | bytes 32768 | tf_op jit(solution)/shard_map/all_to_all | solution.py:505
  41.5 0.0 collective-permute-done.5.rest_9_
  41.5 0.0 collective-permute-done.6.rest_10_
  41.5 0.0 collective-permute-done.7.rest_11_
  41.5 1.0 %shard_map.79 = (f32[16,64]{1,0:T(8,128)}, f32[32,128]{1,0:T(8,128)}, f32[64,256]{1,0:T(8,128)}, f32[128,512]{1,0:T(8,128)}, f32[32,2048]{1,0:T(8,128)}) custom-call(f32[32,128]{1,0:T(8,128)S(1)} %bitcast.4, f32[16,64]{1,0:T(8,128)S(1)} %get-tuple-element.33.rest_0_, f32[32,128]{1,0:T(8,128)S(1)} %get-tuple-element.34.rest_1_, ...), custom_call_target="tpu_custom_call" | custom-call | tf_op jit(solution)/shard_map/pallas_call | solution.py:162
  (1 shorter events, 0.0 us)
Async XLA Ops:
  1.6 1.0 %copy-start.1 = (f32[32,2048]{1,0:T(8,128)S(1)}, f32[32,2048]{1,0:T(8,128)}, u32[]{:S(2)}) copy-start(f32[32,2048]{1,0:T(8,128)} %obs_ref.3) | copy-start | bytes 786436
  2.6 8.8 %collective-permute-start = (f32[224,128]{1,0:T(8,128)S(1)}, f32[224,128]{1,0:T(8,128)S(1)}, u32[]{:S(2)}, u32[]{:S(2)}) collective-permute-start(f32[224,128]{1,0:T(8,128)S(1)} %get-tuple-element.26), channel_id=1, source_target_pairs={{0,1},{1,2},{2,3},{3,0},{4,5},{5,6},{6,7},{7,4},{8,9},{9,10},{10,1... | collective-permute-start | bytes 344072 | tf_op jit(solution)/shard_map/ppermute | solution.py:478
  3.2 8.3 %collective-permute-start.1 = (f32[224,128]{1,0:T(8,128)S(1)}, f32[224,128]{1,0:T(8,128)S(1)}, u32[]{:S(2)}, u32[]{:S(2)}) collective-permute-start(f32[224,128]{1,0:T(8,128)S(1)} %get-tuple-element.27), channel_id=1, source_target_pairs={{0,3},{1,0},{2,1},{3,2},{4,7},{5,4},{6,5},{7,6},{8,11},{9,8},{10,9... | collective-permute-start | bytes 344072 | tf_op jit(solution)/shard_map/ppermute | solution.py:478
  5.2 6.3 %collective-permute-start.2 = (f32[32,640]{1,0:T(8,128)S(1)}, f32[32,640]{1,0:T(8,128)S(1)}, u32[]{:S(2)}, u32[]{:S(2)}) collective-permute-start(f32[32,640]{1,0:T(8,128)S(1)} %shard_map.75), channel_id=1, source_target_pairs={{0,2},{1,3},{2,0},{3,1},{4,6},{5,7},{6,4},{7,5},{8,10},{9,11},{10,... | collective-permute-start | bytes 245768 | tf_op jit(solution)/shard_map/ppermute | solution.py:478
  11.7 9.3 %collective-permute-start.3 = (f32[80,640]{1,0:T(8,128)S(1)}, f32[80,640]{1,0:T(8,128)S(1)}, u32[]{:S(2)}, u32[]{:S(2)}) collective-permute-start(f32[80,640]{1,0:T(8,128)S(1)} %get-tuple-element.30), channel_id=1, source_target_pairs={{0,4},{4,0},{8,12},{12,8},{16,20},{20,16},{24,28},{28,24},{1,5},{5... | collective-permute-start | bytes 614408 | tf_op jit(solution)/shard_map/ppermute | solution.py:482
  13.3 7.8 %collective-permute-start.4 = (f32[80,640]{1,0:T(8,128)S(1)}, f32[80,640]{1,0:T(8,128)S(1)}, u32[]{:S(2)}, u32[]{:S(2)}) collective-permute-start(f32[80,640]{1,0:T(8,128)S(1)} %get-tuple-element.31), channel_id=1, source_target_pairs={{4,8},{12,16},{20,24},{8,4},{16,12},{24,20},{5,9},{13,17},{21,25},... | collective-permute-start | bytes 614408 | tf_op jit(solution)/shard_map/ppermute | solution.py:487
  13.9 2.5 %copy-start = (bf16[2,768,1664]{2,1,0:T(8,128)(2,1)S(1)}, bf16[2,768,1664]{2,1,0:T(8,128)(2,1)}, u32[]{:S(2)}) copy-start(bf16[2,768,1664]{2,1,0:T(8,128)(2,1)} %constant.4.clone.table_ref) | copy-start | bytes 15335428
  26.4 15.0 %collective-permute-start.5 = (f32[64,512]{1,0:T(8,128)S(1)}, f32[64,512]{1,0:T(8,128)S(1)}, u32[]{:S(2)}, u32[]{:S(2)}) collective-permute-start(f32[64,512]{1,0:T(8,128)S(1)} %get-tuple-element.42), channel_id=1, source_target_pairs={{0,1},{1,0},{2,3},{3,2},{4,5},{5,4},{6,7},{7,6},{8,9},{9,8},{10,11... | collective-permute-start | bytes 393224 | tf_op jit(solution)/shard_map/ppermute | solution.py:482
  26.5 15.0 %collective-permute-start.6 = (f32[64,512]{1,0:T(8,128)S(1)}, f32[64,512]{1,0:T(8,128)S(1)}, u32[]{:S(2)}, u32[]{:S(2)}) collective-permute-start(f32[64,512]{1,0:T(8,128)S(1)} %get-tuple-element.43), channel_id=1, source_target_pairs={{0,2},{1,3},{2,0},{3,1},{4,6},{5,7},{6,4},{7,5},{8,10},{9,11},{10,... | collective-permute-start | bytes 393224 | tf_op jit(solution)/shard_map/ppermute | solution.py:482
  28.4 13.1 %collective-permute-start.7 = (f32[64,512]{1,0:T(8,128)S(1)}, f32[64,512]{1,0:T(8,128)S(1)}, u32[]{:S(2)}, u32[]{:S(2)}) collective-permute-start(f32[64,512]{1,0:T(8,128)S(1)} %get-tuple-element.44), channel_id=1, source_target_pairs={{0,3},{1,2},{2,1},{3,0},{4,7},{5,6},{6,5},{7,4},{8,11},{9,10},{10,... | collective-permute-start | bytes 393224 | tf_op jit(solution)/shard_map/ppermute | solution.py:482

commit v2 on v1

--- a/solution.py
+++ b/solution.py
@@ -60,7 +60,9 @@
 
 def dot3(a, b, contract=(1, 0)):
     (ah, al), (bh, bl) = a, b
-    return dot(ah, bh, contract) + (dot(ah, bl, contract) + dot(al, bh, contract))
+    n = ah.shape[0]
+    both = dot(jnp.concatenate([ah, al], axis=0), bh, contract)
+    return both[0:n] + (both[n:] + dot(ah, bl, contract))
 
 
 TAPS = (float(wendland(np.float64(0.4))), float(wendland(np.float64(0.8))))
@@ -165,23 +167,10 @@
             in_specs=[pl.BlockSpec(memory_space=space) for space in in_spaces],
             out_specs=[pl.BlockSpec(memory_space=pltpu.VMEM)] * len(outs),
             scratch_shapes=list(scratch),
-            compiler_params=pltpu.CompilerParams(vmem_limit_bytes=limit * MIB),
+            compiler_params=pltpu.CompilerParams(vmem_limit_bytes=int(limit * MIB)),
         )(*operands)
 
     return run
-
-
-def opposite(plan, observed):
-    sr, width, cols, n = plan.swath_rows, plan.width, plan.cols, plan.lon_total
-
-    def kernel(obs_ref, *out_refs):
-        at = lax.axis_index("lon")
-        for k, ref in enumerate(out_refs, 2):
-            main, sides = window(plan, obs_ref, lax.rem(at + k, n))
-            ref[:, 0:cols] = main
-            ref[:, cols:] = sides
-
-    return call(kernel, [(sr, plan.col_frame)] * (n - 3), 4)(observed)
 
 
 def window(plan, obs_ref, to):
@@ -195,29 +184,46 @@
     return obs_ref[:, pl.ds(base, cols)], jnp.where(lane < HALO, after, before)
 
 
-def beside(plan, observed, weight):
-    sr, cols, rows, n = plan.swath_rows, plan.cols, plan.rows, plan.lon_total
+def pack(plan, observed, gauged):
+    sr, width, cols, rows, n = plan.swath_rows, plan.width, plan.cols, plan.rows, plan.lon_total
     tiles = plan.col_frame // LANES
 
-    def kernel(obs_ref, wt_ref, own_ref, right_ref, left_ref):
+    def kernel(obs_hbm, gauge_hbm, *rest):
+        wt_ref, out_refs, (obs_ref, gauge_ref, sems) = rest[0], rest[1 : n + 1], rest[n + 1 :]
+        copies = [
+            pltpu.make_async_copy(obs_hbm, obs_ref, sems.at[0]),
+            pltpu.make_async_copy(gauge_hbm, gauge_ref, sems.at[1]),
+        ]
+        for copy in copies:
+            copy.start()
         at = lax.axis_index("lon")
-        main, sides = window(plan, obs_ref, at)
-        own_ref[:, 0:cols] = main
-        own_ref[:, cols:] = sides
         half_lane = lax.broadcasted_iota(jnp.int32, (rows // 2, LANES), 1)
-        for ref, k in ((right_ref, 1), (left_ref, n - 1)):
+        copies[0].wait()
+        for k, ref in enumerate(out_refs):
             main, sides = window(plan, obs_ref, lax.rem(at + k, n))
-            for t in range(tiles - 1):
-                ref[t * sr : (t + 1) * sr, :] = main[:, t * LANES : (t + 1) * LANES]
-            ref[(tiles - 1) * sr : tiles * sr, :] = sides
+            if k in (1, n - 1):
+                for t in range(tiles - 1):
+                    ref[t * sr : (t + 1) * sr, :] = main[:, t * LANES : (t + 1) * LANES]
+                ref[(tiles - 1) * sr : tiles * sr, :] = sides
+            else:
+                ref[:, 0:cols] = main
+                ref[:, cols:] = sides
+        copies[1].wait()
+        wt_ref[...] = data_weight * gauge_ref[...].astype(jnp.float32)
+        for k in (1, n - 1):
             edge = wt_ref[:, cols - LANES :] if k == 1 else wt_ref[:, 0:LANES]
             kept = (half_lane >= HALO) if k == 1 else (half_lane < HALO)
             turned = pltpu.roll(edge[rows // 2 :], HALO, 1)
-            ref[tiles * sr :, :] = jnp.where(kept, edge[0 : rows // 2], turned)
+            out_refs[k][tiles * sr :, :] = jnp.where(kept, edge[0 : rows // 2], turned)
 
     side = (tiles * sr + rows // 2, LANES)
-    outs = [(sr, plan.col_frame), side, side]
-    return call(kernel, outs, 4)(observed, weight)
+    outs = [(rows, cols)] + [side if k in (1, n - 1) else (sr, plan.col_frame) for k in range(n)]
+    scratch = [
+        pltpu.VMEM((sr, width), jnp.float32),
+        pltpu.VMEM((rows, cols), jnp.int32),
+        pltpu.SemaphoreType.DMA((2,)),
+    ]
+    return call(kernel, outs, 53.25, scratch, [pltpu.HBM] * 2)(observed, gauged)
 
 
 def misfit(plan, own, right, left, far, weight):
@@ -490,12 +496,8 @@
 def body(observed, gauged):
     lat_total, lon_total = lax.axis_size("lat"), lax.axis_size("lon")
     plan = Plan(observed.shape, gauged.shape, lat_total, lon_total)
-    far = opposite(plan, observed)
-    far = [turn(x, "lon", lon_total, k) for k, x in enumerate(far, 2)]
-    weight = data_weight * gauged.astype(jnp.float32)
-    own, right, left = beside(plan, observed, weight)
-    right = turn(right, "lon", lon_total, 1)
-    left = turn(left, "lon", lon_total, lon_total - 1)
+    weight, own, *windows = pack(plan, observed, gauged)
+    right, *far, left = [turn(x, "lon", lon_total, k) for k, x in enumerate(windows, 1)]
     mis, side, near, following = misfit(plan, own, right, left, far, weight)
     tables = fetch(plan, side)
     near = flip(near, "lat", lat_total, 1)

time: 42.7 us -> 41.3 us (0.967)
  other arithmetic: 0.97 us -> 0 us
  local copies, waits for them, and re-layouts: 3.39 us -> 2.44 us
  Pallas kernels: 7.28 us -> 7.76 us
    mul x1 -> x0, other arithmetic: 0.97 us -> none  [body(): weight = data_weight * gauged.astype(jnp.float32)]
    unnamed x4 -> x2, local copies, waits for them, and re-layouts: 3.39 us -> 2.44 us
    pallas_call x5 -> x4, Pallas kernels: 6.77 us -> 7.25 us  [run(): pl.pallas_call(kernel, out_shape=[jax.ShapeDtypeStruct(shape, jnp.float32...]
where the time goes in v2:
time: 41.3 us; the launch traced here: 41.1 us
  blocking collectives  13 us (31%)
  starting transfers between devices  8.99 us (22%)
  waiting for transfers between devices  8.17 us (20%)
  Pallas kernels  7.76 us (19%)
  local copies, waits for them, and re-layouts  2.44 us (6%)
  between operations  0.68 us (2%)
    all_to_all x1, blocking collectives, body(): lax.all_to_all(parts, ('lat', 'lon'), split_axis=0, concat_axis=0, tiled=...  13 us
    pallas_call x4, Pallas kernels, run(): pl.pallas_call(kernel, out_shape=[jax.ShapeDtypeStruct(shape, jnp.float32...  7.25 us
    ppermute x3, starting transfers between devices, turn(): return lax.ppermute(x, axis, [(i, (i + k) % total) for i in range(total)])  4.76 us
    ppermute x4, waiting for transfers between devices, flip(): return lax.ppermute(x, axis, [(i, i ^ k) for i in range(total)])  4.19 us
    ppermute x3, waiting for transfers between devices, turn(): return lax.ppermute(x, axis, [(i, (i + k) % total) for i in range(total)])  3.99 us
    ppermute x4, starting transfers between devices, flip(): return lax.ppermute(x, axis, [(i, i ^ k) for i in range(total)])  3.56 us
    unnamed x2, local copies, waits for them, and re-layouts  2.44 us
  transfers between devices with their start and end apart: 8, of which 2 were waited for; matrix products, arithmetic and copies ran while one was open for 0% of the time, Pallas kernels for 1%

profile of v2, /device:TPU:0, one launch (start us, length us, event | category | flops | bytes accessed | tf_op | source)
XLA Modules:
  0.0 41.1 jit_solution(16028587891417285665)
XLA Ops:
  0.6 1.1 %shard_map.74 = (f32[128,512]{1,0:T(8,128)S(1)}, f32[32,640]{1,0:T(8,128)S(1)}, f32[224,128]{1,0:T(8,128)S(1)}, f32[32,640]{1,0:T(8,128)S(1)}, f32[224,128]{1,0:T(8,128)S(1)}) custom-call(f32[32,2048]{1,0:T(8,128)} %obs_hbm.1, s32[128,512]{1,0:T(8,128)} %gauge_hbm.1), custom_call_target="tpu_custom_call" | custom-call | tf_op jit(solution)/shard_map/pallas_call | solution.py:164
  1.8 0.5 %collective-permute-start = (f32[224,128]{1,0:T(8,128)S(1)}, f32[224,128]{1,0:T(8,128)S(1)}, u32[]{:S(2)}, u32[]{:S(2)}) collective-permute-start(f32[224,128]{1,0:T(8,128)S(1)} %get-tuple-element.28), channel_id=1, source_target_pairs={{0,1},{1,2},{2,3},{3,0},{4,5},{5,6},{6,7},{7,4},{8,9},{9,10},{10,1... | collective-permute-start | bytes 344072 | tf_op jit(solution)/shard_map/ppermute | solution.py:484
  2.3 2.0 %collective-permute-start.1 = (f32[224,128]{1,0:T(8,128)S(1)}, f32[224,128]{1,0:T(8,128)S(1)}, u32[]{:S(2)}, u32[]{:S(2)}) collective-permute-start(f32[224,128]{1,0:T(8,128)S(1)} %get-tuple-element.29), channel_id=1, source_target_pairs={{0,3},{1,0},{2,1},{3,2},{4,7},{5,4},{6,5},{7,6},{8,11},{9,8},{10,9... | collective-permute-start | bytes 344072 | tf_op jit(solution)/shard_map/ppermute | solution.py:484
  4.3 2.2 %collective-permute-start.2 = (f32[32,640]{1,0:T(8,128)S(1)}, f32[32,640]{1,0:T(8,128)S(1)}, u32[]{:S(2)}, u32[]{:S(2)}) collective-permute-start(f32[32,640]{1,0:T(8,128)S(1)} %get-tuple-element.31), channel_id=1, source_target_pairs={{0,2},{1,3},{2,0},{3,1},{4,6},{5,7},{6,4},{7,5},{8,10},{9,11},{10,... | collective-permute-start | bytes 245768 | tf_op jit(solution)/shard_map/ppermute | solution.py:484
  6.5 4.0 %collective-permute-done.2.rest_0_ = f32[32,640]{1,0:T(8,128)S(1)} collective-permute-done((f32[32,640]{1,0:T(8,128)S(1)}, f32[32,640]{1,0:T(8,128)S(1)}, u32[]{:S(2)}, u32[]{:S(2)}) %collective-permute-start.2) | collective-permute-done | bytes 81952 | tf_op jit(solution)/shard_map/ppermute | solution.py:484
  10.5 0.0 collective-permute-done.right_ref
  10.5 0.0 collective-permute-done.1.left_ref
  10.5 0.3 shard_map.75
  10.8 1.5 %collective-permute-start.3 = (f32[80,640]{1,0:T(8,128)S(1)}, f32[80,640]{1,0:T(8,128)S(1)}, u32[]{:S(2)}, u32[]{:S(2)}) collective-permute-start(f32[80,640]{1,0:T(8,128)S(1)} %get-tuple-element.34), channel_id=1, source_target_pairs={{0,4},{4,0},{8,12},{12,8},{16,20},{20,16},{24,28},{28,24},{1,5},{5... | collective-permute-start | bytes 614408 | tf_op jit(solution)/shard_map/ppermute | solution.py:488
  12.3 0.7 %collective-permute-start.4 = (f32[80,640]{1,0:T(8,128)S(1)}, f32[80,640]{1,0:T(8,128)S(1)}, u32[]{:S(2)}, u32[]{:S(2)}) collective-permute-start(f32[80,640]{1,0:T(8,128)S(1)} %get-tuple-element.35), channel_id=1, source_target_pairs={{4,8},{12,16},{20,24},{8,4},{16,12},{24,20},{5,9},{13,17},{21,25},... | collective-permute-start | bytes 614408 | tf_op jit(solution)/shard_map/ppermute | solution.py:493
  13.0 0.0 copy-start
  13.0 2.4 %copy-done = bf16[2,768,1664]{2,1,0:T(8,128)(2,1)S(1)} copy-done((bf16[2,768,1664]{2,1,0:T(8,128)(2,1)S(1)}, bf16[2,768,1664]{2,1,0:T(8,128)(2,1)}, u32[]{:S(2)}) %copy-start) | copy-done | bytes 5111832
  15.5 0.5 %shard_map.76.table_ref = bf16[2,768,1664]{2,1,0:T(8,128)(2,1)S(1)} custom-call(bf16[2,768,1664]{2,1,0:T(8,128)(2,1)S(1)} %copy-done, f32[128,128]{1,0:T(8,128)S(1)} %get-tuple-element.33.after_ref.side_ref), custom_call_target="tpu_custom_call" | custom-call | bytes 10223616 | tf_op jit(solution)/shard_map/pallas_call | solution.py:287
  16.0 4.2 %collective-permute-done.3.near_ref = f32[80,640]{1,0:T(8,128)S(1)} collective-permute-done((f32[80,640]{1,0:T(8,128)S(1)}, f32[80,640]{1,0:T(8,128)S(1)}, u32[]{:S(2)}, u32[]{:S(2)}) %collective-permute-start.3) | collective-permute-done | bytes 204832 | tf_op jit(solution)/shard_map/ppermute | solution.py:488
  20.2 0.0 collective-permute-done.4.next_ref
  20.2 4.8 %shard_map.77 = (f32[16,64]{1,0:T(8,128)S(1)}, f32[32,128]{1,0:T(8,128)S(1)}, f32[64,256]{1,0:T(8,128)S(1)}, f32[128,512]{1,0:T(8,128)S(1)}, f32[16,64]{1,0:T(8,...) custom-call(f32[128,640]{1,0:T(8,128)S(1)} %get-tuple-element.32.mis, ...), custom_call_target="tpu_custom_call" | custom-call | tf_op jit(solution)/shard_map/pallas_call | solution.py:164
  25.0 0.0 collective-permute-start.5
  25.0 2.0 %collective-permute-start.6 = (f32[64,512]{1,0:T(8,128)S(1)}, f32[64,512]{1,0:T(8,128)S(1)}, u32[]{:S(2)}, u32[]{:S(2)}) collective-permute-start(f32[64,512]{1,0:T(8,128)S(1)} %get-tuple-element.47), channel_id=1, source_target_pairs={{0,2},{1,3},{2,0},{3,1},{4,6},{5,7},{6,4},{7,5},{8,10},{9,11},{10,... | collective-permute-start | bytes 393224 | tf_op jit(solution)/shard_map/ppermute | solution.py:488
  26.9 0.1 collective-permute-start.7
  27.0 13.0 %all_to_all.11 = f32[32,1,128]{2,1,0:T(1,128)S(1)} all-to-all(f32[32,1,128]{2,1,0:T(1,128)S(1)} %bitcast.5), channel_id=1, replica_groups=mesh['lat'=8,'lon'=4] {'lat','lon'}, dimensions={0} | all-to-all | bytes 32768 | tf_op jit(solution)/shard_map/all_to_all | solution.py:507
  40.0 0.0 collective-permute-done.5.rest_9_
  40.0 0.0 collective-permute-done.6.rest_10_
  40.0 0.0 collective-permute-done.7.rest_11_
  40.0 1.0 %shard_map.78 = (f32[16,64]{1,0:T(8,128)}, f32[32,128]{1,0:T(8,128)}, f32[64,256]{1,0:T(8,128)}, f32[128,512]{1,0:T(8,128)}, f32[32,2048]{1,0:T(8,128)}) custom-call(f32[32,128]{1,0:T(8,128)S(1)} %bitcast.4, f32[16,64]{1,0:T(8,128)S(1)} %get-tuple-element.37.rest_0_, f32[32,128]{1,0:T(8,128)S(1)} %get-tuple-element.38.rest_1_, ...), custom_call_target="tpu_custom_call" | custom-call | tf_op jit(solution)/shard_map/pallas_call | solution.py:164
Async XLA Ops:
  1.8 8.7 %collective-permute-start = (f32[224,128]{1,0:T(8,128)S(1)}, f32[224,128]{1,0:T(8,128)S(1)}, u32[]{:S(2)}, u32[]{:S(2)}) collective-permute-start(f32[224,128]{1,0:T(8,128)S(1)} %get-tuple-element.28), channel_id=1, source_target_pairs={{0,1},{1,2},{2,3},{3,0},{4,5},{5,6},{6,7},{7,4},{8,9},{9,10},{10,1... | collective-permute-start | bytes 344072 | tf_op jit(solution)/shard_map/ppermute | solution.py:484
  2.3 8.2 %collective-permute-start.1 = (f32[224,128]{1,0:T(8,128)S(1)}, f32[224,128]{1,0:T(8,128)S(1)}, u32[]{:S(2)}, u32[]{:S(2)}) collective-permute-start(f32[224,128]{1,0:T(8,128)S(1)} %get-tuple-element.29), channel_id=1, source_target_pairs={{0,3},{1,0},{2,1},{3,2},{4,7},{5,4},{6,5},{7,6},{8,11},{9,8},{10,9... | collective-permute-start | bytes 344072 | tf_op jit(solution)/shard_map/ppermute | solution.py:484
  4.3 6.2 %collective-permute-start.2 = (f32[32,640]{1,0:T(8,128)S(1)}, f32[32,640]{1,0:T(8,128)S(1)}, u32[]{:S(2)}, u32[]{:S(2)}) collective-permute-start(f32[32,640]{1,0:T(8,128)S(1)} %get-tuple-element.31), channel_id=1, source_target_pairs={{0,2},{1,3},{2,0},{3,1},{4,6},{5,7},{6,4},{7,5},{8,10},{9,11},{10,... | collective-permute-start | bytes 245768 | tf_op jit(solution)/shard_map/ppermute | solution.py:484
  10.8 9.3 %collective-permute-start.3 = (f32[80,640]{1,0:T(8,128)S(1)}, f32[80,640]{1,0:T(8,128)S(1)}, u32[]{:S(2)}, u32[]{:S(2)}) collective-permute-start(f32[80,640]{1,0:T(8,128)S(1)} %get-tuple-element.34), channel_id=1, source_target_pairs={{0,4},{4,0},{8,12},{12,8},{16,20},{20,16},{24,28},{28,24},{1,5},{5... | collective-permute-start | bytes 614408 | tf_op jit(solution)/shard_map/ppermute | solution.py:488
  12.3 7.8 %collective-permute-start.4 = (f32[80,640]{1,0:T(8,128)S(1)}, f32[80,640]{1,0:T(8,128)S(1)}, u32[]{:S(2)}, u32[]{:S(2)}) collective-permute-start(f32[80,640]{1,0:T(8,128)S(1)} %get-tuple-element.35), channel_id=1, source_target_pairs={{4,8},{12,16},{20,24},{8,4},{16,12},{24,20},{5,9},{13,17},{21,25},... | collective-permute-start | bytes 614408 | tf_op jit(solution)/shard_map/ppermute | solution.py:493
  13.0 2.5 %copy-start = (bf16[2,768,1664]{2,1,0:T(8,128)(2,1)S(1)}, bf16[2,768,1664]{2,1,0:T(8,128)(2,1)}, u32[]{:S(2)}) copy-start(bf16[2,768,1664]{2,1,0:T(8,128)(2,1)} %constant.2.clone.table_ref) | copy-start | bytes 15335428
  25.0 15.1 %collective-permute-start.5 = (f32[64,512]{1,0:T(8,128)S(1)}, f32[64,512]{1,0:T(8,128)S(1)}, u32[]{:S(2)}, u32[]{:S(2)}) collective-permute-start(f32[64,512]{1,0:T(8,128)S(1)} %get-tuple-element.46), channel_id=1, source_target_pairs={{0,1},{1,0},{2,3},{3,2},{4,5},{5,4},{6,7},{7,6},{8,9},{9,8},{10,11... | collective-permute-start | bytes 393224 | tf_op jit(solution)/shard_map/ppermute | solution.py:488
  25.0 15.1 %collective-permute-start.6 = (f32[64,512]{1,0:T(8,128)S(1)}, f32[64,512]{1,0:T(8,128)S(1)}, u32[]{:S(2)}, u32[]{:S(2)}) collective-permute-start(f32[64,512]{1,0:T(8,128)S(1)} %get-tuple-element.47), channel_id=1, source_target_pairs={{0,2},{1,3},{2,0},{3,1},{4,6},{5,7},{6,4},{7,5},{8,10},{9,11},{10,... | collective-permute-start | bytes 393224 | tf_op jit(solution)/shard_map/ppermute | solution.py:488
  26.9 13.1 %collective-permute-start.7 = (f32[64,512]{1,0:T(8,128)S(1)}, f32[64,512]{1,0:T(8,128)S(1)}, u32[]{:S(2)}, u32[]{:S(2)}) collective-permute-start(f32[64,512]{1,0:T(8,128)S(1)} %get-tuple-element.48), channel_id=1, source_target_pairs={{0,3},{1,2},{2,1},{3,0},{4,7},{5,6},{6,5},{7,4},{8,11},{9,10},{10,... | collective-permute-start | bytes 393224 | tf_op jit(solution)/shard_map/ppermute | solution.py:488

commit v3 on v2

--- a/solution.py
+++ b/solution.py
@@ -15,6 +15,7 @@
 INNER = 32
 RAW = 40
 PART_ROWS = 8
+NEAR = 8
 LANES = 128
 
 data_weight = 2.0
@@ -91,19 +92,6 @@
     after = (place < tile + halo) & (at < last)
     before = (place >= total - halo) & (at > 0)
     return ((place < tile) | after | before).astype(jnp.float32)
-
-
-def fold(x):
-    rows, cols = x.shape
-    total = x[0:8]
-    for r in range(8, rows, 8):
-        total = total + x[r : r + 8]
-    if cols < LANES:
-        return jnp.concatenate([total, jnp.zeros((8, LANES - cols), jnp.float32)], axis=1)
-    out = total[:, 0:LANES]
-    for c in range(LANES, cols, LANES):
-        out = out + total[:, c : c + LANES]
-    return out
 
 
 class Plan:
@@ -114,23 +102,28 @@
         self.col_frame = self.cols + 2 * HALO
         self.outer_rows = self.rows + 2 * RAW
         self.inner_rows = self.rows + 2 * INNER
-        self.node_rows = [(self.rows + 2 * HALO) // s for s in SPACINGS[:COARSE]] + [self.outer_rows]
+        wide = [-(-(self.rows // s + 2 * (INNER // s + 2)) // 16) * 16 for s in SPACINGS[:COARSE]]
+        self.node_rows = wide + [self.outer_rows]
+        self.near_rows = [min(w, self.rows // s + 2 * NEAR) for w, s in zip(wide, SPACINGS)] + [self.inner_rows]
+        self.near_starts = np.cumsum([0] + self.near_rows[:COARSE]).tolist()
         self.node_cols = [-(-self.col_frame // (s * LANES)) * LANES for s in SPACINGS]
         self.row_starts = np.cumsum([0] + self.node_rows[:COARSE]).tolist()
         self.col_starts = np.cumsum([0] + self.node_cols[:COARSE]).tolist()
         col_cells = frame_index(self.col_frame, self.cols, HALO)
         outer = frame_index(self.outer_rows, self.rows, RAW)
         inner = frame_index(self.inner_rows, self.rows, INNER)
-        col_tables, outer_rows, inner_rows = [], [], []
+        col_tables, outer_rows, inner_rows, wide_rows = [], [], [], []
         self.part_nodes, place_all = [], []
         for k in range(COARSE):
             s = SPACINGS[k]
             tile = self.rows // s
             col_nodes = frame_index(self.node_cols[k], self.cols // s, HALO // s)
-            row_nodes = frame_index(self.node_rows[k], tile, HALO // s)
+            row_nodes = frame_index(self.node_rows[k], tile, (self.node_rows[k] - tile) // 2)
+            near_nodes = frame_index(self.near_rows[k], tile, (self.near_rows[k] - tile) // 2)
             col_tables.append(basis(col_cells, col_nodes, s))
             outer_rows.append(basis(outer, row_nodes, s))
-            inner_rows.append(basis(inner, row_nodes, s))
+            wide_rows.append(basis(inner, row_nodes, s))
+            inner_rows.append(basis(inner, near_nodes, s))
             for away in range((RAW - 2 * s) // s, INNER // s + 2):
                 self.part_nodes.append((s, away))
                 at = self.row_starts[k]
@@ -142,7 +135,8 @@
             joins[PART_ROWS + n, before_at] = 1.0
         outer_all = np.concatenate([np.concatenate(outer_rows, axis=1), joins], axis=0)
         inner_all = np.concatenate(inner_rows, axis=1)
-        row_tables = [outer_all.T, inner_all.T, inner_all]
+        wide_all = np.concatenate(wide_rows, axis=1)
+        row_tables = [outer_all.T, inner_all.T, wide_all, inner_all[: self.rows]]
         self.row_places, at = [], 0
         for table in row_tables:
             self.row_places.append((at, table.shape[0], table.shape[1]))
@@ -156,6 +150,15 @@
         for (start, height, width), table in zip(self.row_places, row_tables):
             whole[start : start + height, self.col_starts[-1] : self.col_starts[-1] + width] = table
         self.tables = halves(whole)
+        tiles = self.col_frame // LANES
+        self.sums = len(self.part_nodes)
+        self.letter_rows = -(-(self.letter()[-1] + tiles * self.sums) // 8) * 8
+
+    def letter(self):
+        tiles = self.col_frame // LANES
+        weights = tiles * RAW
+        corner = weights + (tiles - 1) * INNER
+        return 0, weights, corner, corner + INNER // 2
 
 
 def call(kernel, outs, limit, scratch=(), spaces=None):
@@ -265,16 +268,41 @@
             for m, (s, away) in enumerate(plan.part_nodes):
                 numerator = jnp.abs(2 * distance - 2 * s * away - (s - 1)).astype(jnp.float32)
                 table = jnp.where(line == m, wendland(numerator / (5.0 * s), jnp) / math.sqrt(s), table)
-            ref[0:RAW, :] = mis_ref[pl.ds(pl.multiple_of(low * (rows - RAW), 8), RAW), :]
-            ref[RAW : RAW + PART_ROWS, :] = jnp.dot(
-                table, far, precision=lax.Precision.HIGHEST, preferred_element_type=jnp.float32
-            )
             edge = pl.ds(pl.multiple_of(low * (rows - INNER), 8), INNER)
-            ref[RAW + PART_ROWS :, 0:cols] = wt_ref[edge, :]
-            ref[RAW + PART_ROWS :, cols:] = side_ref[edge, :]
-
-    outs = [(rows, plan.col_frame), (rows, LANES)] + [(RAW + PART_ROWS + INNER, plan.col_frame)] * 2
+            sums = jnp.dot(table, far, precision=lax.Precision.HIGHEST, preferred_element_type=jnp.float32)
+            near = mis_ref[pl.ds(pl.multiple_of(low * (rows - RAW), 8), RAW), :]
+            raw, weights, corner, parts = plan.letter()
+            for t in range(tiles):
+                lanes = slice(t * LANES, (t + 1) * LANES)
+                ref[raw + t * RAW : raw + (t + 1) * RAW, :] = near[:, lanes]
+                if t < tiles - 1:
+                    ref[weights + t * INNER : weights + (t + 1) * INNER, :] = wt_ref[edge, lanes]
+                ref[parts + t * plan.sums : parts + (t + 1) * plan.sums, :] = sums[0 : plan.sums, lanes]
+            beside = side_ref[edge, :]
+            turned = pltpu.roll(beside[INNER // 2 :], HALO, 1)
+            some = lax.broadcasted_iota(jnp.int32, (INNER // 2, LANES), 1)
+            outer = (some < INNER) | (some >= LANES - INNER)
+            ref[corner : corner + INNER // 2, :] = jnp.where(outer, beside[0 : INNER // 2], turned)
+            ref[parts + tiles * plan.sums :, :] = jnp.zeros((plan.letter_rows - parts - tiles * plan.sums, LANES), jnp.float32)
+
+    outs = [(rows, plan.col_frame), (rows, LANES)] + [(plan.letter_rows, LANES)] * 2
     return call(kernel, outs, 4)(own, right, left, weight, *far)
+
+
+def open_letter(plan, letter):
+    tiles = plan.col_frame // LANES
+    raw, weights, corner, parts = plan.letter()
+    near = [letter[raw + t * RAW : raw + (t + 1) * RAW] for t in range(tiles)]
+    sums = [letter[parts + t * plan.sums : parts + (t + 1) * plan.sums] for t in range(tiles)]
+    sums = jnp.concatenate(sums, axis=1)
+    sums = jnp.concatenate([sums, jnp.zeros((PART_ROWS - plan.sums, plan.col_frame), jnp.float32)], axis=0)
+    rows = [letter[weights + t * INNER : weights + (t + 1) * INNER] for t in range(tiles - 1)]
+    both = letter[corner : corner + INNER // 2]
+    some = lax.broadcasted_iota(jnp.int32, (INNER // 2, LANES), 1)
+    outer = (some < INNER) | (some >= LANES - INNER)
+    beside = [jnp.where(outer, x, 0.0) for x in (both, pltpu.roll(both, HALO, 1))]
+    rows.append(jnp.concatenate(beside, axis=0))
+    return jnp.concatenate(near, axis=1), sums, jnp.concatenate(rows, axis=1)
 
 
 def fetch(plan, after):
@@ -297,8 +325,6 @@
 
 def operate(plan, mis, wt, side, near, following, tables):
     rows, cols, sr, lon_total = plan.rows, plan.cols, plan.swath_rows, plan.lon_total
-    starts = plan.row_starts
-    inner_rows = plan.inner_rows
     n_dev = plan.lat_total * lon_total
 
     def kernel(mis_ref, wt_ref, side_ref, near_ref, next_ref, table_ref, *out_refs):
@@ -316,50 +342,57 @@
         for start, height, width in plan.row_places:
             lanes = slice(plan.col_starts[-1], plan.col_starts[-1] + width)
             row_tables.append(tuple(table_ref[half, start : start + height, lanes] for half in (0, 1)))
-        outer_t, inner_t, inner_s = row_tables
+        outer_t, inner_t, wide_s, tile_s = row_tables
 
         near_all, next_all = near_ref[...], next_ref[...]
         below = jnp.where(even, near_all, next_all)
         above = jnp.where(even, next_all, near_all)
-        cells = jnp.concatenate([mis_ref[...], below[0:RAW], above[0:RAW]], axis=0)
-        sums = slice(RAW, RAW + PART_ROWS)
-        outer = jnp.concatenate([cells, below[sums], above[sums]], axis=0)
+        below, below_sums, below_wt = open_letter(plan, below)
+        above, above_sums, above_wt = open_letter(plan, above)
+        cells = jnp.concatenate([mis_ref[...], below, above], axis=0)
+        outer = jnp.concatenate([cells, below_sums, above_sums], axis=0)
         own_weight = jnp.concatenate([wt_ref[...], side_ref[...]], axis=1)
-        weight = jnp.concatenate([own_weight, below[RAW + PART_ROWS :], above[RAW + PART_ROWS :]], axis=0)
+        weight = jnp.concatenate([own_weight, below_wt, above_wt], axis=0)
 
         masks = []
         for k in range(LEVELS):
             s = SPACINGS[k]
             masks.append(
-                side_mask(plan.node_rows[k], rows // s, (HALO if k < COARSE else RAW) // s, lat, plan.lat_total - 1, 0)
+                side_mask(plan.node_rows[k], rows // s, (plan.node_rows[k] - rows // s) // 2, lat, plan.lat_total - 1, 0)
                 * side_mask(plan.node_cols[k], cols // s, HALO // s, lon, lon_total - 1, 1)
             )
-        inner_mask = side_mask(inner_rows, rows, INNER, lat, plan.lat_total - 1, 0) * side_mask(
-            plan.col_frame, cols, HALO, lon, lon_total - 1, 1
-        )
-
-        def collect(values, row_table):
+        def collect(values, row_table, starts):
             gathered = dot3(row_table, split(values))
             return [
                 dot3(split(gathered[starts[k] : starts[k + 1]]), col_tables[k]) for k in range(COARSE)
             ]
 
-        def spread(coeffs):
-            return split(
-                jnp.concatenate([dot3(split(coeffs[k]), turned_tables[k]) for k in range(COARSE)], axis=0)
-            )
-
-        def cut(x):
-            return jnp.concatenate([x[0 : rows + INNER], x[x.shape[0] - INNER :]], axis=0)
-
-        base = collect(outer, outer_t)
+        def spread(coeffs, width):
+            turned = [tuple(part[:, 0:width] for part in table) for table in turned_tables]
+            return split(jnp.concatenate([dot3(split(coeffs[k]), turned[k]) for k in range(COARSE)], axis=0))
+
+        def cut(x, k):
+            total = plan.near_rows[k]
+            if x.shape[0] == total:
+                return x
+            side = (total - rows // SPACINGS[k]) // 2
+            return jnp.concatenate([x[0 : total - side], x[x.shape[0] - side :]], axis=0)
+
+        base = collect(outer, outer_t, plan.row_starts)
         base = [base[k] * masks[k] for k in range(COARSE)]
         finest = smooth(cells) * masks[COARSE]
-        surface = dot3(inner_s, spread(base)) + cut(smooth(finest))
-        base.append(cut(finest))
-        masks[COARSE] = inner_mask
-
-        image = collect(weight * surface, inner_t)
+        surface = dot3(wide_s, spread(base, plan.col_frame)) + cut(smooth(finest), COARSE)
+        base = [cut(x, k) for k, x in enumerate(base + [finest])]
+        masks = []
+        for k in range(LEVELS):
+            tile = rows // SPACINGS[k]
+            side = (plan.near_rows[k] - tile) // 2
+            masks.append(
+                side_mask(plan.near_rows[k], tile, side, lat, plan.lat_total - 1, 0)
+                * side_mask(plan.node_cols[k], cols // SPACINGS[k], HALO // SPACINGS[k], lon, lon_total - 1, 1)
+            )
+
+        image = collect(weight * surface, inner_t, plan.near_starts)
         image.append(smooth(weight * surface))
         rough_base, rough_image = [], []
         for k in range(LEVELS):
@@ -367,8 +400,7 @@
             rough_base.append(once)
             image[k] = (image[k] + level_scales[k] * autoreg(once)) * masks[k]
             rough_image.append(autoreg(image[k]))
-        tile_table = tuple(part[0:rows] for part in inner_s)
-        second = dot3(tile_table, spread(image)) + smooth(image[COARSE])[0:rows]
+        second = dot3(tile_s, spread(image, cols)) + smooth(image[COARSE])[0:rows, 0:cols]
 
         own = [(slice(0, rows // s), slice(0, cols // s)) for s in SPACINGS]
         b = [base[k][own[k]] for k in range(LEVELS)]
@@ -389,38 +421,51 @@
             take = pl.ds(pl.multiple_of(rows + (lon ^ k) * sr, sr), sr)
             surface_refs[k][sr:, :] = surface_refs[0][take, :]
 
-        def inner(first, other):
-            total = fold(first[0] * other[0])
-            for k in range(1, LEVELS):
-                total = total + fold(first[k] * other[k])
-            return total
-
-        def curvature(first, other, field, other_field):
-            total = fold(w * field * other_field)
-            for k in range(LEVELS):
-                total = total + level_scales[k] * fold(first[k] * other[k])
-            return total
-
-        a0 = inner(b, b)
-        a1 = curvature(rb, rb, sb, sb)
+        def pieces(*arrays):
+            height, width = arrays[0].shape
+            for at in range(0, height, 8):
+                for lane in range(0, width, LANES):
+                    yield [x[at : at + 8, lane : min(lane + LANES, width)] for x in arrays]
+
+        def gather(terms):
+            totals = None
+            for values in terms:
+                totals = values if totals is None else [t + v for t, v in zip(totals, values)]
+            short = LANES - totals[0].shape[1]
+            if short:
+                totals = [jnp.concatenate([t, jnp.zeros((8, short), jnp.float32)], axis=1) for t in totals]
+            return totals
+
+        def add_levels(per_level, scaled_from):
+            out = list(per_level[0])
+            for n in range(len(out)):
+                scales = level_scales if n >= scaled_from else (1.0,) * LEVELS
+                out[n] = sum(scales[k] * per_level[k][n] for k in range(LEVELS))
+            return out
+
+        first_sums = add_levels(
+            [gather([x * x, y * y] for x, y in pieces(b[k], rb[k])) for k in range(LEVELS)], 1
+        )
+        a0 = first_sums[0]
+        a1 = first_sums[1] + gather([v * f * f] for v, f in pieces(w, sb))[0]
         top = jnp.sum(a0, keepdims=True)
         bottom = jnp.sum(a1, keepdims=True)
         tau = jnp.where(bottom > 0.0, top / jnp.where(bottom > 0.0, bottom, 1.0), 0.0)
-        r = [b[k] - tau * ab[k] for k in range(LEVELS)]
-        rr = [rb[k] - tau * rab[k] for k in range(LEVELS)]
-        sr_field = sb - tau * sab
-        blocks = [
-            a0,
-            a1,
-            inner(r, r),
-            inner(r, ab),
-            inner(ab, ab),
-            curvature(rr, rr, sr_field, sr_field),
-            curvature(rr, rab, sr_field, sab),
-            curvature(rab, rab, sab, sab),
-            curvature(rr, rb, sr_field, sb),
-            curvature(rab, rb, sab, sb),
-        ]
+
+        def residual_terms(x, ax, y, ay):
+            r, rr = x - tau * ax, y - tau * ay
+            return [r * r, r * ax, ax * ax, rr * rr, rr * ay, ay * ay, rr * y, ay * y]
+
+        def field_terms(v, f, af):
+            r = f - tau * af
+            vr, va = v * r, v * af
+            return [vr * r, vr * af, va * af, vr * f, va * f]
+
+        later_sums = add_levels(
+            [gather(residual_terms(*p) for p in pieces(b[k], ab[k], rb[k], rab[k])) for k in range(LEVELS)], 3
+        )
+        fields = gather(field_terms(*p) for p in pieces(w, sb, sab))
+        blocks = [a0, a1, *later_sums[:3], *(x + y for x, y in zip(later_sums[3:], fields))]
         lines = [jnp.sum(block, axis=0, keepdims=True) for block in blocks]
         lane = lax.broadcasted_iota(jnp.int32, (1, LANES), 1)
         lines.append(jnp.where(lane == 0, tau, 0.0))

time: 41.3 us -> 40.5 us (0.981)
  waiting for transfers between devices: 8.17 us -> 7.65 us
    ppermute x4, waiting for transfers between devices: 4.19 us -> 3.66 us  [flip(): return lax.ppermute(x, axis, [(i, i ^ k) for i in range(total)])]
where the time goes in v3:
time: 40.5 us; the launch traced here: 40.3 us
  blocking collectives  13 us (32%)
  starting transfers between devices  8.98 us (22%)
  waiting for transfers between devices  7.65 us (19%)
  Pallas kernels  7.53 us (19%)
  local copies, waits for them, and re-layouts  2.44 us (6%)
  between operations  0.68 us (2%)
    all_to_all x1, blocking collectives, body(): lax.all_to_all(parts, ('lat', 'lon'), split_axis=0, concat_axis=0, tiled=...  13 us
    pallas_call x4, Pallas kernels, run(): pl.pallas_call(kernel, out_shape=[jax.ShapeDtypeStruct(shape, jnp.float32...  7.02 us
    ppermute x3, starting transfers between devices, turn(): return lax.ppermute(x, axis, [(i, (i + k) % total) for i in range(total)])  4.76 us
    ppermute x3, waiting for transfers between devices, turn(): return lax.ppermute(x, axis, [(i, (i + k) % total) for i in range(total)])  3.99 us
    ppermute x4, waiting for transfers between devices, flip(): return lax.ppermute(x, axis, [(i, i ^ k) for i in range(total)])  3.66 us
    ppermute x4, starting transfers between devices, flip(): return lax.ppermute(x, axis, [(i, i ^ k) for i in range(total)])  3.56 us
    unnamed x2, local copies, waits for them, and re-layouts  2.44 us
  transfers between devices with their start and end apart: 8, of which 2 were waited for; matrix products, arithmetic and copies ran while one was open for 0% of the time, Pallas kernels for 1%

profile of v3, /device:TPU:0, one launch (start us, length us, event | category | flops | bytes accessed | tf_op | source)
XLA Modules:
  0.0 40.3 jit_solution(17627177807932274966)
XLA Ops:
  0.6 1.1 %shard_map.74 = (f32[128,512]{1,0:T(8,128)S(1)}, f32[32,640]{1,0:T(8,128)S(1)}, f32[224,128]{1,0:T(8,128)S(1)}, f32[32,640]{1,0:T(8,128)S(1)}, f32[224,128]{1,0:T(8,128)S(1)}) custom-call(f32[32,2048]{1,0:T(8,128)} %obs_hbm.1, s32[128,512]{1,0:T(8,128)} %gauge_hbm.1), custom_call_target="tpu_custom_call" | custom-call | tf_op jit(solution)/shard_map/pallas_call | solution.py:167
  1.8 0.5 %collective-permute-start = (f32[224,128]{1,0:T(8,128)S(1)}, f32[224,128]{1,0:T(8,128)S(1)}, u32[]{:S(2)}, u32[]{:S(2)}) collective-permute-start(f32[224,128]{1,0:T(8,128)S(1)} %get-tuple-element.28), channel_id=1, source_target_pairs={{0,1},{1,2},{2,3},{3,0},{4,5},{5,6},{6,7},{7,4},{8,9},{9,10},{10,1... | collective-permute-start | bytes 344072 | tf_op jit(solution)/shard_map/ppermute | solution.py:529
  2.3 2.0 %collective-permute-start.1 = (f32[224,128]{1,0:T(8,128)S(1)}, f32[224,128]{1,0:T(8,128)S(1)}, u32[]{:S(2)}, u32[]{:S(2)}) collective-permute-start(f32[224,128]{1,0:T(8,128)S(1)} %get-tuple-element.29), channel_id=1, source_target_pairs={{0,3},{1,0},{2,1},{3,2},{4,7},{5,4},{6,5},{7,6},{8,11},{9,8},{10,9... | collective-permute-start | bytes 344072 | tf_op jit(solution)/shard_map/ppermute | solution.py:529
  4.3 2.2 %collective-permute-start.2 = (f32[32,640]{1,0:T(8,128)S(1)}, f32[32,640]{1,0:T(8,128)S(1)}, u32[]{:S(2)}, u32[]{:S(2)}) collective-permute-start(f32[32,640]{1,0:T(8,128)S(1)} %get-tuple-element.31), channel_id=1, source_target_pairs={{0,2},{1,3},{2,0},{3,1},{4,6},{5,7},{6,4},{7,5},{8,10},{9,11},{10,... | collective-permute-start | bytes 245768 | tf_op jit(solution)/shard_map/ppermute | solution.py:529
  6.5 4.0 %collective-permute-done.2.rest_0_ = f32[32,640]{1,0:T(8,128)S(1)} collective-permute-done((f32[32,640]{1,0:T(8,128)S(1)}, f32[32,640]{1,0:T(8,128)S(1)}, u32[]{:S(2)}, u32[]{:S(2)}) %collective-permute-start.2) | collective-permute-done | bytes 81952 | tf_op jit(solution)/shard_map/ppermute | solution.py:529
  10.5 0.0 collective-permute-done.right_ref
  10.5 0.0 collective-permute-done.1.left_ref
  10.5 0.3 shard_map.75
  10.8 1.5 %collective-permute-start.3 = (f32[376,128]{1,0:T(8,128)S(1)}, f32[376,128]{1,0:T(8,128)S(1)}, u32[]{:S(2)}, u32[]{:S(2)}) collective-permute-start(f32[376,128]{1,0:T(8,128)S(1)} %get-tuple-element.34), channel_id=1, source_target_pairs={{0,4},{4,0},{8,12},{12,8},{16,20},{20,16},{24,28},{28,24},{1,5},{5... | collective-permute-start | bytes 577544 | tf_op jit(solution)/shard_map/ppermute | solution.py:533
  12.3 0.7 %collective-permute-start.4 = (f32[376,128]{1,0:T(8,128)S(1)}, f32[376,128]{1,0:T(8,128)S(1)}, u32[]{:S(2)}, u32[]{:S(2)}) collective-permute-start(f32[376,128]{1,0:T(8,128)S(1)} %get-tuple-element.35), channel_id=1, source_target_pairs={{4,8},{12,16},{20,24},{8,4},{16,12},{24,20},{5,9},{13,17},{21,25},... | collective-permute-start | bytes 577544 | tf_op jit(solution)/shard_map/ppermute | solution.py:538
  13.0 0.0 copy-start
  13.0 2.4 %copy-done = bf16[2,768,1664]{2,1,0:T(8,128)(2,1)S(1)} copy-done((bf16[2,768,1664]{2,1,0:T(8,128)(2,1)S(1)}, bf16[2,768,1664]{2,1,0:T(8,128)(2,1)}, u32[]{:S(2)}) %copy-start) | copy-done | bytes 5111832
  15.5 0.5 %shard_map.76.table_ref = bf16[2,768,1664]{2,1,0:T(8,128)(2,1)S(1)} custom-call(bf16[2,768,1664]{2,1,0:T(8,128)(2,1)S(1)} %copy-done, f32[128,128]{1,0:T(8,128)S(1)} %get-tuple-element.33.after_ref.side_ref), custom_call_target="tpu_custom_call" | custom-call | bytes 10223616 | tf_op jit(solution)/shard_map/pallas_call | solution.py:315
  16.0 3.7 %collective-permute-done.3.near_ref = f32[376,128]{1,0:T(8,128)S(1)} collective-permute-done((f32[376,128]{1,0:T(8,128)S(1)}, f32[376,128]{1,0:T(8,128)S(1)}, u32[]{:S(2)}, u32[]{:S(2)}) %collective-permute-start.3) | collective-permute-done | bytes 192544 | tf_op jit(solution)/shard_map/ppermute | solution.py:533
  19.6 0.0 collective-permute-done.4.next_ref
  19.6 4.6 %shard_map.77 = (f32[16,64]{1,0:T(8,128)S(1)}, f32[32,128]{1,0:T(8,128)S(1)}, f32[64,256]{1,0:T(8,128)S(1)}, f32[128,512]{1,0:T(8,128)S(1)}, f32[16,64]{1,0:T(8,...) custom-call(f32[128,640]{1,0:T(8,128)S(1)} %get-tuple-element.32.mis, ...), custom_call_target="tpu_custom_call" | custom-call | tf_op jit(solution)/shard_map/pallas_call | solution.py:167
  24.2 0.0 collective-permute-start.5
  24.2 2.0 %collective-permute-start.6 = (f32[64,512]{1,0:T(8,128)S(1)}, f32[64,512]{1,0:T(8,128)S(1)}, u32[]{:S(2)}, u32[]{:S(2)}) collective-permute-start(f32[64,512]{1,0:T(8,128)S(1)} %get-tuple-element.47), channel_id=1, source_target_pairs={{0,2},{1,3},{2,0},{3,1},{4,6},{5,7},{6,4},{7,5},{8,10},{9,11},{10,... | collective-permute-start | bytes 393224 | tf_op jit(solution)/shard_map/ppermute | solution.py:533
  26.2 0.1 collective-permute-start.7
  26.3 13.0 %all_to_all.11 = f32[32,1,128]{2,1,0:T(1,128)S(1)} all-to-all(f32[32,1,128]{2,1,0:T(1,128)S(1)} %bitcast.5), channel_id=1, replica_groups=mesh['lat'=8,'lon'=4] {'lat','lon'}, dimensions={0} | all-to-all | bytes 32768 | tf_op jit(solution)/shard_map/all_to_all | solution.py:552
  39.3 0.0 collective-permute-done.5.rest_9_
  39.3 0.0 collective-permute-done.6.rest_10_
  39.3 0.0 collective-permute-done.7.rest_11_
  39.3 1.0 %shard_map.78 = (f32[16,64]{1,0:T(8,128)}, f32[32,128]{1,0:T(8,128)}, f32[64,256]{1,0:T(8,128)}, f32[128,512]{1,0:T(8,128)}, f32[32,2048]{1,0:T(8,128)}) custom-call(f32[32,128]{1,0:T(8,128)S(1)} %bitcast.4, f32[16,64]{1,0:T(8,128)S(1)} %get-tuple-element.37.rest_0_, f32[32,128]{1,0:T(8,128)S(1)} %get-tuple-element.38.rest_1_, ...), custom_call_target="tpu_custom_call" | custom-call | tf_op jit(solution)/shard_map/pallas_call | solution.py:167
Async XLA Ops:
  1.8 8.7 %collective-permute-start = (f32[224,128]{1,0:T(8,128)S(1)}, f32[224,128]{1,0:T(8,128)S(1)}, u32[]{:S(2)}, u32[]{:S(2)}) collective-permute-start(f32[224,128]{1,0:T(8,128)S(1)} %get-tuple-element.28), channel_id=1, source_target_pairs={{0,1},{1,2},{2,3},{3,0},{4,5},{5,6},{6,7},{7,4},{8,9},{9,10},{10,1... | collective-permute-start | bytes 344072 | tf_op jit(solution)/shard_map/ppermute | solution.py:529
  2.3 8.2 %collective-permute-start.1 = (f32[224,128]{1,0:T(8,128)S(1)}, f32[224,128]{1,0:T(8,128)S(1)}, u32[]{:S(2)}, u32[]{:S(2)}) collective-permute-start(f32[224,128]{1,0:T(8,128)S(1)} %get-tuple-element.29), channel_id=1, source_target_pairs={{0,3},{1,0},{2,1},{3,2},{4,7},{5,4},{6,5},{7,6},{8,11},{9,8},{10,9... | collective-permute-start | bytes 344072 | tf_op jit(solution)/shard_map/ppermute | solution.py:529
  4.3 6.2 %collective-permute-start.2 = (f32[32,640]{1,0:T(8,128)S(1)}, f32[32,640]{1,0:T(8,128)S(1)}, u32[]{:S(2)}, u32[]{:S(2)}) collective-permute-start(f32[32,640]{1,0:T(8,128)S(1)} %get-tuple-element.31), channel_id=1, source_target_pairs={{0,2},{1,3},{2,0},{3,1},{4,6},{5,7},{6,4},{7,5},{8,10},{9,11},{10,... | collective-permute-start | bytes 245768 | tf_op jit(solution)/shard_map/ppermute | solution.py:529
  10.8 8.8 %collective-permute-start.3 = (f32[376,128]{1,0:T(8,128)S(1)}, f32[376,128]{1,0:T(8,128)S(1)}, u32[]{:S(2)}, u32[]{:S(2)}) collective-permute-start(f32[376,128]{1,0:T(8,128)S(1)} %get-tuple-element.34), channel_id=1, source_target_pairs={{0,4},{4,0},{8,12},{12,8},{16,20},{20,16},{24,28},{28,24},{1,5},{5... | collective-permute-start | bytes 577544 | tf_op jit(solution)/shard_map/ppermute | solution.py:533
  12.3 7.3 %collective-permute-start.4 = (f32[376,128]{1,0:T(8,128)S(1)}, f32[376,128]{1,0:T(8,128)S(1)}, u32[]{:S(2)}, u32[]{:S(2)}) collective-permute-start(f32[376,128]{1,0:T(8,128)S(1)} %get-tuple-element.35), channel_id=1, source_target_pairs={{4,8},{12,16},{20,24},{8,4},{16,12},{24,20},{5,9},{13,17},{21,25},... | collective-permute-start | bytes 577544 | tf_op jit(solution)/shard_map/ppermute | solution.py:538
  13.0 2.5 %copy-start = (bf16[2,768,1664]{2,1,0:T(8,128)(2,1)S(1)}, bf16[2,768,1664]{2,1,0:T(8,128)(2,1)}, u32[]{:S(2)}) copy-start(bf16[2,768,1664]{2,1,0:T(8,128)(2,1)} %constant.2.clone.table_ref) | copy-start | bytes 15335428
  24.2 15.1 %collective-permute-start.5 = (f32[64,512]{1,0:T(8,128)S(1)}, f32[64,512]{1,0:T(8,128)S(1)}, u32[]{:S(2)}, u32[]{:S(2)}) collective-permute-start(f32[64,512]{1,0:T(8,128)S(1)} %get-tuple-element.46), channel_id=1, source_target_pairs={{0,1},{1,0},{2,3},{3,2},{4,5},{5,4},{6,7},{7,6},{8,9},{9,8},{10,11... | collective-permute-start | bytes 393224 | tf_op jit(solution)/shard_map/ppermute | solution.py:533
  24.2 15.1 %collective-permute-start.6 = (f32[64,512]{1,0:T(8,128)S(1)}, f32[64,512]{1,0:T(8,128)S(1)}, u32[]{:S(2)}, u32[]{:S(2)}) collective-permute-start(f32[64,512]{1,0:T(8,128)S(1)} %get-tuple-element.47), channel_id=1, source_target_pairs={{0,2},{1,3},{2,0},{3,1},{4,6},{5,7},{6,4},{7,5},{8,10},{9,11},{10,... | collective-permute-start | bytes 393224 | tf_op jit(solution)/shard_map/ppermute | solution.py:533
  26.2 13.1 %collective-permute-start.7 = (f32[64,512]{1,0:T(8,128)S(1)}, f32[64,512]{1,0:T(8,128)S(1)}, u32[]{:S(2)}, u32[]{:S(2)}) collective-permute-start(f32[64,512]{1,0:T(8,128)S(1)} %get-tuple-element.48), channel_id=1, source_target_pairs={{0,3},{1,2},{2,1},{3,0},{4,7},{5,6},{6,5},{7,4},{8,11},{9,10},{10,... | collective-permute-start | bytes 393224 | tf_op jit(solution)/shard_map/ppermute | solution.py:533

commit v4 on v3

--- a/solution.py
+++ b/solution.py
@@ -15,6 +15,7 @@
 INNER = 32
 RAW = 40
 PART_ROWS = 8
+EDGE = 32
 NEAR = 8
 LANES = 128
 
@@ -104,7 +105,8 @@
         self.inner_rows = self.rows + 2 * INNER
         wide = [-(-(self.rows // s + 2 * (INNER // s + 2)) // 16) * 16 for s in SPACINGS[:COARSE]]
         self.node_rows = wide + [self.outer_rows]
-        self.near_rows = [min(w, self.rows // s + 2 * NEAR) for w, s in zip(wide, SPACINGS)] + [self.inner_rows]
+        self.near_rows = [min(w, self.rows // s + 2 * NEAR) for w, s in zip(wide, SPACINGS)]
+        self.near_rows.append(self.rows + 2 * NEAR)
         self.near_starts = np.cumsum([0] + self.near_rows[:COARSE]).tolist()
         self.node_cols = [-(-self.col_frame // (s * LANES)) * LANES for s in SPACINGS]
         self.row_starts = np.cumsum([0] + self.node_rows[:COARSE]).tolist()
@@ -136,23 +138,60 @@
         outer_all = np.concatenate([np.concatenate(outer_rows, axis=1), joins], axis=0)
         inner_all = np.concatenate(inner_rows, axis=1)
         wide_all = np.concatenate(wide_rows, axis=1)
-        row_tables = [outer_all.T, inner_all.T, wide_all, inner_all[: self.rows]]
-        self.row_places, at = [], 0
+        self.edge_nodes, sel = [], []
+        for k in range(COARSE):
+            first, total = self.rows // SPACINGS[k] - NEAR, self.node_rows[k]
+            self.edge_nodes.append(total - first + NEAR)
+            sel += [self.row_starts[k] + at for at in (*range(first, total), *range(NEAR))]
+        self.edge_starts = np.cumsum([0] + self.edge_nodes).tolist()
+        edge_rows = [*range(self.rows - EDGE, self.inner_rows), *range(EDGE)]
+        row_tables = [
+            outer_all[: self.rows].T,
+            outer_all[self.rows :].T[sel],
+            inner_all.T,
+            wide_all,
+            wide_all[edge_rows][:, sel],
+            inner_all[: self.rows],
+        ]
+        lanes = -(-max(t.shape[1] for t in row_tables) // LANES) * LANES
+        self.row_places, ends = [], [0, 0]
         for table in row_tables:
-            self.row_places.append((at, table.shape[0], table.shape[1]))
-            at += table.shape[0]
-        lanes = -(-max(t.shape[1] for t in row_tables) // LANES) * LANES
+            side = int(ends[1] < ends[0])
+            self.row_places.append((ends[side], table.shape[0], self.col_starts[-1] + side * lanes, table.shape[1]))
+            ends[side] += table.shape[0]
+        at = max(ends)
         col_all = np.concatenate(col_tables, axis=1)
-        self.turned_start = self.col_starts[-1] + lanes
+        self.turned_start = self.col_starts[-1] + 2 * lanes
         whole = np.zeros((max(at, *col_all.shape), self.turned_start + self.col_frame), np.float32)
         whole[: self.col_frame, : self.col_starts[-1]] = col_all
         whole[: self.col_starts[-1], self.turned_start :] = col_all.T
-        for (start, height, width), table in zip(self.row_places, row_tables):
-            whole[start : start + height, self.col_starts[-1] : self.col_starts[-1] + width] = table
+        for (start, height, lane, width), table in zip(self.row_places, row_tables):
+            whole[start : start + height, lane : lane + width] = table
         self.tables = halves(whole)
         tiles = self.col_frame // LANES
         self.sums = len(self.part_nodes)
         self.letter_rows = -(-(self.letter()[-1] + tiles * self.sums) // 8) * 8
+
+    def pick(self, table_ref):
+        col_tables, turned_tables, row_tables = [], [], []
+        for k in range(COARSE):
+            places = slice(self.col_starts[k], self.col_starts[k + 1])
+            turned_tables.append(tuple(table_ref[half, places, self.turned_start :] for half in (0, 1)))
+            col_tables.append(tuple(table_ref[half, 0 : self.col_frame, places] for half in (0, 1)))
+        for start, height, lane, width in self.row_places:
+            rows, lanes = slice(start, start + height), slice(lane, lane + width)
+            row_tables.append(tuple(table_ref[half, rows, lanes] for half in (0, 1)))
+        return col_tables, turned_tables, row_tables
+
+    def masks(self, heights):
+        lat, lon = lax.axis_index("lat"), lax.axis_index("lon")
+        out = []
+        for k, s in enumerate(SPACINGS):
+            tile = self.rows // s
+            rows = side_mask(heights[k], tile, (heights[k] - tile) // 2, lat, self.lat_total - 1, 0)
+            cols = side_mask(self.node_cols[k], self.cols // s, HALO // s, lon, self.lon_total - 1, 1)
+            out.append(rows * cols)
+        return out
 
     def letter(self):
         tiles = self.col_frame // LANES
@@ -229,11 +268,11 @@
     return call(kernel, outs, 53.25, scratch, [pltpu.HBM] * 2)(observed, gauged)
 
 
-def misfit(plan, own, right, left, far, weight):
+def misfit(plan, own, right, left, far, weight, tables):
     sr, cols, rows, n = plan.swath_rows, plan.cols, plan.rows, plan.lon_total
     tiles = plan.col_frame // LANES
 
-    def kernel(own_ref, right_ref, left_ref, wt_ref, *rest):
+    def kernel(own_ref, right_ref, left_ref, wt_ref, table_ref, *rest):
         far_refs, (mis_ref, side_ref, near_ref, next_ref) = rest[: n - 3], rest[n - 3 :]
         at = lax.axis_index("lon")
         lane = lax.broadcasted_iota(jnp.int32, (rows, LANES), 1)
@@ -286,7 +325,7 @@
             ref[parts + tiles * plan.sums :, :] = jnp.zeros((plan.letter_rows - parts - tiles * plan.sums, LANES), jnp.float32)
 
     outs = [(rows, plan.col_frame), (rows, LANES)] + [(plan.letter_rows, LANES)] * 2
-    return call(kernel, outs, 4)(own, right, left, weight, *far)
+    return call(kernel, outs, 4)(own, right, left, weight, tables, *far)
 
 
 def open_letter(plan, letter):
@@ -323,77 +362,102 @@
     )(table, after)
 
 
-def operate(plan, mis, wt, side, near, following, tables):
+def inside(plan, mis, tables):
+    rows, inner_rows = plan.rows, plan.inner_rows
+    shapes = [(plan.node_rows[k], plan.node_cols[k]) for k in range(COARSE)] + [(rows + 2 * NEAR, plan.col_frame)]
+
+    def kernel(mis_ref, table_ref, *out_refs):
+        base_refs, surface_ref = out_refs[:LEVELS], out_refs[LEVELS]
+        col_tables, turned_tables, (own_t, _, _, wide_s, _, _) = plan.pick(table_ref)
+        masks = plan.masks([height for height, _ in shapes])
+        mis = mis_ref[...]
+        gathered = dot3(own_t, split(mis))
+        starts = plan.row_starts
+        base = [dot3(split(gathered[starts[k] : starts[k + 1]]), col_tables[k]) * masks[k] for k in range(COARSE)]
+        blank = jnp.zeros((2 * NEAR, plan.col_frame), jnp.float32)
+        base.append(smooth(jnp.concatenate([mis, blank], axis=0)) * masks[COARSE])
+        for k in range(LEVELS):
+            base_refs[k][...] = base[k]
+        fine = smooth(base[COARSE])
+        blank = jnp.zeros((inner_rows - rows - 2 * NEAR, plan.col_frame), jnp.float32)
+        fine = jnp.concatenate([fine[0 : rows + NEAR], blank, fine[rows + NEAR :]], axis=0)
+        spread = jnp.concatenate([dot3(split(base[k]), turned_tables[k]) for k in range(COARSE)], axis=0)
+        surface_ref[...] = fine + dot3(wide_s, split(spread))
+
+    *base, surface = call(kernel, shapes + [(inner_rows, plan.col_frame)], 24)(mis, tables)
+    return base, surface
+
+
+def operate(plan, mid, mid_surface, wt, side, near, following, tables):
     rows, cols, sr, lon_total = plan.rows, plan.cols, plan.swath_rows, plan.lon_total
     n_dev = plan.lat_total * lon_total
 
-    def kernel(mis_ref, wt_ref, side_ref, near_ref, next_ref, table_ref, *out_refs):
+    def kernel(mid_surface_ref, wt_ref, side_ref, near_ref, next_ref, table_ref, *out_refs):
+        mid_refs, out_refs = out_refs[:LEVELS], out_refs[LEVELS:]
         base_refs, image_refs = out_refs[:LEVELS], out_refs[LEVELS : 2 * LEVELS]
         surface_refs, part_ref = out_refs[2 * LEVELS : -1], out_refs[-1]
         lat = lax.axis_index("lat")
         lon = lax.axis_index("lon")
         even = lat % 2 == 0
-        col_tables, turned_tables, row_tables = [], [], []
-        for k in range(COARSE):
-            places = slice(plan.col_starts[k], plan.col_starts[k + 1])
-            turned_tables.append(tuple(table_ref[half, places, plan.turned_start :] for half in (0, 1)))
-            lanes = slice(plan.col_starts[k], plan.col_starts[k + 1])
-            col_tables.append(tuple(table_ref[half, 0 : plan.col_frame, lanes] for half in (0, 1)))
-        for start, height, width in plan.row_places:
-            lanes = slice(plan.col_starts[-1], plan.col_starts[-1] + width)
-            row_tables.append(tuple(table_ref[half, start : start + height, lanes] for half in (0, 1)))
-        outer_t, inner_t, wide_s, tile_s = row_tables
-
+        col_tables, turned_tables, row_tables = plan.pick(table_ref)
+        _, edge_t, inner_t, _, edge_s, tile_s = row_tables
         near_all, next_all = near_ref[...], next_ref[...]
         below = jnp.where(even, near_all, next_all)
         above = jnp.where(even, next_all, near_all)
         below, below_sums, below_wt = open_letter(plan, below)
         above, above_sums, above_wt = open_letter(plan, above)
-        cells = jnp.concatenate([mis_ref[...], below, above], axis=0)
-        outer = jnp.concatenate([cells, below_sums, above_sums], axis=0)
         own_weight = jnp.concatenate([wt_ref[...], side_ref[...]], axis=1)
         weight = jnp.concatenate([own_weight, below_wt, above_wt], axis=0)
 
-        masks = []
-        for k in range(LEVELS):
-            s = SPACINGS[k]
-            masks.append(
-                side_mask(plan.node_rows[k], rows // s, (plan.node_rows[k] - rows // s) // 2, lat, plan.lat_total - 1, 0)
-                * side_mask(plan.node_cols[k], cols // s, HALO // s, lon, lon_total - 1, 1)
-            )
-        def collect(values, row_table, starts):
-            gathered = dot3(row_table, split(values))
-            return [
-                dot3(split(gathered[starts[k] : starts[k + 1]]), col_tables[k]) for k in range(COARSE)
-            ]
+        masks = plan.masks(plan.node_rows)
+
+        def collect(gathered, starts):
+            return [dot3(split(gathered[starts[k] : starts[k + 1]]), col_tables[k]) for k in range(COARSE)]
 
         def spread(coeffs, width):
             turned = [tuple(part[:, 0:width] for part in table) for table in turned_tables]
             return split(jnp.concatenate([dot3(split(coeffs[k]), turned[k]) for k in range(COARSE)], axis=0))
 
-        def cut(x, k):
-            total = plan.near_rows[k]
+        def cut(x, k, total):
             if x.shape[0] == total:
                 return x
             side = (total - rows // SPACINGS[k]) // 2
             return jnp.concatenate([x[0 : total - side], x[x.shape[0] - side :]], axis=0)
 
-        base = collect(outer, outer_t, plan.row_starts)
-        base = [base[k] * masks[k] for k in range(COARSE)]
-        finest = smooth(cells) * masks[COARSE]
-        surface = dot3(wide_s, spread(base, plan.col_frame)) + cut(smooth(finest), COARSE)
-        base = [cut(x, k) for k, x in enumerate(base + [finest])]
-        masks = []
-        for k in range(LEVELS):
+        def blank(height, like):
+            return jnp.zeros((height, like.shape[1]), jnp.float32)
+
+        around = jnp.concatenate([below, above, below_sums, above_sums], axis=0)
+        edge = collect(dot3(edge_t, split(around)), plan.edge_starts)
+        base = []
+        for k in range(COARSE):
+            first = plan.edge_nodes[k] - NEAR
             tile = rows // SPACINGS[k]
-            side = (plan.near_rows[k] - tile) // 2
-            masks.append(
-                side_mask(plan.near_rows[k], tile, side, lat, plan.lat_total - 1, 0)
-                * side_mask(plan.node_cols[k], cols // SPACINGS[k], HALO // SPACINGS[k], lon, lon_total - 1, 1)
-            )
-
-        image = collect(weight * surface, inner_t, plan.near_starts)
-        image.append(smooth(weight * surface))
+            mask = jnp.concatenate([masks[k][tile - NEAR :], masks[k][0:NEAR]], axis=0)
+            edge[k] = edge[k] * mask
+            added = [edge[k][first:], edge[k][0:first]]
+            if tile > 2 * NEAR:
+                added.insert(1, blank(tile - 2 * NEAR, edge[k]))
+            base.append(cut(mid_refs[k][...] + jnp.concatenate(added, axis=0), k, plan.near_rows[k]))
+        strip = jnp.concatenate([blank(NEAR, below), below, above, blank(NEAR, above)], axis=0)
+        fine_mask = masks[COARSE]
+        strip_mask = jnp.concatenate([fine_mask[rows - NEAR :], fine_mask[0:NEAR]], axis=0)
+        strip = smooth(strip) * strip_mask
+        last = strip.shape[0] - NEAR
+        added = [strip[last:], blank(rows - 2 * NEAR, strip), strip[0 : 2 * NEAR], strip[last - NEAR : last]]
+        base.append(mid_refs[COARSE][...] + jnp.concatenate(added, axis=0))
+        fine = smooth(strip)
+        added = [fine[last:], blank(rows - 2 * NEAR, fine), fine[0 : NEAR + INNER], fine[last - INNER : last]]
+        surface = mid_surface_ref[...] + jnp.concatenate(added, axis=0)
+        coarse = dot3(edge_s, spread(edge, plan.col_frame))
+        body_rows = coarse.shape[0] - EDGE
+        added = [coarse[body_rows:], blank(rows - 2 * EDGE, coarse), coarse[0:body_rows]]
+        surface = surface + jnp.concatenate(added, axis=0)
+        masks = plan.masks(plan.near_rows)
+
+        misfit_again = weight * surface
+        image = collect(dot3(inner_t, split(misfit_again)), plan.near_starts)
+        image.append(smooth(cut(misfit_again, COARSE, plan.near_rows[COARSE])))
         rough_base, rough_image = [], []
         for k in range(LEVELS):
             once = autoreg(base[k]) * masks[k]
@@ -478,7 +542,7 @@
 
     level_shapes = [(rows // s, cols // s) for s in SPACINGS]
     outs = level_shapes * 2 + [(2 * rows, cols)] + [(2 * sr, cols)] * (lon_total - 1) + [(n_dev, LANES)]
-    results = call(kernel, outs, 24)(mis, wt, side, near, following, tables)
+    results = call(kernel, outs, 24)(mid_surface, wt, side, near, following, tables, *mid)
     return results[:LEVELS], results[LEVELS : 2 * LEVELS], results[2 * LEVELS : -1], results[-1]
 
 
@@ -542,12 +606,13 @@
     lat_total, lon_total = lax.axis_size("lat"), lax.axis_size("lon")
     plan = Plan(observed.shape, gauged.shape, lat_total, lon_total)
     weight, own, *windows = pack(plan, observed, gauged)
+    tables = fetch(plan, own)
     right, *far, left = [turn(x, "lon", lon_total, k) for k, x in enumerate(windows, 1)]
-    mis, side, near, following = misfit(plan, own, right, left, far, weight)
-    tables = fetch(plan, side)
+    mis, side, near, following = misfit(plan, own, right, left, far, weight, tables)
+    mid, mid_surface = inside(plan, mis, tables)
     near = flip(near, "lat", lat_total, 1)
     following = odd_swap(following, "lat", lat_total)
-    base, image, surfaces, parts = operate(plan, mis, weight, side, near, following, tables)
+    base, image, surfaces, parts = operate(plan, mid, mid_surface, weight, side, near, following, tables)
     far_surfaces = [flip(x, "lon", lon_total, k) for k, x in enumerate(surfaces[1:], 1)]
     parts = lax.all_to_all(parts, ("lat", "lon"), split_axis=0, concat_axis=0, tiled=True)
     return tuple(finish(plan, parts, base, image, surfaces[0], far_surfaces))

time: 40.5 us -> 40.2 us (level)
  waiting for transfers between devices: 7.65 us -> 5.24 us
  Pallas kernels: 7.53 us -> 9.36 us
    ppermute x3, waiting for transfers between devices: 3.99 us -> 0.74 us  [turn(): return lax.ppermute(x, axis, [(i, (i + k) % total) for i in range(total)])]
    pallas_call x4 -> x5, Pallas kernels: 7.02 us -> 8.8 us  [run(): pl.pallas_call(kernel, out_shape=[jax.ShapeDtypeStruct(shape, jnp.float32...]
    ppermute x4, waiting for transfers between devices: 3.66 us -> 4.5 us  [flip(): return lax.ppermute(x, axis, [(i, i ^ k) for i in range(total)])]
  transfers between devices with their start and end apart: 8 -> 8, of which waited for: 2 -> 2; matrix products, arithmetic and copies ran while one was open for 0% -> 0% of each run, Pallas kernels for 1% -> 7%
where the time goes in v4:
time: 40.2 us; the launch traced here: 40 us
  blocking collectives  13 us (32%)
  Pallas kernels  9.36 us (23%)
  starting transfers between devices  8.99 us (22%)
  waiting for transfers between devices  5.24 us (13%)
  local copies, waits for them, and re-layouts  2.67 us (7%)
  between operations  0.68 us (2%)
    all_to_all x1, blocking collectives, body(): lax.all_to_all(parts, ('lat', 'lon'), split_axis=0, concat_axis=0, tiled=...  13 us
    pallas_call x5, Pallas kernels, run(): pl.pallas_call(kernel, out_shape=[jax.ShapeDtypeStruct(shape, jnp.float32...  8.8 us
    ppermute x3, starting transfers between devices, turn(): return lax.ppermute(x, axis, [(i, (i + k) % total) for i in range(total)])  4.76 us
    ppermute x4, waiting for transfers between devices, flip(): return lax.ppermute(x, axis, [(i, i ^ k) for i in range(total)])  4.5 us
    ppermute x4, starting transfers between devices, flip(): return lax.ppermute(x, axis, [(i, i ^ k) for i in range(total)])  3.57 us
    unnamed x2, local copies, waits for them, and re-layouts  2.67 us
  transfers between devices with their start and end apart: 8, of which 2 were waited for; matrix products, arithmetic and copies ran while one was open for 0% of the time, Pallas kernels for 7%

profile of v4, /device:TPU:0, one launch (start us, length us, event | category | flops | bytes accessed | tf_op | source)
XLA Modules:
  0.0 40.0 jit_solution(7180790834263413263)
XLA Ops:
  0.6 1.1 %shard_map.74 = (f32[128,512]{1,0:T(8,128)S(1)}, f32[32,640]{1,0:T(8,128)S(1)}, f32[224,128]{1,0:T(8,128)S(1)}, f32[32,640]{1,0:T(8,128)S(1)}, f32[224,128]{1,0:T(8,128)S(1)}) custom-call(f32[32,2048]{1,0:T(8,128)} %obs_hbm.1, s32[128,512]{1,0:T(8,128)} %gauge_hbm.1), custom_call_target="tpu_custom_call" | custom-call | tf_op jit(solution)/shard_map/pallas_call | solution.py:206
  1.8 0.5 %collective-permute-start = (f32[224,128]{1,0:T(8,128)S(1)}, f32[224,128]{1,0:T(8,128)S(1)}, u32[]{:S(2)}, u32[]{:S(2)}) collective-permute-start(f32[224,128]{1,0:T(8,128)S(1)} %get-tuple-element.33), channel_id=1, source_target_pairs={{0,1},{1,2},{2,3},{3,0},{4,5},{5,6},{6,7},{7,4},{8,9},{9,10},{10,1... | collective-permute-start | bytes 344072 | tf_op jit(solution)/shard_map/ppermute | solution.py:593
  2.3 2.0 %collective-permute-start.1 = (f32[224,128]{1,0:T(8,128)S(1)}, f32[224,128]{1,0:T(8,128)S(1)}, u32[]{:S(2)}, u32[]{:S(2)}) collective-permute-start(f32[224,128]{1,0:T(8,128)S(1)} %get-tuple-element.34), channel_id=1, source_target_pairs={{0,3},{1,0},{2,1},{3,2},{4,7},{5,4},{6,5},{7,6},{8,11},{9,8},{10,9... | collective-permute-start | bytes 344072 | tf_op jit(solution)/shard_map/ppermute | solution.py:593
  4.3 2.2 %collective-permute-start.2 = (f32[32,640]{1,0:T(8,128)S(1)}, f32[32,640]{1,0:T(8,128)S(1)}, u32[]{:S(2)}, u32[]{:S(2)}) collective-permute-start(f32[32,640]{1,0:T(8,128)S(1)} %get-tuple-element.36), channel_id=1, source_target_pairs={{0,2},{1,3},{2,0},{3,1},{4,6},{5,7},{6,4},{7,5},{8,10},{9,11},{10,... | collective-permute-start | bytes 245768 | tf_op jit(solution)/shard_map/ppermute | solution.py:593
  6.5 0.0 copy-start
  6.5 2.7 %copy-done = bf16[2,768,1920]{2,1,0:T(8,128)(2,1)S(1)} copy-done((bf16[2,768,1920]{2,1,0:T(8,128)(2,1)S(1)}, bf16[2,768,1920]{2,1,0:T(8,128)(2,1)}, u32[]{:S(2)}) %copy-start) | copy-done | bytes 5898264
  9.2 0.6 %shard_map.75.table_ref = bf16[2,768,1920]{2,1,0:T(8,128)(2,1)S(1)} custom-call(bf16[2,768,1920]{2,1,0:T(8,128)(2,1)S(1)} %copy-done, f32[32,640]{1,0:T(8,128)S(1)} %get-tuple-element.32.after_ref.own_ref), custom_call_target="tpu_custom_call" | custom-call | bytes 11796480 | tf_op jit(solution)/shard_map/pallas_call | solution.py:354
  9.8 0.7 %collective-permute-done.2.rest_0_ = f32[32,640]{1,0:T(8,128)S(1)} collective-permute-done((f32[32,640]{1,0:T(8,128)S(1)}, f32[32,640]{1,0:T(8,128)S(1)}, u32[]{:S(2)}, u32[]{:S(2)}) %collective-permute-start.2) | collective-permute-done | bytes 81952 | tf_op jit(solution)/shard_map/ppermute | solution.py:593
  10.5 0.0 collective-permute-done.right_ref
  10.5 0.0 collective-permute-done.1.left_ref
  10.5 0.3 shard_map.76
  10.8 1.5 %collective-permute-start.3 = (f32[376,128]{1,0:T(8,128)S(1)}, f32[376,128]{1,0:T(8,128)S(1)}, u32[]{:S(2)}, u32[]{:S(2)}) collective-permute-start(f32[376,128]{1,0:T(8,128)S(1)} %get-tuple-element.40), channel_id=1, source_target_pairs={{0,4},{4,0},{8,12},{12,8},{16,20},{20,16},{24,28},{28,24},{1,5},{5... | collective-permute-start | bytes 577544 | tf_op jit(solution)/shard_map/ppermute | solution.py:597
  12.3 0.7 %collective-permute-start.4 = (f32[376,128]{1,0:T(8,128)S(1)}, f32[376,128]{1,0:T(8,128)S(1)}, u32[]{:S(2)}, u32[]{:S(2)}) collective-permute-start(f32[376,128]{1,0:T(8,128)S(1)} %get-tuple-element.41), channel_id=1, source_target_pairs={{4,8},{12,16},{20,24},{8,4},{16,12},{24,20},{5,9},{13,17},{21,25},... | collective-permute-start | bytes 577544 | tf_op jit(solution)/shard_map/ppermute | solution.py:602
  13.0 2.1 %shard_map.77 = (f32[32,128]{1,0:T(8,128)S(1)}, f32[64,256]{1,0:T(8,128)S(1)}, f32[112,384]{1,0:T(8,128)S(1)}, f32[144,640]{1,0:T(8,128)S(1)}, f32[192,640]{1,0:T(8,128)S(1)}) custom-call(f32[128,640]{1,0:T(8,128)S(1)} %get-tuple-element.37.mis_ref, bf16[2,768,1920]{2,1,0:T(8,128)(2,1)S(1)} %shard_map.75.table_ref), custom_call_target="tpu_custom_call" | custom-call | tf_op jit(solution)/shard_map/pallas_call | solution.py:206
  15.1 4.5 %collective-permute-done.3.near_ref = f32[376,128]{1,0:T(8,128)S(1)} collective-permute-done((f32[376,128]{1,0:T(8,128)S(1)}, f32[376,128]{1,0:T(8,128)S(1)}, u32[]{:S(2)}, u32[]{:S(2)}) %collective-permute-start.3) | collective-permute-done | bytes 192544 | tf_op jit(solution)/shard_map/ppermute | solution.py:597
  19.6 0.0 collective-permute-done.4.next_ref
  19.6 4.2 %shard_map.78 = (f32[16,64]{1,0:T(8,128)S(1)}, f32[32,128]{1,0:T(8,128)S(1)}, f32[64,256]{1,0:T(8,128)S(1)}, f32[128,512]{1,0:T(8,128)S(1)}, f32[16,64]{1,0:T(8,...) custom-call(f32[192,640]{1,0:T(8,128)S(1)} %get-tuple-element.38.mid, ...), custom_call_target="tpu_custom_call" | custom-call | tf_op jit(solution)/shard_map/pallas_call | solution.py:206
  23.8 0.0 collective-permute-start.5
  23.9 2.0 %collective-permute-start.6 = (f32[64,512]{1,0:T(8,128)S(1)}, f32[64,512]{1,0:T(8,128)S(1)}, u32[]{:S(2)}, u32[]{:S(2)}) collective-permute-start(f32[64,512]{1,0:T(8,128)S(1)} %get-tuple-element.57), channel_id=1, source_target_pairs={{0,2},{1,3},{2,0},{3,1},{4,6},{5,7},{6,4},{7,5},{8,10},{9,11},{10,... | collective-permute-start | bytes 393224 | tf_op jit(solution)/shard_map/ppermute | solution.py:597
  25.8 0.1 collective-permute-start.7
  25.9 13.0 %all_to_all.11 = f32[32,1,128]{2,1,0:T(1,128)S(1)} all-to-all(f32[32,1,128]{2,1,0:T(1,128)S(1)} %bitcast.5), channel_id=1, replica_groups=mesh['lat'=8,'lon'=4] {'lat','lon'}, dimensions={0} | all-to-all | bytes 32768 | tf_op jit(solution)/shard_map/all_to_all | solution.py:617
  38.9 0.0 collective-permute-done.5.rest_9_
  38.9 0.0 collective-permute-done.6.rest_10_
  38.9 0.0 collective-permute-done.7.rest_11_
  38.9 1.0 %shard_map.79 = (f32[16,64]{1,0:T(8,128)}, f32[32,128]{1,0:T(8,128)}, f32[64,256]{1,0:T(8,128)}, f32[128,512]{1,0:T(8,128)}, f32[32,2048]{1,0:T(8,128)}) custom-call(f32[32,128]{1,0:T(8,128)S(1)} %bitcast.4, f32[16,64]{1,0:T(8,128)S(1)} %get-tuple-element.47.rest_0_, f32[32,128]{1,0:T(8,128)S(1)} %get-tuple-element.48.rest_1_, ...), custom_call_target="tpu_custom_call" | custom-call | tf_op jit(solution)/shard_map/pallas_call | solution.py:206
Async XLA Ops:
  1.8 8.7 %collective-permute-start = (f32[224,128]{1,0:T(8,128)S(1)}, f32[224,128]{1,0:T(8,128)S(1)}, u32[]{:S(2)}, u32[]{:S(2)}) collective-permute-start(f32[224,128]{1,0:T(8,128)S(1)} %get-tuple-element.33), channel_id=1, source_target_pairs={{0,1},{1,2},{2,3},{3,0},{4,5},{5,6},{6,7},{7,4},{8,9},{9,10},{10,1... | collective-permute-start | bytes 344072 | tf_op jit(solution)/shard_map/ppermute | solution.py:593
  2.3 8.2 %collective-permute-start.1 = (f32[224,128]{1,0:T(8,128)S(1)}, f32[224,128]{1,0:T(8,128)S(1)}, u32[]{:S(2)}, u32[]{:S(2)}) collective-permute-start(f32[224,128]{1,0:T(8,128)S(1)} %get-tuple-element.34), channel_id=1, source_target_pairs={{0,3},{1,0},{2,1},{3,2},{4,7},{5,4},{6,5},{7,6},{8,11},{9,8},{10,9... | collective-permute-start | bytes 344072 | tf_op jit(solution)/shard_map/ppermute | solution.py:593
  4.3 6.2 %collective-permute-start.2 = (f32[32,640]{1,0:T(8,128)S(1)}, f32[32,640]{1,0:T(8,128)S(1)}, u32[]{:S(2)}, u32[]{:S(2)}) collective-permute-start(f32[32,640]{1,0:T(8,128)S(1)} %get-tuple-element.36), channel_id=1, source_target_pairs={{0,2},{1,3},{2,0},{3,1},{4,6},{5,7},{6,4},{7,5},{8,10},{9,11},{10,... | collective-permute-start | bytes 245768 | tf_op jit(solution)/shard_map/ppermute | solution.py:593
  6.5 2.7 %copy-start = (bf16[2,768,1920]{2,1,0:T(8,128)(2,1)S(1)}, bf16[2,768,1920]{2,1,0:T(8,128)(2,1)}, u32[]{:S(2)}) copy-start(bf16[2,768,1920]{2,1,0:T(8,128)(2,1)} %constant.2.clone.table_ref) | copy-start | bytes 17694724
  10.8 8.8 %collective-permute-start.3 = (f32[376,128]{1,0:T(8,128)S(1)}, f32[376,128]{1,0:T(8,128)S(1)}, u32[]{:S(2)}, u32[]{:S(2)}) collective-permute-start(f32[376,128]{1,0:T(8,128)S(1)} %get-tuple-element.40), channel_id=1, source_target_pairs={{0,4},{4,0},{8,12},{12,8},{16,20},{20,16},{24,28},{28,24},{1,5},{5... | collective-permute-start | bytes 577544 | tf_op jit(solution)/shard_map/ppermute | solution.py:597
  12.3 7.3 %collective-permute-start.4 = (f32[376,128]{1,0:T(8,128)S(1)}, f32[376,128]{1,0:T(8,128)S(1)}, u32[]{:S(2)}, u32[]{:S(2)}) collective-permute-start(f32[376,128]{1,0:T(8,128)S(1)} %get-tuple-element.41), channel_id=1, source_target_pairs={{4,8},{12,16},{20,24},{8,4},{16,12},{24,20},{5,9},{13,17},{21,25},... | collective-permute-start | bytes 577544 | tf_op jit(solution)/shard_map/ppermute | solution.py:602
  23.8 15.1 %collective-permute-start.5 = (f32[64,512]{1,0:T(8,128)S(1)}, f32[64,512]{1,0:T(8,128)S(1)}, u32[]{:S(2)}, u32[]{:S(2)}) collective-permute-start(f32[64,512]{1,0:T(8,128)S(1)} %get-tuple-element.56), channel_id=1, source_target_pairs={{0,1},{1,0},{2,3},{3,2},{4,5},{5,4},{6,7},{7,6},{8,9},{9,8},{10,11... | collective-permute-start | bytes 393224 | tf_op jit(solution)/shard_map/ppermute | solution.py:597
  23.9 15.1 %collective-permute-start.6 = (f32[64,512]{1,0:T(8,128)S(1)}, f32[64,512]{1,0:T(8,128)S(1)}, u32[]{:S(2)}, u32[]{:S(2)}) collective-permute-start(f32[64,512]{1,0:T(8,128)S(1)} %get-tuple-element.57), channel_id=1, source_target_pairs={{0,2},{1,3},{2,0},{3,1},{4,6},{5,7},{6,4},{7,5},{8,10},{9,11},{10,... | collective-permute-start | bytes 393224 | tf_op jit(solution)/shard_map/ppermute | solution.py:597
  25.8 13.1 %collective-permute-start.7 = (f32[64,512]{1,0:T(8,128)S(1)}, f32[64,512]{1,0:T(8,128)S(1)}, u32[]{:S(2)}, u32[]{:S(2)}) collective-permute-start(f32[64,512]{1,0:T(8,128)S(1)} %get-tuple-element.58), channel_id=1, source_target_pairs={{0,3},{1,2},{2,1},{3,0},{4,7},{5,6},{6,5},{7,4},{8,11},{9,10},{10,... | collective-permute-start | bytes 393224 | tf_op jit(solution)/shard_map/ppermute | solution.py:597

commit v5 on v4

--- a/solution.py
+++ b/solution.py
@@ -367,7 +367,7 @@
     shapes = [(plan.node_rows[k], plan.node_cols[k]) for k in range(COARSE)] + [(rows + 2 * NEAR, plan.col_frame)]
 
     def kernel(mis_ref, table_ref, *out_refs):
-        base_refs, surface_ref = out_refs[:LEVELS], out_refs[LEVELS]
+        base_refs, (surface_ref, once_ref, twice_ref) = out_refs[:LEVELS], out_refs[LEVELS:]
         col_tables, turned_tables, (own_t, _, _, wide_s, _, _) = plan.pick(table_ref)
         masks = plan.masks([height for height, _ in shapes])
         mis = mis_ref[...]
@@ -378,22 +378,26 @@
         base.append(smooth(jnp.concatenate([mis, blank], axis=0)) * masks[COARSE])
         for k in range(LEVELS):
             base_refs[k][...] = base[k]
+        once = autoreg(base[COARSE]) * masks[COARSE]
+        once_ref[...] = once
+        twice_ref[...] = level_scales[COARSE] * autoreg(once)
         fine = smooth(base[COARSE])
         blank = jnp.zeros((inner_rows - rows - 2 * NEAR, plan.col_frame), jnp.float32)
         fine = jnp.concatenate([fine[0 : rows + NEAR], blank, fine[rows + NEAR :]], axis=0)
         spread = jnp.concatenate([dot3(split(base[k]), turned_tables[k]) for k in range(COARSE)], axis=0)
         surface_ref[...] = fine + dot3(wide_s, split(spread))
 
-    *base, surface = call(kernel, shapes + [(inner_rows, plan.col_frame)], 24)(mis, tables)
-    return base, surface
-
-
-def operate(plan, mid, mid_surface, wt, side, near, following, tables):
+    outs = shapes + [(inner_rows, plan.col_frame)] + shapes[COARSE:] * 2
+    *base, surface, once, twice = call(kernel, outs, 24)(mis, tables)
+    return base, surface, once, twice
+
+
+def operate(plan, mid, mid_surface, mid_once, mid_twice, wt, side, near, following, tables):
     rows, cols, sr, lon_total = plan.rows, plan.cols, plan.swath_rows, plan.lon_total
     n_dev = plan.lat_total * lon_total
 
     def kernel(mid_surface_ref, wt_ref, side_ref, near_ref, next_ref, table_ref, *out_refs):
-        mid_refs, out_refs = out_refs[:LEVELS], out_refs[LEVELS:]
+        mid_refs, (once_ref, twice_ref), out_refs = out_refs[:LEVELS], out_refs[LEVELS : LEVELS + 2], out_refs[LEVELS + 2 :]
         base_refs, image_refs = out_refs[:LEVELS], out_refs[LEVELS : 2 * LEVELS]
         surface_refs, part_ref = out_refs[2 * LEVELS : -1], out_refs[-1]
         lat = lax.axis_index("lat")
@@ -446,6 +450,15 @@
         last = strip.shape[0] - NEAR
         added = [strip[last:], blank(rows - 2 * NEAR, strip), strip[0 : 2 * NEAR], strip[last - NEAR : last]]
         base.append(mid_refs[COARSE][...] + jnp.concatenate(added, axis=0))
+        short, short_mask = [jnp.concatenate([x[0 : 3 * NEAR], x[last - 2 * NEAR :]], axis=0) for x in (strip, strip_mask)]
+        once = autoreg(short) * short_mask
+
+        def place(x):
+            parts = [x[5 * NEAR :], blank(rows - 2 * NEAR, x), x[0 : 2 * NEAR], x[4 * NEAR : 5 * NEAR]]
+            return jnp.concatenate(parts, axis=0)
+
+        fine_once = once_ref[...] + place(once)
+        fine_twice = twice_ref[...] + place(level_scales[COARSE] * autoreg(once))
         fine = smooth(strip)
         added = [fine[last:], blank(rows - 2 * NEAR, fine), fine[0 : NEAR + INNER], fine[last - INNER : last]]
         surface = mid_surface_ref[...] + jnp.concatenate(added, axis=0)
@@ -460,9 +473,13 @@
         image.append(smooth(cut(misfit_again, COARSE, plan.near_rows[COARSE])))
         rough_base, rough_image = [], []
         for k in range(LEVELS):
-            once = autoreg(base[k]) * masks[k]
+            if k == COARSE:
+                once, twice = fine_once, fine_twice
+            else:
+                once = autoreg(base[k]) * masks[k]
+                twice = level_scales[k] * autoreg(once)
             rough_base.append(once)
-            image[k] = (image[k] + level_scales[k] * autoreg(once)) * masks[k]
+            image[k] = (image[k] + twice) * masks[k]
             rough_image.append(autoreg(image[k]))
         second = dot3(tile_s, spread(image, cols)) + smooth(image[COARSE])[0:rows, 0:cols]
 
@@ -542,7 +559,7 @@
 
     level_shapes = [(rows // s, cols // s) for s in SPACINGS]
     outs = level_shapes * 2 + [(2 * rows, cols)] + [(2 * sr, cols)] * (lon_total - 1) + [(n_dev, LANES)]
-    results = call(kernel, outs, 24)(mid_surface, wt, side, near, following, tables, *mid)
+    results = call(kernel, outs, 24)(mid_surface, wt, side, near, following, tables, *mid, mid_once, mid_twice)
     return results[:LEVELS], results[LEVELS : 2 * LEVELS], results[2 * LEVELS : -1], results[-1]
 
 
@@ -609,10 +626,10 @@
     tables = fetch(plan, own)
     right, *far, left = [turn(x, "lon", lon_total, k) for k, x in enumerate(windows, 1)]
     mis, side, near, following = misfit(plan, own, right, left, far, weight, tables)
-    mid, mid_surface = inside(plan, mis, tables)
+    mid, mid_surface, mid_once, mid_twice = inside(plan, mis, tables)
     near = flip(near, "lat", lat_total, 1)
     following = odd_swap(following, "lat", lat_total)
-    base, image, surfaces, parts = operate(plan, mid, mid_surface, weight, side, near, following, tables)
+    base, image, surfaces, parts = operate(plan, mid, mid_surface, mid_once, mid_twice, weight, side, near, following, tables)
     far_surfaces = [flip(x, "lon", lon_total, k) for k, x in enumerate(surfaces[1:], 1)]
     parts = lax.all_to_all(parts, ("lat", "lon"), split_axis=0, concat_axis=0, tiled=True)
     return tuple(finish(plan, parts, base, image, surfaces[0], far_surfaces))

time: 40.2 us -> 39.8 us (0.990)
  transfers between devices with their start and end apart: 8 -> 8, of which waited for: 2 -> 2; matrix products, arithmetic and copies ran while one was open for 0% -> 0% of each run, Pallas kernels for 7% -> 8%
where the time goes in v5:
time: 39.8 us; the launch traced here: 39.6 us
  blocking collectives  13 us (33%)
  Pallas kernels  9.25 us (23%)
  starting transfers between devices  8.99 us (23%)
  waiting for transfers between devices  4.96 us (12%)
  local copies, waits for them, and re-layouts  2.67 us (7%)
  between operations  0.68 us (2%)
    all_to_all x1, blocking collectives, body(): lax.all_to_all(parts, ('lat', 'lon'), split_axis=0, concat_axis=0, tiled=...  13 us
    pallas_call x5, Pallas kernels, run(): pl.pallas_call(kernel, out_shape=[jax.ShapeDtypeStruct(shape, jnp.float32...  8.68 us
    ppermute x3, starting transfers between devices, turn(): return lax.ppermute(x, axis, [(i, (i + k) % total) for i in range(total)])  4.76 us
    ppermute x4, waiting for transfers between devices, flip(): return lax.ppermute(x, axis, [(i, i ^ k) for i in range(total)])  4.22 us
    ppermute x4, starting transfers between devices, flip(): return lax.ppermute(x, axis, [(i, i ^ k) for i in range(total)])  3.56 us
    unnamed x2, local copies, waits for them, and re-layouts  2.67 us
  transfers between devices with their start and end apart: 8, of which 2 were waited for; matrix products, arithmetic and copies ran while one was open for 0% of the time, Pallas kernels for 8%

profile of v5, /device:TPU:0, one launch (start us, length us, event | category | flops | bytes accessed | tf_op | source)
XLA Modules:
  0.0 39.6 jit_solution(9758410408480743661)
XLA Ops:
  0.6 1.1 %shard_map.74 = (f32[128,512]{1,0:T(8,128)S(1)}, f32[32,640]{1,0:T(8,128)S(1)}, f32[224,128]{1,0:T(8,128)S(1)}, f32[32,640]{1,0:T(8,128)S(1)}, f32[224,128]{1,0:T(8,128)S(1)}) custom-call(f32[32,2048]{1,0:T(8,128)} %obs_hbm.1, s32[128,512]{1,0:T(8,128)} %gauge_hbm.1), custom_call_target="tpu_custom_call" | custom-call | tf_op jit(solution)/shard_map/pallas_call | solution.py:206
  1.8 0.5 %collective-permute-start = (f32[224,128]{1,0:T(8,128)S(1)}, f32[224,128]{1,0:T(8,128)S(1)}, u32[]{:S(2)}, u32[]{:S(2)}) collective-permute-start(f32[224,128]{1,0:T(8,128)S(1)} %get-tuple-element.35), channel_id=1, source_target_pairs={{0,1},{1,2},{2,3},{3,0},{4,5},{5,6},{6,7},{7,4},{8,9},{9,10},{10,1... | collective-permute-start | bytes 344072 | tf_op jit(solution)/shard_map/ppermute | solution.py:610
  2.3 2.0 %collective-permute-start.1 = (f32[224,128]{1,0:T(8,128)S(1)}, f32[224,128]{1,0:T(8,128)S(1)}, u32[]{:S(2)}, u32[]{:S(2)}) collective-permute-start(f32[224,128]{1,0:T(8,128)S(1)} %get-tuple-element.36), channel_id=1, source_target_pairs={{0,3},{1,0},{2,1},{3,2},{4,7},{5,4},{6,5},{7,6},{8,11},{9,8},{10,9... | collective-permute-start | bytes 344072 | tf_op jit(solution)/shard_map/ppermute | solution.py:610
  4.3 2.2 %collective-permute-start.2 = (f32[32,640]{1,0:T(8,128)S(1)}, f32[32,640]{1,0:T(8,128)S(1)}, u32[]{:S(2)}, u32[]{:S(2)}) collective-permute-start(f32[32,640]{1,0:T(8,128)S(1)} %get-tuple-element.38), channel_id=1, source_target_pairs={{0,2},{1,3},{2,0},{3,1},{4,6},{5,7},{6,4},{7,5},{8,10},{9,11},{10,... | collective-permute-start | bytes 245768 | tf_op jit(solution)/shard_map/ppermute | solution.py:610
  6.5 0.0 copy-start
  6.5 2.7 %copy-done = bf16[2,768,1920]{2,1,0:T(8,128)(2,1)S(1)} copy-done((bf16[2,768,1920]{2,1,0:T(8,128)(2,1)S(1)}, bf16[2,768,1920]{2,1,0:T(8,128)(2,1)}, u32[]{:S(2)}) %copy-start) | copy-done | bytes 5898264
  9.2 0.6 %shard_map.75.table_ref = bf16[2,768,1920]{2,1,0:T(8,128)(2,1)S(1)} custom-call(bf16[2,768,1920]{2,1,0:T(8,128)(2,1)S(1)} %copy-done, f32[32,640]{1,0:T(8,128)S(1)} %get-tuple-element.34.after_ref.own_ref), custom_call_target="tpu_custom_call" | custom-call | bytes 11796480 | tf_op jit(solution)/shard_map/pallas_call | solution.py:354
  9.8 0.7 %collective-permute-done.2.rest_0_ = f32[32,640]{1,0:T(8,128)S(1)} collective-permute-done((f32[32,640]{1,0:T(8,128)S(1)}, f32[32,640]{1,0:T(8,128)S(1)}, u32[]{:S(2)}, u32[]{:S(2)}) %collective-permute-start.2) | collective-permute-done | bytes 81952 | tf_op jit(solution)/shard_map/ppermute | solution.py:610
  10.5 0.0 collective-permute-done.right_ref
  10.5 0.0 collective-permute-done.1.left_ref
  10.5 0.3 shard_map.76
  10.8 1.5 %collective-permute-start.3 = (f32[376,128]{1,0:T(8,128)S(1)}, f32[376,128]{1,0:T(8,128)S(1)}, u32[]{:S(2)}, u32[]{:S(2)}) collective-permute-start(f32[376,128]{1,0:T(8,128)S(1)} %get-tuple-element.42), channel_id=1, source_target_pairs={{0,4},{4,0},{8,12},{12,8},{16,20},{20,16},{24,28},{28,24},{1,5},{5... | collective-permute-start | bytes 577544 | tf_op jit(solution)/shard_map/ppermute | solution.py:614
  12.3 0.7 %collective-permute-start.4 = (f32[376,128]{1,0:T(8,128)S(1)}, f32[376,128]{1,0:T(8,128)S(1)}, u32[]{:S(2)}, u32[]{:S(2)}) collective-permute-start(f32[376,128]{1,0:T(8,128)S(1)} %get-tuple-element.43), channel_id=1, source_target_pairs={{4,8},{12,16},{20,24},{8,4},{16,12},{24,20},{5,9},{13,17},{21,25},... | collective-permute-start | bytes 577544 | tf_op jit(solution)/shard_map/ppermute | solution.py:619
  13.0 2.4 %shard_map.77 = (f32[32,128]{1,0:T(8,128)S(1)}, f32[64,256]{1,0:T(8,128)S(1)}, f32[112,384]{1,0:T(8,128)S(1)}, f32[144,640]{1,0:T(8,128)S(1)}, f32[192,640]{1,0:...) custom-call(f32[128,640]{1,0:T(8,128)S(1)} %get-tuple-element.39.mis_ref, ...), custom_call_target="tpu_custom_call" | custom-call | tf_op jit(solution)/shard_map/pallas_call | solution.py:206
  15.4 4.2 %collective-permute-done.3.near_ref = f32[376,128]{1,0:T(8,128)S(1)} collective-permute-done((f32[376,128]{1,0:T(8,128)S(1)}, f32[376,128]{1,0:T(8,128)S(1)}, u32[]{:S(2)}, u32[]{:S(2)}) %collective-permute-start.3) | collective-permute-done | bytes 192544 | tf_op jit(solution)/shard_map/ppermute | solution.py:614
  19.6 0.0 collective-permute-done.4.next_ref
  19.6 3.8 %shard_map.78 = (f32[16,64]{1,0:T(8,128)S(1)}, f32[32,128]{1,0:T(8,128)S(1)}, f32[64,256]{1,0:T(8,128)S(1)}, f32[128,512]{1,0:T(8,128)S(1)}, f32[16,64]{1,0:T(8,...) custom-call(f32[192,640]{1,0:T(8,128)S(1)} %get-tuple-element.40.mid, ...), custom_call_target="tpu_custom_call" | custom-call | tf_op jit(solution)/shard_map/pallas_call | solution.py:206
  23.4 0.0 collective-permute-start.5
  23.5 2.0 %collective-permute-start.6 = (f32[64,512]{1,0:T(8,128)S(1)}, f32[64,512]{1,0:T(8,128)S(1)}, u32[]{:S(2)}, u32[]{:S(2)}) collective-permute-start(f32[64,512]{1,0:T(8,128)S(1)} %get-tuple-element.61), channel_id=1, source_target_pairs={{0,2},{1,3},{2,0},{3,1},{4,6},{5,7},{6,4},{7,5},{8,10},{9,11},{10,... | collective-permute-start | bytes 393224 | tf_op jit(solution)/shard_map/ppermute | solution.py:614
  25.4 0.1 collective-permute-start.7
  25.5 13.0 %all_to_all.11 = f32[32,1,128]{2,1,0:T(1,128)S(1)} all-to-all(f32[32,1,128]{2,1,0:T(1,128)S(1)} %bitcast.5), channel_id=1, replica_groups=mesh['lat'=8,'lon'=4] {'lat','lon'}, dimensions={0} | all-to-all | bytes 32768 | tf_op jit(solution)/shard_map/all_to_all | solution.py:634
  38.5 0.0 collective-permute-done.5.rest_9_
  38.5 0.0 collective-permute-done.6.rest_10_
  38.5 0.0 collective-permute-done.7.rest_11_
  38.6 1.0 %shard_map.79 = (f32[16,64]{1,0:T(8,128)}, f32[32,128]{1,0:T(8,128)}, f32[64,256]{1,0:T(8,128)}, f32[128,512]{1,0:T(8,128)}, f32[32,2048]{1,0:T(8,128)}) custom-call(f32[32,128]{1,0:T(8,128)S(1)} %bitcast.4, f32[16,64]{1,0:T(8,128)S(1)} %get-tuple-element.51.rest_0_, f32[32,128]{1,0:T(8,128)S(1)} %get-tuple-element.52.rest_1_, ...), custom_call_target="tpu_custom_call" | custom-call | tf_op jit(solution)/shard_map/pallas_call | solution.py:206
Async XLA Ops:
  1.8 8.7 %collective-permute-start = (f32[224,128]{1,0:T(8,128)S(1)}, f32[224,128]{1,0:T(8,128)S(1)}, u32[]{:S(2)}, u32[]{:S(2)}) collective-permute-start(f32[224,128]{1,0:T(8,128)S(1)} %get-tuple-element.35), channel_id=1, source_target_pairs={{0,1},{1,2},{2,3},{3,0},{4,5},{5,6},{6,7},{7,4},{8,9},{9,10},{10,1... | collective-permute-start | bytes 344072 | tf_op jit(solution)/shard_map/ppermute | solution.py:610
  2.3 8.2 %collective-permute-start.1 = (f32[224,128]{1,0:T(8,128)S(1)}, f32[224,128]{1,0:T(8,128)S(1)}, u32[]{:S(2)}, u32[]{:S(2)}) collective-permute-start(f32[224,128]{1,0:T(8,128)S(1)} %get-tuple-element.36), channel_id=1, source_target_pairs={{0,3},{1,0},{2,1},{3,2},{4,7},{5,4},{6,5},{7,6},{8,11},{9,8},{10,9... | collective-permute-start | bytes 344072 | tf_op jit(solution)/shard_map/ppermute | solution.py:610
  4.3 6.2 %collective-permute-start.2 = (f32[32,640]{1,0:T(8,128)S(1)}, f32[32,640]{1,0:T(8,128)S(1)}, u32[]{:S(2)}, u32[]{:S(2)}) collective-permute-start(f32[32,640]{1,0:T(8,128)S(1)} %get-tuple-element.38), channel_id=1, source_target_pairs={{0,2},{1,3},{2,0},{3,1},{4,6},{5,7},{6,4},{7,5},{8,10},{9,11},{10,... | collective-permute-start | bytes 245768 | tf_op jit(solution)/shard_map/ppermute | solution.py:610
  6.5 2.7 %copy-start = (bf16[2,768,1920]{2,1,0:T(8,128)(2,1)S(1)}, bf16[2,768,1920]{2,1,0:T(8,128)(2,1)}, u32[]{:S(2)}) copy-start(bf16[2,768,1920]{2,1,0:T(8,128)(2,1)} %constant.2.clone.table_ref) | copy-start | bytes 17694724
  10.8 8.8 %collective-permute-start.3 = (f32[376,128]{1,0:T(8,128)S(1)}, f32[376,128]{1,0:T(8,128)S(1)}, u32[]{:S(2)}, u32[]{:S(2)}) collective-permute-start(f32[376,128]{1,0:T(8,128)S(1)} %get-tuple-element.42), channel_id=1, source_target_pairs={{0,4},{4,0},{8,12},{12,8},{16,20},{20,16},{24,28},{28,24},{1,5},{5... | collective-permute-start | bytes 577544 | tf_op jit(solution)/shard_map/ppermute | solution.py:614
  12.3 7.3 %collective-permute-start.4 = (f32[376,128]{1,0:T(8,128)S(1)}, f32[376,128]{1,0:T(8,128)S(1)}, u32[]{:S(2)}, u32[]{:S(2)}) collective-permute-start(f32[376,128]{1,0:T(8,128)S(1)} %get-tuple-element.43), channel_id=1, source_target_pairs={{4,8},{12,16},{20,24},{8,4},{16,12},{24,20},{5,9},{13,17},{21,25},... | collective-permute-start | bytes 577544 | tf_op jit(solution)/shard_map/ppermute | solution.py:619
  23.4 15.1 %collective-permute-start.5 = (f32[64,512]{1,0:T(8,128)S(1)}, f32[64,512]{1,0:T(8,128)S(1)}, u32[]{:S(2)}, u32[]{:S(2)}) collective-permute-start(f32[64,512]{1,0:T(8,128)S(1)} %get-tuple-element.60), channel_id=1, source_target_pairs={{0,1},{1,0},{2,3},{3,2},{4,5},{5,4},{6,7},{7,6},{8,9},{9,8},{10,11... | collective-permute-start | bytes 393224 | tf_op jit(solution)/shard_map/ppermute | solution.py:614
  23.5 15.1 %collective-permute-start.6 = (f32[64,512]{1,0:T(8,128)S(1)}, f32[64,512]{1,0:T(8,128)S(1)}, u32[]{:S(2)}, u32[]{:S(2)}) collective-permute-start(f32[64,512]{1,0:T(8,128)S(1)} %get-tuple-element.61), channel_id=1, source_target_pairs={{0,2},{1,3},{2,0},{3,1},{4,6},{5,7},{6,4},{7,5},{8,10},{9,11},{10,... | collective-permute-start | bytes 393224 | tf_op jit(solution)/shard_map/ppermute | solution.py:614
  25.4 13.1 %collective-permute-start.7 = (f32[64,512]{1,0:T(8,128)S(1)}, f32[64,512]{1,0:T(8,128)S(1)}, u32[]{:S(2)}, u32[]{:S(2)}) collective-permute-start(f32[64,512]{1,0:T(8,128)S(1)} %get-tuple-element.62), channel_id=1, source_target_pairs={{0,3},{1,2},{2,1},{3,0},{4,7},{5,6},{6,5},{7,4},{8,11},{9,10},{10,... | collective-permute-start | bytes 393224 | tf_op jit(solution)/shard_map/ppermute | solution.py:614

commit v6 on v5

--- a/solution.py
+++ b/solution.py
@@ -362,12 +362,12 @@
     )(table, after)
 
 
-def inside(plan, mis, tables):
+def inside(plan, mis, wt, side, tables):
     rows, inner_rows = plan.rows, plan.inner_rows
     shapes = [(plan.node_rows[k], plan.node_cols[k]) for k in range(COARSE)] + [(rows + 2 * NEAR, plan.col_frame)]
 
-    def kernel(mis_ref, table_ref, *out_refs):
-        base_refs, (surface_ref, once_ref, twice_ref) = out_refs[:LEVELS], out_refs[LEVELS:]
+    def kernel(mis_ref, wt_ref, side_ref, table_ref, *out_refs):
+        base_refs, (surface_ref, once_ref, twice_ref, again_ref) = out_refs[:LEVELS], out_refs[LEVELS:]
         col_tables, turned_tables, (own_t, _, _, wide_s, _, _) = plan.pick(table_ref)
         masks = plan.masks([height for height, _ in shapes])
         mis = mis_ref[...]
@@ -385,19 +385,24 @@
         blank = jnp.zeros((inner_rows - rows - 2 * NEAR, plan.col_frame), jnp.float32)
         fine = jnp.concatenate([fine[0 : rows + NEAR], blank, fine[rows + NEAR :]], axis=0)
         spread = jnp.concatenate([dot3(split(base[k]), turned_tables[k]) for k in range(COARSE)], axis=0)
-        surface_ref[...] = fine + dot3(wide_s, split(spread))
-
-    outs = shapes + [(inner_rows, plan.col_frame)] + shapes[COARSE:] * 2
-    *base, surface, once, twice = call(kernel, outs, 24)(mis, tables)
-    return base, surface, once, twice
-
-
-def operate(plan, mid, mid_surface, mid_once, mid_twice, wt, side, near, following, tables):
+        surface = fine + dot3(wide_s, split(spread))
+        surface_ref[...] = surface
+        again = jnp.concatenate([wt_ref[...], side_ref[...]], axis=1) * surface[0:rows]
+        blank = jnp.zeros((2 * NEAR, plan.col_frame), jnp.float32)
+        again_ref[...] = smooth(jnp.concatenate([again, blank], axis=0))
+
+    outs = shapes + [(inner_rows, plan.col_frame)] + shapes[COARSE:] * 3
+    *base, surface, once, twice, again = call(kernel, outs, 24)(mis, wt, side, tables)
+    return base, surface, once, twice, again
+
+
+def operate(plan, mid, mid_surface, mid_once, mid_twice, mid_again, wt, side, near, following, tables):
     rows, cols, sr, lon_total = plan.rows, plan.cols, plan.swath_rows, plan.lon_total
     n_dev = plan.lat_total * lon_total
 
     def kernel(mid_surface_ref, wt_ref, side_ref, near_ref, next_ref, table_ref, *out_refs):
-        mid_refs, (once_ref, twice_ref), out_refs = out_refs[:LEVELS], out_refs[LEVELS : LEVELS + 2], out_refs[LEVELS + 2 :]
+        mid_refs, (once_ref, twice_ref, again_ref) = out_refs[:LEVELS], out_refs[LEVELS : LEVELS + 3]
+        out_refs = out_refs[LEVELS + 3 :]
         base_refs, image_refs = out_refs[:LEVELS], out_refs[LEVELS : 2 * LEVELS]
         surface_refs, part_ref = out_refs[2 * LEVELS : -1], out_refs[-1]
         lat = lax.axis_index("lat")
@@ -461,16 +466,27 @@
         fine_twice = twice_ref[...] + place(level_scales[COARSE] * autoreg(once))
         fine = smooth(strip)
         added = [fine[last:], blank(rows - 2 * NEAR, fine), fine[0 : NEAR + INNER], fine[last - INNER : last]]
-        surface = mid_surface_ref[...] + jnp.concatenate(added, axis=0)
+        extra = jnp.concatenate(added, axis=0)
         coarse = dot3(edge_s, spread(edge, plan.col_frame))
         body_rows = coarse.shape[0] - EDGE
         added = [coarse[body_rows:], blank(rows - 2 * EDGE, coarse), coarse[0:body_rows]]
-        surface = surface + jnp.concatenate(added, axis=0)
+        extra = extra + jnp.concatenate(added, axis=0)
+        surface = mid_surface_ref[...] + extra
         masks = plan.masks(plan.near_rows)
 
         misfit_again = weight * surface
         image = collect(dot3(inner_t, split(misfit_again)), plan.near_starts)
-        image.append(smooth(cut(misfit_again, COARSE, plan.near_rows[COARSE])))
+        reach = EDGE + NEAR
+        changed = [
+            weight[rows - reach : rows] * extra[rows - reach : rows],
+            misfit_again[rows : rows + NEAR],
+            misfit_again[plan.inner_rows - NEAR :],
+            weight[0:reach] * extra[0:reach],
+        ]
+        changed = smooth(jnp.concatenate(changed, axis=0))
+        first = reach + 2 * NEAR
+        changed = [changed[first:], blank(rows - 2 * reach, changed), changed[0:first]]
+        image.append(again_ref[...] + jnp.concatenate(changed, axis=0))
         rough_base, rough_image = [], []
         for k in range(LEVELS):
             if k == COARSE:
@@ -559,7 +575,7 @@
 
     level_shapes = [(rows // s, cols // s) for s in SPACINGS]
     outs = level_shapes * 2 + [(2 * rows, cols)] + [(2 * sr, cols)] * (lon_total - 1) + [(n_dev, LANES)]
-    results = call(kernel, outs, 24)(mid_surface, wt, side, near, following, tables, *mid, mid_once, mid_twice)
+    results = call(kernel, outs, 24)(mid_surface, wt, side, near, following, tables, *mid, mid_once, mid_twice, mid_again)
     return results[:LEVELS], results[LEVELS : 2 * LEVELS], results[2 * LEVELS : -1], results[-1]
 
 
@@ -626,10 +642,12 @@
     tables = fetch(plan, own)
     right, *far, left = [turn(x, "lon", lon_total, k) for k, x in enumerate(windows, 1)]
     mis, side, near, following = misfit(plan, own, right, left, far, weight, tables)
-    mid, mid_surface, mid_once, mid_twice = inside(plan, mis, tables)
+    mid, mid_surface, mid_once, mid_twice, mid_again = inside(plan, mis, weight, side, tables)
     near = flip(near, "lat", lat_total, 1)
     following = odd_swap(following, "lat", lat_total)
-    base, image, surfaces, parts = operate(plan, mid, mid_surface, mid_once, mid_twice, weight, side, near, following, tables)
+    base, image, surfaces, parts = operate(
+        plan, mid, mid_surface, mid_once, mid_twice, mid_again, weight, side, near, following, tables
+    )
     far_surfaces = [flip(x, "lon", lon_total, k) for k, x in enumerate(surfaces[1:], 1)]
     parts = lax.all_to_all(parts, ("lat", "lon"), split_axis=0, concat_axis=0, tiled=True)
     return tuple(finish(plan, parts, base, image, surfaces[0], far_surfaces))

time: 39.8 us -> 39.5 us (level)
  no operation moved by 1% of the time
where the time goes in v6:
time: 39.5 us; the launch traced here: 39.3 us
  blocking collectives  13 us (33%)
  Pallas kernels  9.12 us (23%)
  starting transfers between devices  8.99 us (23%)
  waiting for transfers between devices  4.8 us (12%)
  local copies, waits for them, and re-layouts  2.67 us (7%)
  between operations  0.68 us (2%)
    all_to_all x1, blocking collectives, body(): lax.all_to_all(parts, ('lat', 'lon'), split_axis=0, concat_axis=0, tiled=...  13 us
    pallas_call x5, Pallas kernels, run(): pl.pallas_call(kernel, out_shape=[jax.ShapeDtypeStruct(shape, jnp.float32...  8.55 us
    ppermute x3, starting transfers between devices, turn(): return lax.ppermute(x, axis, [(i, (i + k) % total) for i in range(total)])  4.76 us
    ppermute x4, waiting for transfers between devices, flip(): return lax.ppermute(x, axis, [(i, i ^ k) for i in range(total)])  4.06 us
    ppermute x4, starting transfers between devices, flip(): return lax.ppermute(x, axis, [(i, i ^ k) for i in range(total)])  3.56 us
    unnamed x2, local copies, waits for them, and re-layouts  2.67 us
  transfers between devices with their start and end apart: 8, of which 2 were waited for; matrix products, arithmetic and copies ran while one was open for 0% of the time, Pallas kernels for 8%

profile of v6, /device:TPU:0, one launch (start us, length us, event | category | flops | bytes accessed | tf_op | source)
XLA Modules:
  0.0 39.3 jit_solution(626625488759270947)
XLA Ops:
  0.6 1.1 %shard_map.74 = (f32[128,512]{1,0:T(8,128)S(1)}, f32[32,640]{1,0:T(8,128)S(1)}, f32[224,128]{1,0:T(8,128)S(1)}, f32[32,640]{1,0:T(8,128)S(1)}, f32[224,128]{1,0:T(8,128)S(1)}) custom-call(f32[32,2048]{1,0:T(8,128)} %obs_hbm.1, s32[128,512]{1,0:T(8,128)} %gauge_hbm.1), custom_call_target="tpu_custom_call" | custom-call | tf_op jit(solution)/shard_map/pallas_call | solution.py:206
  1.8 0.5 %collective-permute-start = (f32[224,128]{1,0:T(8,128)S(1)}, f32[224,128]{1,0:T(8,128)S(1)}, u32[]{:S(2)}, u32[]{:S(2)}) collective-permute-start(f32[224,128]{1,0:T(8,128)S(1)} %get-tuple-element.36), channel_id=1, source_target_pairs={{0,1},{1,2},{2,3},{3,0},{4,5},{5,6},{6,7},{7,4},{8,9},{9,10},{10,1... | collective-permute-start | bytes 344072 | tf_op jit(solution)/shard_map/ppermute | solution.py:626
  2.3 2.0 %collective-permute-start.1 = (f32[224,128]{1,0:T(8,128)S(1)}, f32[224,128]{1,0:T(8,128)S(1)}, u32[]{:S(2)}, u32[]{:S(2)}) collective-permute-start(f32[224,128]{1,0:T(8,128)S(1)} %get-tuple-element.37), channel_id=1, source_target_pairs={{0,3},{1,0},{2,1},{3,2},{4,7},{5,4},{6,5},{7,6},{8,11},{9,8},{10,9... | collective-permute-start | bytes 344072 | tf_op jit(solution)/shard_map/ppermute | solution.py:626
  4.3 2.2 %collective-permute-start.2 = (f32[32,640]{1,0:T(8,128)S(1)}, f32[32,640]{1,0:T(8,128)S(1)}, u32[]{:S(2)}, u32[]{:S(2)}) collective-permute-start(f32[32,640]{1,0:T(8,128)S(1)} %get-tuple-element.39), channel_id=1, source_target_pairs={{0,2},{1,3},{2,0},{3,1},{4,6},{5,7},{6,4},{7,5},{8,10},{9,11},{10,... | collective-permute-start | bytes 245768 | tf_op jit(solution)/shard_map/ppermute | solution.py:626
  6.5 0.0 copy-start
  6.5 2.7 %copy-done = bf16[2,768,1920]{2,1,0:T(8,128)(2,1)S(1)} copy-done((bf16[2,768,1920]{2,1,0:T(8,128)(2,1)S(1)}, bf16[2,768,1920]{2,1,0:T(8,128)(2,1)}, u32[]{:S(2)}) %copy-start) | copy-done | bytes 5898264
  9.2 0.6 %shard_map.75.table_ref = bf16[2,768,1920]{2,1,0:T(8,128)(2,1)S(1)} custom-call(bf16[2,768,1920]{2,1,0:T(8,128)(2,1)S(1)} %copy-done, f32[32,640]{1,0:T(8,128)S(1)} %get-tuple-element.35.after_ref.own_ref), custom_call_target="tpu_custom_call" | custom-call | bytes 11796480 | tf_op jit(solution)/shard_map/pallas_call | solution.py:354
  9.8 0.7 %collective-permute-done.2.rest_0_ = f32[32,640]{1,0:T(8,128)S(1)} collective-permute-done((f32[32,640]{1,0:T(8,128)S(1)}, f32[32,640]{1,0:T(8,128)S(1)}, u32[]{:S(2)}, u32[]{:S(2)}) %collective-permute-start.2) | collective-permute-done | bytes 81952 | tf_op jit(solution)/shard_map/ppermute | solution.py:626
  10.5 0.0 collective-permute-done.right_ref
  10.5 0.0 collective-permute-done.1.left_ref
  10.5 0.3 shard_map.76
  10.8 1.5 %collective-permute-start.3 = (f32[376,128]{1,0:T(8,128)S(1)}, f32[376,128]{1,0:T(8,128)S(1)}, u32[]{:S(2)}, u32[]{:S(2)}) collective-permute-start(f32[376,128]{1,0:T(8,128)S(1)} %get-tuple-element.43), channel_id=1, source_target_pairs={{0,4},{4,0},{8,12},{12,8},{16,20},{20,16},{24,28},{28,24},{1,5},{5... | collective-permute-start | bytes 577544 | tf_op jit(solution)/shard_map/ppermute | solution.py:630
  12.3 0.7 %collective-permute-start.4 = (f32[376,128]{1,0:T(8,128)S(1)}, f32[376,128]{1,0:T(8,128)S(1)}, u32[]{:S(2)}, u32[]{:S(2)}) collective-permute-start(f32[376,128]{1,0:T(8,128)S(1)} %get-tuple-element.44), channel_id=1, source_target_pairs={{4,8},{12,16},{20,24},{8,4},{16,12},{24,20},{5,9},{13,17},{21,25},... | collective-permute-start | bytes 577544 | tf_op jit(solution)/shard_map/ppermute | solution.py:635
  13.0 2.6 %shard_map.77 = (f32[32,128]{1,0:T(8,128)S(1)}, f32[64,256]{1,0:T(8,128)S(1)}, f32[112,384]{1,0:T(8,128)S(1)}, f32[144,640]{1,0:T(8,128)S(1)}, f32[192,640]{1,0:...) custom-call(f32[128,640]{1,0:T(8,128)S(1)} %get-tuple-element.40.mis_ref, ...), custom_call_target="tpu_custom_call" | custom-call | tf_op jit(solution)/shard_map/pallas_call | solution.py:206
  15.6 4.0 %collective-permute-done.3.near_ref = f32[376,128]{1,0:T(8,128)S(1)} collective-permute-done((f32[376,128]{1,0:T(8,128)S(1)}, f32[376,128]{1,0:T(8,128)S(1)}, u32[]{:S(2)}, u32[]{:S(2)}) %collective-permute-start.3) | collective-permute-done | bytes 192544 | tf_op jit(solution)/shard_map/ppermute | solution.py:630
  19.6 0.0 collective-permute-done.4.next_ref
  19.6 3.5 %shard_map.78 = (f32[16,64]{1,0:T(8,128)S(1)}, f32[32,128]{1,0:T(8,128)S(1)}, f32[64,256]{1,0:T(8,128)S(1)}, f32[128,512]{1,0:T(8,128)S(1)}, f32[16,64]{1,0:T(8,...) custom-call(f32[192,640]{1,0:T(8,128)S(1)} %get-tuple-element.42.mid, ...), custom_call_target="tpu_custom_call" | custom-call | tf_op jit(solution)/shard_map/pallas_call | solution.py:206
  23.2 0.0 collective-permute-start.5
  23.2 2.0 %collective-permute-start.6 = (f32[64,512]{1,0:T(8,128)S(1)}, f32[64,512]{1,0:T(8,128)S(1)}, u32[]{:S(2)}, u32[]{:S(2)}) collective-permute-start(f32[64,512]{1,0:T(8,128)S(1)} %get-tuple-element.63), channel_id=1, source_target_pairs={{0,2},{1,3},{2,0},{3,1},{4,6},{5,7},{6,4},{7,5},{8,10},{9,11},{10,... | collective-permute-start | bytes 393224 | tf_op jit(solution)/shard_map/ppermute | solution.py:630
  25.2 0.1 collective-permute-start.7
  25.2 13.0 %all_to_all.11 = f32[32,1,128]{2,1,0:T(1,128)S(1)} all-to-all(f32[32,1,128]{2,1,0:T(1,128)S(1)} %bitcast.5), channel_id=1, replica_groups=mesh['lat'=8,'lon'=4] {'lat','lon'}, dimensions={0} | all-to-all | bytes 32768 | tf_op jit(solution)/shard_map/all_to_all | solution.py:652
  38.3 0.0 collective-permute-done.5.rest_9_
  38.3 0.0 collective-permute-done.6.rest_10_
  38.3 0.0 collective-permute-done.7.rest_11_
  38.3 1.0 %shard_map.79 = (f32[16,64]{1,0:T(8,128)}, f32[32,128]{1,0:T(8,128)}, f32[64,256]{1,0:T(8,128)}, f32[128,512]{1,0:T(8,128)}, f32[32,2048]{1,0:T(8,128)}) custom-call(f32[32,128]{1,0:T(8,128)S(1)} %bitcast.4, f32[16,64]{1,0:T(8,128)S(1)} %get-tuple-element.53.rest_0_, f32[32,128]{1,0:T(8,128)S(1)} %get-tuple-element.54.rest_1_, ...), custom_call_target="tpu_custom_call" | custom-call | tf_op jit(solution)/shard_map/pallas_call | solution.py:206
Async XLA Ops:
  1.8 8.7 %collective-permute-start = (f32[224,128]{1,0:T(8,128)S(1)}, f32[224,128]{1,0:T(8,128)S(1)}, u32[]{:S(2)}, u32[]{:S(2)}) collective-permute-start(f32[224,128]{1,0:T(8,128)S(1)} %get-tuple-element.36), channel_id=1, source_target_pairs={{0,1},{1,2},{2,3},{3,0},{4,5},{5,6},{6,7},{7,4},{8,9},{9,10},{10,1... | collective-permute-start | bytes 344072 | tf_op jit(solution)/shard_map/ppermute | solution.py:626
  2.3 8.2 %collective-permute-start.1 = (f32[224,128]{1,0:T(8,128)S(1)}, f32[224,128]{1,0:T(8,128)S(1)}, u32[]{:S(2)}, u32[]{:S(2)}) collective-permute-start(f32[224,128]{1,0:T(8,128)S(1)} %get-tuple-element.37), channel_id=1, source_target_pairs={{0,3},{1,0},{2,1},{3,2},{4,7},{5,4},{6,5},{7,6},{8,11},{9,8},{10,9... | collective-permute-start | bytes 344072 | tf_op jit(solution)/shard_map/ppermute | solution.py:626
  4.3 6.2 %collective-permute-start.2 = (f32[32,640]{1,0:T(8,128)S(1)}, f32[32,640]{1,0:T(8,128)S(1)}, u32[]{:S(2)}, u32[]{:S(2)}) collective-permute-start(f32[32,640]{1,0:T(8,128)S(1)} %get-tuple-element.39), channel_id=1, source_target_pairs={{0,2},{1,3},{2,0},{3,1},{4,6},{5,7},{6,4},{7,5},{8,10},{9,11},{10,... | collective-permute-start | bytes 245768 | tf_op jit(solution)/shard_map/ppermute | solution.py:626
  6.5 2.7 %copy-start = (bf16[2,768,1920]{2,1,0:T(8,128)(2,1)S(1)}, bf16[2,768,1920]{2,1,0:T(8,128)(2,1)}, u32[]{:S(2)}) copy-start(bf16[2,768,1920]{2,1,0:T(8,128)(2,1)} %constant.2.clone.table_ref) | copy-start | bytes 17694724
  10.8 8.8 %collective-permute-start.3 = (f32[376,128]{1,0:T(8,128)S(1)}, f32[376,128]{1,0:T(8,128)S(1)}, u32[]{:S(2)}, u32[]{:S(2)}) collective-permute-start(f32[376,128]{1,0:T(8,128)S(1)} %get-tuple-element.43), channel_id=1, source_target_pairs={{0,4},{4,0},{8,12},{12,8},{16,20},{20,16},{24,28},{28,24},{1,5},{5... | collective-permute-start | bytes 577544 | tf_op jit(solution)/shard_map/ppermute | solution.py:630
  12.3 7.3 %collective-permute-start.4 = (f32[376,128]{1,0:T(8,128)S(1)}, f32[376,128]{1,0:T(8,128)S(1)}, u32[]{:S(2)}, u32[]{:S(2)}) collective-permute-start(f32[376,128]{1,0:T(8,128)S(1)} %get-tuple-element.44), channel_id=1, source_target_pairs={{4,8},{12,16},{20,24},{8,4},{16,12},{24,20},{5,9},{13,17},{21,25},... | collective-permute-start | bytes 577544 | tf_op jit(solution)/shard_map/ppermute | solution.py:635
  23.2 15.1 %collective-permute-start.5 = (f32[64,512]{1,0:T(8,128)S(1)}, f32[64,512]{1,0:T(8,128)S(1)}, u32[]{:S(2)}, u32[]{:S(2)}) collective-permute-start(f32[64,512]{1,0:T(8,128)S(1)} %get-tuple-element.62), channel_id=1, source_target_pairs={{0,1},{1,0},{2,3},{3,2},{4,5},{5,4},{6,7},{7,6},{8,9},{9,8},{10,11... | collective-permute-start | bytes 393224 | tf_op jit(solution)/shard_map/ppermute | solution.py:630
  23.2 15.1 %collective-permute-start.6 = (f32[64,512]{1,0:T(8,128)S(1)}, f32[64,512]{1,0:T(8,128)S(1)}, u32[]{:S(2)}, u32[]{:S(2)}) collective-permute-start(f32[64,512]{1,0:T(8,128)S(1)} %get-tuple-element.63), channel_id=1, source_target_pairs={{0,2},{1,3},{2,0},{3,1},{4,6},{5,7},{6,4},{7,5},{8,10},{9,11},{10,... | collective-permute-start | bytes 393224 | tf_op jit(solution)/shard_map/ppermute | solution.py:630
  25.2 13.1 %collective-permute-start.7 = (f32[64,512]{1,0:T(8,128)S(1)}, f32[64,512]{1,0:T(8,128)S(1)}, u32[]{:S(2)}, u32[]{:S(2)}) collective-permute-start(f32[64,512]{1,0:T(8,128)S(1)} %get-tuple-element.64), channel_id=1, source_target_pairs={{0,3},{1,2},{2,1},{3,0},{4,7},{5,6},{6,5},{7,4},{8,11},{9,10},{10,... | collective-permute-start | bytes 393224 | tf_op jit(solution)/shard_map/ppermute | solution.py:630

commit v7 on v6

--- a/solution.py
+++ b/solution.py
@@ -367,7 +367,7 @@
     shapes = [(plan.node_rows[k], plan.node_cols[k]) for k in range(COARSE)] + [(rows + 2 * NEAR, plan.col_frame)]
 
     def kernel(mis_ref, wt_ref, side_ref, table_ref, *out_refs):
-        base_refs, (surface_ref, once_ref, twice_ref, again_ref) = out_refs[:LEVELS], out_refs[LEVELS:]
+        base_refs, (surface_ref, once_ref, image_ref, rough_ref, second_ref) = out_refs[:LEVELS], out_refs[LEVELS:]
         col_tables, turned_tables, (own_t, _, _, wide_s, _, _) = plan.pick(table_ref)
         masks = plan.masks([height for height, _ in shapes])
         mis = mis_ref[...]
@@ -380,7 +380,7 @@
             base_refs[k][...] = base[k]
         once = autoreg(base[COARSE]) * masks[COARSE]
         once_ref[...] = once
-        twice_ref[...] = level_scales[COARSE] * autoreg(once)
+        twice = level_scales[COARSE] * autoreg(once)
         fine = smooth(base[COARSE])
         blank = jnp.zeros((inner_rows - rows - 2 * NEAR, plan.col_frame), jnp.float32)
         fine = jnp.concatenate([fine[0 : rows + NEAR], blank, fine[rows + NEAR :]], axis=0)
@@ -389,20 +389,23 @@
         surface_ref[...] = surface
         again = jnp.concatenate([wt_ref[...], side_ref[...]], axis=1) * surface[0:rows]
         blank = jnp.zeros((2 * NEAR, plan.col_frame), jnp.float32)
-        again_ref[...] = smooth(jnp.concatenate([again, blank], axis=0))
-
-    outs = shapes + [(inner_rows, plan.col_frame)] + shapes[COARSE:] * 3
-    *base, surface, once, twice, again = call(kernel, outs, 24)(mis, wt, side, tables)
-    return base, surface, once, twice, again
-
-
-def operate(plan, mid, mid_surface, mid_once, mid_twice, mid_again, wt, side, near, following, tables):
+        image = (smooth(jnp.concatenate([again, blank], axis=0)) + twice) * masks[COARSE]
+        image_ref[...] = image
+        rough_ref[...] = autoreg(image)
+        second_ref[...] = smooth(image)[0:rows, 0 : plan.cols]
+
+    outs = shapes + [(inner_rows, plan.col_frame)] + shapes[COARSE:] * 3 + [(rows, plan.cols)]
+    results = call(kernel, outs, 24)(mis, wt, side, tables)
+    return results[:LEVELS], results[LEVELS], results[LEVELS + 1 :]
+
+
+def operate(plan, mid, mid_surface, mid_fine, wt, side, near, following, tables):
     rows, cols, sr, lon_total = plan.rows, plan.cols, plan.swath_rows, plan.lon_total
     n_dev = plan.lat_total * lon_total
 
     def kernel(mid_surface_ref, wt_ref, side_ref, near_ref, next_ref, table_ref, *out_refs):
-        mid_refs, (once_ref, twice_ref, again_ref) = out_refs[:LEVELS], out_refs[LEVELS : LEVELS + 3]
-        out_refs = out_refs[LEVELS + 3 :]
+        mid_refs, (once_ref, fine_ref, rough_ref, second_ref) = out_refs[:LEVELS], out_refs[LEVELS : LEVELS + 4]
+        out_refs = out_refs[LEVELS + 4 :]
         base_refs, image_refs = out_refs[:LEVELS], out_refs[LEVELS : 2 * LEVELS]
         surface_refs, part_ref = out_refs[2 * LEVELS : -1], out_refs[-1]
         lat = lax.axis_index("lat")
@@ -463,7 +466,7 @@
             return jnp.concatenate(parts, axis=0)
 
         fine_once = once_ref[...] + place(once)
-        fine_twice = twice_ref[...] + place(level_scales[COARSE] * autoreg(once))
+        twice_edge = level_scales[COARSE] * autoreg(once)
         fine = smooth(strip)
         added = [fine[last:], blank(rows - 2 * NEAR, fine), fine[0 : NEAR + INNER], fine[last - INNER : last]]
         extra = jnp.concatenate(added, axis=0)
@@ -484,20 +487,26 @@
             weight[0:reach] * extra[0:reach],
         ]
         changed = smooth(jnp.concatenate(changed, axis=0))
-        first = reach + 2 * NEAR
-        changed = [changed[first:], blank(rows - 2 * reach, changed), changed[0:first]]
-        image.append(again_ref[...] + jnp.concatenate(changed, axis=0))
+        ends = [blank(EDGE, below), twice_edge[0 : 2 * NEAR], twice_edge[4 * NEAR :], blank(EDGE, below)]
+        fine_mask = masks[COARSE]
+        changed_mask = jnp.concatenate([fine_mask[rows - reach :], fine_mask[0:reach]], axis=0)
+        changed = (changed + jnp.concatenate(ends, axis=0)) * changed_mask
+
+        def spot(x):
+            first = reach + 2 * NEAR
+            return jnp.concatenate([x[first:], blank(rows - 2 * reach, x), x[0:first]], axis=0)
+
         rough_base, rough_image = [], []
-        for k in range(LEVELS):
-            if k == COARSE:
-                once, twice = fine_once, fine_twice
-            else:
-                once = autoreg(base[k]) * masks[k]
-                twice = level_scales[k] * autoreg(once)
+        for k in range(COARSE):
+            once = autoreg(base[k]) * masks[k]
             rough_base.append(once)
-            image[k] = (image[k] + twice) * masks[k]
+            image[k] = (image[k] + level_scales[k] * autoreg(once)) * masks[k]
             rough_image.append(autoreg(image[k]))
-        second = dot3(tile_s, spread(image, cols)) + smooth(image[COARSE])[0:rows, 0:cols]
+        rough_base.append(fine_once)
+        image.append(fine_ref[...] + spot(changed))
+        rough_image.append(rough_ref[...] + spot(autoreg(changed)))
+        second_fine = second_ref[...] + spot(smooth(changed))[0:rows, 0:cols]
+        second = dot3(tile_s, spread(image, cols)) + second_fine
 
         own = [(slice(0, rows // s), slice(0, cols // s)) for s in SPACINGS]
         b = [base[k][own[k]] for k in range(LEVELS)]
@@ -575,7 +584,7 @@
 
     level_shapes = [(rows // s, cols // s) for s in SPACINGS]
     outs = level_shapes * 2 + [(2 * rows, cols)] + [(2 * sr, cols)] * (lon_total - 1) + [(n_dev, LANES)]
-    results = call(kernel, outs, 24)(mid_surface, wt, side, near, following, tables, *mid, mid_once, mid_twice, mid_again)
+    results = call(kernel, outs, 24)(mid_surface, wt, side, near, following, tables, *mid, *mid_fine)
     return results[:LEVELS], results[LEVELS : 2 * LEVELS], results[2 * LEVELS : -1], results[-1]
 
 
@@ -642,12 +651,10 @@
     tables = fetch(plan, own)
     right, *far, left = [turn(x, "lon", lon_total, k) for k, x in enumerate(windows, 1)]
     mis, side, near, following = misfit(plan, own, right, left, far, weight, tables)
-    mid, mid_surface, mid_once, mid_twice, mid_again = inside(plan, mis, weight, side, tables)
+    mid, mid_surface, mid_fine = inside(plan, mis, weight, side, tables)
     near = flip(near, "lat", lat_total, 1)
     following = odd_swap(following, "lat", lat_total)
-    base, image, surfaces, parts = operate(
-        plan, mid, mid_surface, mid_once, mid_twice, mid_again, weight, side, near, following, tables
-    )
+    base, image, surfaces, parts = operate(plan, mid, mid_surface, mid_fine, weight, side, near, following, tables)
     far_surfaces = [flip(x, "lon", lon_total, k) for k, x in enumerate(surfaces[1:], 1)]
     parts = lax.all_to_all(parts, ("lat", "lon"), split_axis=0, concat_axis=0, tiled=True)
     return tuple(finish(plan, parts, base, image, surfaces[0], far_surfaces))

time: 39.5 us -> 39.3 us (level)
  waiting for transfers between devices: 4.8 us -> 4.22 us
  Pallas kernels: 9.12 us -> 9.52 us
    ppermute x4, waiting for transfers between devices: 4.06 us -> 3.48 us  [flip(): return lax.ppermute(x, axis, [(i, i ^ k) for i in range(total)])]
    pallas_call x5, Pallas kernels: 8.55 us -> 8.95 us  [run(): pl.pallas_call(kernel, out_shape=[jax.ShapeDtypeStruct(shape, jnp.float32...]
  transfers between devices with their start and end apart: 8 -> 8, of which waited for: 2 -> 2; matrix products, arithmetic and copies ran while one was open for 0% -> 0% of each run, Pallas kernels for 8% -> 9%
where the time goes in v7:
time: 39.3 us; the launch traced here: 39.1 us
  blocking collectives  13 us (33%)
  Pallas kernels  9.52 us (24%)
  starting transfers between devices  8.99 us (23%)
  waiting for transfers between devices  4.22 us (11%)
  local copies, waits for them, and re-layouts  2.67 us (7%)
  between operations  0.68 us (2%)
    all_to_all x1, blocking collectives, body(): lax.all_to_all(parts, ('lat', 'lon'), split_axis=0, concat_axis=0, tiled=...  13 us
    pallas_call x5, Pallas kernels, run(): pl.pallas_call(kernel, out_shape=[jax.ShapeDtypeStruct(shape, jnp.float32...  8.95 us
    ppermute x3, starting transfers between devices, turn(): return lax.ppermute(x, axis, [(i, (i + k) % total) for i in range(total)])  4.76 us
    ppermute x4, starting transfers between devices, flip(): return lax.ppermute(x, axis, [(i, i ^ k) for i in range(total)])  3.56 us
    ppermute x4, waiting for transfers between devices, flip(): return lax.ppermute(x, axis, [(i, i ^ k) for i in range(total)])  3.48 us
    unnamed x2, local copies, waits for them, and re-layouts  2.67 us
  transfers between devices with their start and end apart: 8, of which 2 were waited for; matrix products, arithmetic and copies ran while one was open for 0% of the time, Pallas kernels for 9%

profile of v7, /device:TPU:0, one launch (start us, length us, event | category | flops | bytes accessed | tf_op | source)
XLA Modules:
  0.0 39.1 jit_solution(9570231196641551142)
XLA Ops:
  0.6 1.1 %shard_map.74 = (f32[128,512]{1,0:T(8,128)S(1)}, f32[32,640]{1,0:T(8,128)S(1)}, f32[224,128]{1,0:T(8,128)S(1)}, f32[32,640]{1,0:T(8,128)S(1)}, f32[224,128]{1,0:T(8,128)S(1)}) custom-call(f32[32,2048]{1,0:T(8,128)} %obs_hbm.1, s32[128,512]{1,0:T(8,128)} %gauge_hbm.1), custom_call_target="tpu_custom_call" | custom-call | tf_op jit(solution)/shard_map/pallas_call | solution.py:206
  1.8 0.5 %collective-permute-start = (f32[224,128]{1,0:T(8,128)S(1)}, f32[224,128]{1,0:T(8,128)S(1)}, u32[]{:S(2)}, u32[]{:S(2)}) collective-permute-start(f32[224,128]{1,0:T(8,128)S(1)} %get-tuple-element.37), channel_id=1, source_target_pairs={{0,1},{1,2},{2,3},{3,0},{4,5},{5,6},{6,7},{7,4},{8,9},{9,10},{10,1... | collective-permute-start | bytes 344072 | tf_op jit(solution)/shard_map/ppermute | solution.py:635
  2.3 2.0 %collective-permute-start.1 = (f32[224,128]{1,0:T(8,128)S(1)}, f32[224,128]{1,0:T(8,128)S(1)}, u32[]{:S(2)}, u32[]{:S(2)}) collective-permute-start(f32[224,128]{1,0:T(8,128)S(1)} %get-tuple-element.38), channel_id=1, source_target_pairs={{0,3},{1,0},{2,1},{3,2},{4,7},{5,4},{6,5},{7,6},{8,11},{9,8},{10,9... | collective-permute-start | bytes 344072 | tf_op jit(solution)/shard_map/ppermute | solution.py:635
  4.3 2.2 %collective-permute-start.2 = (f32[32,640]{1,0:T(8,128)S(1)}, f32[32,640]{1,0:T(8,128)S(1)}, u32[]{:S(2)}, u32[]{:S(2)}) collective-permute-start(f32[32,640]{1,0:T(8,128)S(1)} %get-tuple-element.40), channel_id=1, source_target_pairs={{0,2},{1,3},{2,0},{3,1},{4,6},{5,7},{6,4},{7,5},{8,10},{9,11},{10,... | collective-permute-start | bytes 245768 | tf_op jit(solution)/shard_map/ppermute | solution.py:635
  6.5 0.0 copy-start
  6.5 2.7 %copy-done = bf16[2,768,1920]{2,1,0:T(8,128)(2,1)S(1)} copy-done((bf16[2,768,1920]{2,1,0:T(8,128)(2,1)S(1)}, bf16[2,768,1920]{2,1,0:T(8,128)(2,1)}, u32[]{:S(2)}) %copy-start) | copy-done | bytes 5898264
  9.2 0.6 %shard_map.75.table_ref = bf16[2,768,1920]{2,1,0:T(8,128)(2,1)S(1)} custom-call(bf16[2,768,1920]{2,1,0:T(8,128)(2,1)S(1)} %copy-done, f32[32,640]{1,0:T(8,128)S(1)} %get-tuple-element.36.after_ref.own_ref), custom_call_target="tpu_custom_call" | custom-call | bytes 11796480 | tf_op jit(solution)/shard_map/pallas_call | solution.py:354
  9.8 0.7 %collective-permute-done.2.rest_0_ = f32[32,640]{1,0:T(8,128)S(1)} collective-permute-done((f32[32,640]{1,0:T(8,128)S(1)}, f32[32,640]{1,0:T(8,128)S(1)}, u32[]{:S(2)}, u32[]{:S(2)}) %collective-permute-start.2) | collective-permute-done | bytes 81952 | tf_op jit(solution)/shard_map/ppermute | solution.py:635
  10.5 0.0 collective-permute-done.right_ref
  10.5 0.0 collective-permute-done.1.left_ref
  10.5 0.3 shard_map.76
  10.8 1.5 %collective-permute-start.3 = (f32[376,128]{1,0:T(8,128)S(1)}, f32[376,128]{1,0:T(8,128)S(1)}, u32[]{:S(2)}, u32[]{:S(2)}) collective-permute-start(f32[376,128]{1,0:T(8,128)S(1)} %get-tuple-element.44), channel_id=1, source_target_pairs={{0,4},{4,0},{8,12},{12,8},{16,20},{20,16},{24,28},{28,24},{1,5},{5... | collective-permute-start | bytes 577544 | tf_op jit(solution)/shard_map/ppermute | solution.py:639
  12.3 0.7 %collective-permute-start.4 = (f32[376,128]{1,0:T(8,128)S(1)}, f32[376,128]{1,0:T(8,128)S(1)}, u32[]{:S(2)}, u32[]{:S(2)}) collective-permute-start(f32[376,128]{1,0:T(8,128)S(1)} %get-tuple-element.45), channel_id=1, source_target_pairs={{4,8},{12,16},{20,24},{8,4},{16,12},{24,20},{5,9},{13,17},{21,25},... | collective-permute-start | bytes 577544 | tf_op jit(solution)/shard_map/ppermute | solution.py:644
  13.0 3.1 %shard_map.77 = (f32[32,128]{1,0:T(8,128)S(1)}, f32[64,256]{1,0:T(8,128)S(1)}, f32[112,384]{1,0:T(8,128)S(1)}, f32[144,640]{1,0:T(8,128)S(1)}, f32[192,640]{1,0:...) custom-call(f32[128,640]{1,0:T(8,128)S(1)} %get-tuple-element.41.mis, ...), custom_call_target="tpu_custom_call" | custom-call | tf_op jit(solution)/shard_map/pallas_call | solution.py:206
  16.2 3.5 %collective-permute-done.3.near_ref = f32[376,128]{1,0:T(8,128)S(1)} collective-permute-done((f32[376,128]{1,0:T(8,128)S(1)}, f32[376,128]{1,0:T(8,128)S(1)}, u32[]{:S(2)}, u32[]{:S(2)}) %collective-permute-start.3) | collective-permute-done | bytes 192544 | tf_op jit(solution)/shard_map/ppermute | solution.py:639
  19.6 0.0 collective-permute-done.4.next_ref
  19.6 3.4 %shard_map.78 = (f32[16,64]{1,0:T(8,128)S(1)}, f32[32,128]{1,0:T(8,128)S(1)}, f32[64,256]{1,0:T(8,128)S(1)}, f32[128,512]{1,0:T(8,128)S(1)}, f32[16,64]{1,0:T(8,...) custom-call(f32[192,640]{1,0:T(8,128)S(1)} %get-tuple-element.43.mid, ...), custom_call_target="tpu_custom_call" | custom-call | tf_op jit(solution)/shard_map/pallas_call | solution.py:206
  23.0 0.0 collective-permute-start.5
  23.0 2.0 %collective-permute-start.6 = (f32[64,512]{1,0:T(8,128)S(1)}, f32[64,512]{1,0:T(8,128)S(1)}, u32[]{:S(2)}, u32[]{:S(2)}) collective-permute-start(f32[64,512]{1,0:T(8,128)S(1)} %get-tuple-element.65), channel_id=1, source_target_pairs={{0,2},{1,3},{2,0},{3,1},{4,6},{5,7},{6,4},{7,5},{8,10},{9,11},{10,... | collective-permute-start | bytes 393224 | tf_op jit(solution)/shard_map/ppermute | solution.py:639
  25.0 0.1 collective-permute-start.7
  25.1 13.0 %all_to_all.11 = f32[32,1,128]{2,1,0:T(1,128)S(1)} all-to-all(f32[32,1,128]{2,1,0:T(1,128)S(1)} %bitcast.5), channel_id=1, replica_groups=mesh['lat'=8,'lon'=4] {'lat','lon'}, dimensions={0} | all-to-all | bytes 32768 | tf_op jit(solution)/shard_map/all_to_all | solution.py:659
  38.1 0.0 collective-permute-done.5.rest_9_
  38.1 0.0 collective-permute-done.6.rest_10_
  38.1 0.0 collective-permute-done.7.rest_11_
  38.1 1.0 %shard_map.79 = (f32[16,64]{1,0:T(8,128)}, f32[32,128]{1,0:T(8,128)}, f32[64,256]{1,0:T(8,128)}, f32[128,512]{1,0:T(8,128)}, f32[32,2048]{1,0:T(8,128)}) custom-call(f32[32,128]{1,0:T(8,128)S(1)} %bitcast.4, f32[16,64]{1,0:T(8,128)S(1)} %get-tuple-element.55.rest_0_, f32[32,128]{1,0:T(8,128)S(1)} %get-tuple-element.56.rest_1_, ...), custom_call_target="tpu_custom_call" | custom-call | tf_op jit(solution)/shard_map/pallas_call | solution.py:206
Async XLA Ops:
  1.8 8.7 %collective-permute-start = (f32[224,128]{1,0:T(8,128)S(1)}, f32[224,128]{1,0:T(8,128)S(1)}, u32[]{:S(2)}, u32[]{:S(2)}) collective-permute-start(f32[224,128]{1,0:T(8,128)S(1)} %get-tuple-element.37), channel_id=1, source_target_pairs={{0,1},{1,2},{2,3},{3,0},{4,5},{5,6},{6,7},{7,4},{8,9},{9,10},{10,1... | collective-permute-start | bytes 344072 | tf_op jit(solution)/shard_map/ppermute | solution.py:635
  2.3 8.2 %collective-permute-start.1 = (f32[224,128]{1,0:T(8,128)S(1)}, f32[224,128]{1,0:T(8,128)S(1)}, u32[]{:S(2)}, u32[]{:S(2)}) collective-permute-start(f32[224,128]{1,0:T(8,128)S(1)} %get-tuple-element.38), channel_id=1, source_target_pairs={{0,3},{1,0},{2,1},{3,2},{4,7},{5,4},{6,5},{7,6},{8,11},{9,8},{10,9... | collective-permute-start | bytes 344072 | tf_op jit(solution)/shard_map/ppermute | solution.py:635
  4.3 6.2 %collective-permute-start.2 = (f32[32,640]{1,0:T(8,128)S(1)}, f32[32,640]{1,0:T(8,128)S(1)}, u32[]{:S(2)}, u32[]{:S(2)}) collective-permute-start(f32[32,640]{1,0:T(8,128)S(1)} %get-tuple-element.40), channel_id=1, source_target_pairs={{0,2},{1,3},{2,0},{3,1},{4,6},{5,7},{6,4},{7,5},{8,10},{9,11},{10,... | collective-permute-start | bytes 245768 | tf_op jit(solution)/shard_map/ppermute | solution.py:635
  6.5 2.7 %copy-start = (bf16[2,768,1920]{2,1,0:T(8,128)(2,1)S(1)}, bf16[2,768,1920]{2,1,0:T(8,128)(2,1)}, u32[]{:S(2)}) copy-start(bf16[2,768,1920]{2,1,0:T(8,128)(2,1)} %constant.2.clone.table_ref) | copy-start | bytes 17694724
  10.8 8.8 %collective-permute-start.3 = (f32[376,128]{1,0:T(8,128)S(1)}, f32[376,128]{1,0:T(8,128)S(1)}, u32[]{:S(2)}, u32[]{:S(2)}) collective-permute-start(f32[376,128]{1,0:T(8,128)S(1)} %get-tuple-element.44), channel_id=1, source_target_pairs={{0,4},{4,0},{8,12},{12,8},{16,20},{20,16},{24,28},{28,24},{1,5},{5... | collective-permute-start | bytes 577544 | tf_op jit(solution)/shard_map/ppermute | solution.py:639
  12.3 7.3 %collective-permute-start.4 = (f32[376,128]{1,0:T(8,128)S(1)}, f32[376,128]{1,0:T(8,128)S(1)}, u32[]{:S(2)}, u32[]{:S(2)}) collective-permute-start(f32[376,128]{1,0:T(8,128)S(1)} %get-tuple-element.45), channel_id=1, source_target_pairs={{4,8},{12,16},{20,24},{8,4},{16,12},{24,20},{5,9},{13,17},{21,25},... | collective-permute-start | bytes 577544 | tf_op jit(solution)/shard_map/ppermute | solution.py:644
  23.0 15.1 %collective-permute-start.5 = (f32[64,512]{1,0:T(8,128)S(1)}, f32[64,512]{1,0:T(8,128)S(1)}, u32[]{:S(2)}, u32[]{:S(2)}) collective-permute-start(f32[64,512]{1,0:T(8,128)S(1)} %get-tuple-element.64), channel_id=1, source_target_pairs={{0,1},{1,0},{2,3},{3,2},{4,5},{5,4},{6,7},{7,6},{8,9},{9,8},{10,11... | collective-permute-start | bytes 393224 | tf_op jit(solution)/shard_map/ppermute | solution.py:639
  23.0 15.1 %collective-permute-start.6 = (f32[64,512]{1,0:T(8,128)S(1)}, f32[64,512]{1,0:T(8,128)S(1)}, u32[]{:S(2)}, u32[]{:S(2)}) collective-permute-start(f32[64,512]{1,0:T(8,128)S(1)} %get-tuple-element.65), channel_id=1, source_target_pairs={{0,2},{1,3},{2,0},{3,1},{4,6},{5,7},{6,4},{7,5},{8,10},{9,11},{10,... | collective-permute-start | bytes 393224 | tf_op jit(solution)/shard_map/ppermute | solution.py:639
  25.0 13.1 %collective-permute-start.7 = (f32[64,512]{1,0:T(8,128)S(1)}, f32[64,512]{1,0:T(8,128)S(1)}, u32[]{:S(2)}, u32[]{:S(2)}) collective-permute-start(f32[64,512]{1,0:T(8,128)S(1)} %get-tuple-element.66), channel_id=1, source_target_pairs={{0,3},{1,2},{2,1},{3,0},{4,7},{5,6},{6,5},{7,4},{8,11},{9,10},{10,... | collective-permute-start | bytes 393224 | tf_op jit(solution)/shard_map/ppermute | solution.py:639

commit v8 on v7

--- a/solution.py
+++ b/solution.py
@@ -308,7 +308,8 @@
                 numerator = jnp.abs(2 * distance - 2 * s * away - (s - 1)).astype(jnp.float32)
                 table = jnp.where(line == m, wendland(numerator / (5.0 * s), jnp) / math.sqrt(s), table)
             edge = pl.ds(pl.multiple_of(low * (rows - INNER), 8), INNER)
-            sums = jnp.dot(table, far, precision=lax.Precision.HIGHEST, preferred_element_type=jnp.float32)
+            (th, tl), (fh, fl) = split(table), split(far)
+            sums = dot(th, fh, (1, 0)) + (dot(th, fl, (1, 0)) + dot(tl, fh, (1, 0)))
             near = mis_ref[pl.ds(pl.multiple_of(low * (rows - RAW), 8), RAW), :]
             raw, weights, corner, parts = plan.letter()
             for t in range(tiles):

time: 39.3 us -> 39.3 us (level)
  no operation moved by 1% of the time
where the time goes in v8:
time: 39.3 us; the launch traced here: 39.1 us
  blocking collectives  13 us (33%)
  Pallas kernels  9.49 us (24%)
  starting transfers between devices  9.05 us (23%)
  waiting for transfers between devices  4.22 us (11%)
  local copies, waits for them, and re-layouts  2.67 us (7%)
  between operations  0.68 us (2%)
    all_to_all x1, blocking collectives, body(): lax.all_to_all(parts, ('lat', 'lon'), split_axis=0, concat_axis=0, tiled=...  13 us
    pallas_call x5, Pallas kernels, run(): pl.pallas_call(kernel, out_shape=[jax.ShapeDtypeStruct(shape, jnp.float32...  8.93 us
    ppermute x3, starting transfers between devices, turn(): return lax.ppermute(x, axis, [(i, (i + k) % total) for i in range(total)])  4.76 us
    ppermute x4, starting transfers between devices, flip(): return lax.ppermute(x, axis, [(i, i ^ k) for i in range(total)])  3.62 us
    ppermute x4, waiting for transfers between devices, flip(): return lax.ppermute(x, axis, [(i, i ^ k) for i in range(total)])  3.48 us
    unnamed x2, local copies, waits for them, and re-layouts  2.67 us
  transfers between devices with their start and end apart: 8, of which 2 were waited for; matrix products, arithmetic and copies ran while one was open for 0% of the time, Pallas kernels for 9%

profile of v8, /device:TPU:0, one launch (start us, length us, event | category | flops | bytes accessed | tf_op | source)
XLA Modules:
  0.0 39.1 jit_solution(6282100270140705951)
XLA Ops:
  0.6 1.1 %shard_map.74 = (f32[128,512]{1,0:T(8,128)S(1)}, f32[32,640]{1,0:T(8,128)S(1)}, f32[224,128]{1,0:T(8,128)S(1)}, f32[32,640]{1,0:T(8,128)S(1)}, f32[224,128]{1,0:T(8,128)S(1)}) custom-call(f32[32,2048]{1,0:T(8,128)} %obs_hbm.1, s32[128,512]{1,0:T(8,128)} %gauge_hbm.1), custom_call_target="tpu_custom_call" | custom-call | tf_op jit(solution)/shard_map/pallas_call | solution.py:206
  1.8 0.5 %collective-permute-start = (f32[224,128]{1,0:T(8,128)S(1)}, f32[224,128]{1,0:T(8,128)S(1)}, u32[]{:S(2)}, u32[]{:S(2)}) collective-permute-start(f32[224,128]{1,0:T(8,128)S(1)} %get-tuple-element.37), channel_id=1, source_target_pairs={{0,1},{1,2},{2,3},{3,0},{4,5},{5,6},{6,7},{7,4},{8,9},{9,10},{10,1... | collective-permute-start | bytes 344072 | tf_op jit(solution)/shard_map/ppermute | solution.py:636
  2.3 2.0 %collective-permute-start.1 = (f32[224,128]{1,0:T(8,128)S(1)}, f32[224,128]{1,0:T(8,128)S(1)}, u32[]{:S(2)}, u32[]{:S(2)}) collective-permute-start(f32[224,128]{1,0:T(8,128)S(1)} %get-tuple-element.38), channel_id=1, source_target_pairs={{0,3},{1,0},{2,1},{3,2},{4,7},{5,4},{6,5},{7,6},{8,11},{9,8},{10,9... | collective-permute-start | bytes 344072 | tf_op jit(solution)/shard_map/ppermute | solution.py:636
  4.3 2.2 %collective-permute-start.2 = (f32[32,640]{1,0:T(8,128)S(1)}, f32[32,640]{1,0:T(8,128)S(1)}, u32[]{:S(2)}, u32[]{:S(2)}) collective-permute-start(f32[32,640]{1,0:T(8,128)S(1)} %get-tuple-element.40), channel_id=1, source_target_pairs={{0,2},{1,3},{2,0},{3,1},{4,6},{5,7},{6,4},{7,5},{8,10},{9,11},{10,... | collective-permute-start | bytes 245768 | tf_op jit(solution)/shard_map/ppermute | solution.py:636
  6.5 0.0 copy-start
  6.5 2.7 %copy-done = bf16[2,768,1920]{2,1,0:T(8,128)(2,1)S(1)} copy-done((bf16[2,768,1920]{2,1,0:T(8,128)(2,1)S(1)}, bf16[2,768,1920]{2,1,0:T(8,128)(2,1)}, u32[]{:S(2)}) %copy-start) | copy-done | bytes 5898264
  9.2 0.6 %shard_map.75.table_ref = bf16[2,768,1920]{2,1,0:T(8,128)(2,1)S(1)} custom-call(bf16[2,768,1920]{2,1,0:T(8,128)(2,1)S(1)} %copy-done, f32[32,640]{1,0:T(8,128)S(1)} %get-tuple-element.36.after_ref.own_ref), custom_call_target="tpu_custom_call" | custom-call | bytes 11796480 | tf_op jit(solution)/shard_map/pallas_call | solution.py:355
  9.8 0.7 %collective-permute-done.2.rest_0_ = f32[32,640]{1,0:T(8,128)S(1)} collective-permute-done((f32[32,640]{1,0:T(8,128)S(1)}, f32[32,640]{1,0:T(8,128)S(1)}, u32[]{:S(2)}, u32[]{:S(2)}) %collective-permute-start.2) | collective-permute-done | bytes 81952 | tf_op jit(solution)/shard_map/ppermute | solution.py:636
  10.5 0.0 collective-permute-done.right_ref
  10.5 0.0 collective-permute-done.1.left_ref
  10.5 0.3 shard_map.76
  10.8 1.6 %collective-permute-start.3 = (f32[376,128]{1,0:T(8,128)S(1)}, f32[376,128]{1,0:T(8,128)S(1)}, u32[]{:S(2)}, u32[]{:S(2)}) collective-permute-start(f32[376,128]{1,0:T(8,128)S(1)} %get-tuple-element.44), channel_id=1, source_target_pairs={{0,4},{4,0},{8,12},{12,8},{16,20},{20,16},{24,28},{28,24},{1,5},{5... | collective-permute-start | bytes 577544 | tf_op jit(solution)/shard_map/ppermute | solution.py:640
  12.4 0.7 %collective-permute-start.4 = (f32[376,128]{1,0:T(8,128)S(1)}, f32[376,128]{1,0:T(8,128)S(1)}, u32[]{:S(2)}, u32[]{:S(2)}) collective-permute-start(f32[376,128]{1,0:T(8,128)S(1)} %get-tuple-element.45), channel_id=1, source_target_pairs={{4,8},{12,16},{20,24},{8,4},{16,12},{24,20},{5,9},{13,17},{21,25},... | collective-permute-start | bytes 577544 | tf_op jit(solution)/shard_map/ppermute | solution.py:645
  13.0 3.1 %shard_map.77 = (f32[32,128]{1,0:T(8,128)S(1)}, f32[64,256]{1,0:T(8,128)S(1)}, f32[112,384]{1,0:T(8,128)S(1)}, f32[144,640]{1,0:T(8,128)S(1)}, f32[192,640]{1,0:...) custom-call(f32[128,640]{1,0:T(8,128)S(1)} %get-tuple-element.41.mis, ...), custom_call_target="tpu_custom_call" | custom-call | tf_op jit(solution)/shard_map/pallas_call | solution.py:206
  16.2 3.5 %collective-permute-done.3.near_ref = f32[376,128]{1,0:T(8,128)S(1)} collective-permute-done((f32[376,128]{1,0:T(8,128)S(1)}, f32[376,128]{1,0:T(8,128)S(1)}, u32[]{:S(2)}, u32[]{:S(2)}) %collective-permute-start.3) | collective-permute-done | bytes 192544 | tf_op jit(solution)/shard_map/ppermute | solution.py:640
  19.7 0.0 collective-permute-done.4.next_ref
  19.7 3.4 %shard_map.78 = (f32[16,64]{1,0:T(8,128)S(1)}, f32[32,128]{1,0:T(8,128)S(1)}, f32[64,256]{1,0:T(8,128)S(1)}, f32[128,512]{1,0:T(8,128)S(1)}, f32[16,64]{1,0:T(8,...) custom-call(f32[192,640]{1,0:T(8,128)S(1)} %get-tuple-element.43.mid, ...), custom_call_target="tpu_custom_call" | custom-call | tf_op jit(solution)/shard_map/pallas_call | solution.py:206
  23.0 0.0 collective-permute-start.5
  23.0 2.0 %collective-permute-start.6 = (f32[64,512]{1,0:T(8,128)S(1)}, f32[64,512]{1,0:T(8,128)S(1)}, u32[]{:S(2)}, u32[]{:S(2)}) collective-permute-start(f32[64,512]{1,0:T(8,128)S(1)} %get-tuple-element.65), channel_id=1, source_target_pairs={{0,2},{1,3},{2,0},{3,1},{4,6},{5,7},{6,4},{7,5},{8,10},{9,11},{10,... | collective-permute-start | bytes 393224 | tf_op jit(solution)/shard_map/ppermute | solution.py:640
  25.0 0.1 collective-permute-start.7
  25.1 13.0 %all_to_all.11 = f32[32,1,128]{2,1,0:T(1,128)S(1)} all-to-all(f32[32,1,128]{2,1,0:T(1,128)S(1)} %bitcast.5), channel_id=1, replica_groups=mesh['lat'=8,'lon'=4] {'lat','lon'}, dimensions={0} | all-to-all | bytes 32768 | tf_op jit(solution)/shard_map/all_to_all | solution.py:660
  38.1 0.0 collective-permute-done.5.rest_9_
  38.1 0.0 collective-permute-done.6.rest_10_
  38.1 0.0 collective-permute-done.7.rest_11_
  38.1 1.0 %shard_map.79 = (f32[16,64]{1,0:T(8,128)}, f32[32,128]{1,0:T(8,128)}, f32[64,256]{1,0:T(8,128)}, f32[128,512]{1,0:T(8,128)}, f32[32,2048]{1,0:T(8,128)}) custom-call(f32[32,128]{1,0:T(8,128)S(1)} %bitcast.4, f32[16,64]{1,0:T(8,128)S(1)} %get-tuple-element.55.rest_0_, f32[32,128]{1,0:T(8,128)S(1)} %get-tuple-element.56.rest_1_, ...), custom_call_target="tpu_custom_call" | custom-call | tf_op jit(solution)/shard_map/pallas_call | solution.py:206
Async XLA Ops:
  1.8 8.7 %collective-permute-start = (f32[224,128]{1,0:T(8,128)S(1)}, f32[224,128]{1,0:T(8,128)S(1)}, u32[]{:S(2)}, u32[]{:S(2)}) collective-permute-start(f32[224,128]{1,0:T(8,128)S(1)} %get-tuple-element.37), channel_id=1, source_target_pairs={{0,1},{1,2},{2,3},{3,0},{4,5},{5,6},{6,7},{7,4},{8,9},{9,10},{10,1... | collective-permute-start | bytes 344072 | tf_op jit(solution)/shard_map/ppermute | solution.py:636
  2.3 8.2 %collective-permute-start.1 = (f32[224,128]{1,0:T(8,128)S(1)}, f32[224,128]{1,0:T(8,128)S(1)}, u32[]{:S(2)}, u32[]{:S(2)}) collective-permute-start(f32[224,128]{1,0:T(8,128)S(1)} %get-tuple-element.38), channel_id=1, source_target_pairs={{0,3},{1,0},{2,1},{3,2},{4,7},{5,4},{6,5},{7,6},{8,11},{9,8},{10,9... | collective-permute-start | bytes 344072 | tf_op jit(solution)/shard_map/ppermute | solution.py:636
  4.3 6.2 %collective-permute-start.2 = (f32[32,640]{1,0:T(8,128)S(1)}, f32[32,640]{1,0:T(8,128)S(1)}, u32[]{:S(2)}, u32[]{:S(2)}) collective-permute-start(f32[32,640]{1,0:T(8,128)S(1)} %get-tuple-element.40), channel_id=1, source_target_pairs={{0,2},{1,3},{2,0},{3,1},{4,6},{5,7},{6,4},{7,5},{8,10},{9,11},{10,... | collective-permute-start | bytes 245768 | tf_op jit(solution)/shard_map/ppermute | solution.py:636
  6.5 2.7 %copy-start = (bf16[2,768,1920]{2,1,0:T(8,128)(2,1)S(1)}, bf16[2,768,1920]{2,1,0:T(8,128)(2,1)}, u32[]{:S(2)}) copy-start(bf16[2,768,1920]{2,1,0:T(8,128)(2,1)} %constant.2.clone.table_ref) | copy-start | bytes 17694724
  10.8 8.9 %collective-permute-start.3 = (f32[376,128]{1,0:T(8,128)S(1)}, f32[376,128]{1,0:T(8,128)S(1)}, u32[]{:S(2)}, u32[]{:S(2)}) collective-permute-start(f32[376,128]{1,0:T(8,128)S(1)} %get-tuple-element.44), channel_id=1, source_target_pairs={{0,4},{4,0},{8,12},{12,8},{16,20},{20,16},{24,28},{28,24},{1,5},{5... | collective-permute-start | bytes 577544 | tf_op jit(solution)/shard_map/ppermute | solution.py:640
  12.4 7.3 %collective-permute-start.4 = (f32[376,128]{1,0:T(8,128)S(1)}, f32[376,128]{1,0:T(8,128)S(1)}, u32[]{:S(2)}, u32[]{:S(2)}) collective-permute-start(f32[376,128]{1,0:T(8,128)S(1)} %get-tuple-element.45), channel_id=1, source_target_pairs={{4,8},{12,16},{20,24},{8,4},{16,12},{24,20},{5,9},{13,17},{21,25},... | collective-permute-start | bytes 577544 | tf_op jit(solution)/shard_map/ppermute | solution.py:645
  23.0 15.1 %collective-permute-start.5 = (f32[64,512]{1,0:T(8,128)S(1)}, f32[64,512]{1,0:T(8,128)S(1)}, u32[]{:S(2)}, u32[]{:S(2)}) collective-permute-start(f32[64,512]{1,0:T(8,128)S(1)} %get-tuple-element.64), channel_id=1, source_target_pairs={{0,1},{1,0},{2,3},{3,2},{4,5},{5,4},{6,7},{7,6},{8,9},{9,8},{10,11... | collective-permute-start | bytes 393224 | tf_op jit(solution)/shard_map/ppermute | solution.py:640
  23.0 15.1 %collective-permute-start.6 = (f32[64,512]{1,0:T(8,128)S(1)}, f32[64,512]{1,0:T(8,128)S(1)}, u32[]{:S(2)}, u32[]{:S(2)}) collective-permute-start(f32[64,512]{1,0:T(8,128)S(1)} %get-tuple-element.65), channel_id=1, source_target_pairs={{0,2},{1,3},{2,0},{3,1},{4,6},{5,7},{6,4},{7,5},{8,10},{9,11},{10,... | collective-permute-start | bytes 393224 | tf_op jit(solution)/shard_map/ppermute | solution.py:640
  25.0 13.1 %collective-permute-start.7 = (f32[64,512]{1,0:T(8,128)S(1)}, f32[64,512]{1,0:T(8,128)S(1)}, u32[]{:S(2)}, u32[]{:S(2)}) collective-permute-start(f32[64,512]{1,0:T(8,128)S(1)} %get-tuple-element.66), channel_id=1, source_target_pairs={{0,3},{1,2},{2,1},{3,0},{4,7},{5,6},{6,5},{7,4},{8,11},{9,10},{10,... | collective-permute-start | bytes 393224 | tf_op jit(solution)/shard_map/ppermute | solution.py:640
